TPU v7x, 32 devices: a whole 2x2x4 slice. The times are simulated.
32 devices in a mesh: blk: 8 (over z, core), red: 4 (over y, x).
Axes of the slice: x: 2, y: 2, z: 4, core: 2. Of those that a mesh axis runs over, the one named last changes fastest.
Arguments:
- amplitudes: bfloat16 [8, 192, 128, 128], P(None, 'blk', 'red'), may hold values from -6 to 6
- ladder_ints: bfloat16 [16384, 16384], P('red', 'blk'), may hold values from -0.046875 to 0.046875
- cycle_ints: bfloat16 [24576, 24576], P('blk', 'red'), may hold values from -0.0390625 to 0.0390625
- occ_energy: float32 [192], replicated, may hold values from -2 to -0.3
- vir_energy: float32 [128], replicated, may hold values from 0.2 to 3
- slab_index: int32 [8], replicated, may hold values from 0 to 191
Outputs:
- update: float32 [8, 192, 128, 128], P(None, 'red', 'blk')
All inputs are finite; a program needn't handle non-finite values.
Results may differ from a plain program's by a relative error of at most 0.0003.
Values may be sent and summed in bfloat16 or wider, within the bound.
No kernel may reach another device: no remote copies, remote signals or barrier semaphores. Data moves between devices by JAX's collectives and lax.ppermute only.
A program may use at most 192 MiB of HBM per device.

v0:
```python
import jax
import jax.numpy as jnp
from jax import lax
from jax.sharding import PartitionSpec as P


def shards(amplitudes, ladder_ints, cycle_ints, occ_energy, vir_energy, slab_index):
    slab_rows, occ_local, vir_local, virt_width = amplitudes.shape
    occ_all = occ_local * lax.axis_size("blk")
    occ_red = occ_all // lax.axis_size("red")
    shard_piece = lax.all_gather(amplitudes, "blk", axis=1, tiled=True)
    row_count = shard_piece.shape[1]
    flattened = shard_piece.reshape(slab_rows * row_count, vir_local * virt_width)
    product = jnp.dot(flattened, ladder_ints, preferred_element_type=jnp.float32)
    ladder = product.reshape(slab_rows, row_count, ladder_ints.shape[1])
    ladder_own = lax.psum_scatter(ladder, "red", scatter_dimension=1, tiled=True)
    ladder_own = ladder_own.reshape(slab_rows, occ_red, -1, virt_width)
    shard_piece = lax.all_gather(amplitudes, "red", axis=2, tiled=True)
    vir_count = shard_piece.shape[2]
    operand = jnp.transpose(shard_piece, (0, 2, 1, 3)).reshape(
        slab_rows * vir_count, occ_local * virt_width
    )
    product = jnp.dot(operand, cycle_ints, preferred_element_type=jnp.float32)
    cycle_term = product.reshape(slab_rows, vir_count, cycle_ints.shape[1])
    cycle_own = lax.psum_scatter(cycle_term, "blk", scatter_dimension=1, tiled=True)
    vir_block = cycle_own.shape[1]
    cycle_own = jnp.transpose(
        cycle_own.reshape(slab_rows, vir_block, occ_red, virt_width), (0, 2, 1, 3)
    )
    orbital_ids = jnp.arange(occ_energy.shape[0], dtype=jnp.int32)
    chosen = slab_index[:, None] == orbital_ids[None, :]
    slab_energy = jnp.sum(jnp.where(chosen, occ_energy[None, :], jnp.float32(0.0)), axis=1)
    pair_energy = lax.dynamic_slice_in_dim(occ_energy, lax.axis_index("red") * occ_red, occ_red)
    first_virtual = lax.dynamic_slice_in_dim(
        vir_energy, lax.axis_index("blk") * vir_block, vir_block
    )
    denominator = (
        first_virtual[None, None, :, None]
        + vir_energy[None, None, None, :]
        - slab_energy[:, None, None, None]
        - pair_energy[None, :, None, None]
    )
    return (ladder_own + cycle_own) / denominator


def solution(mesh):
    placed = (P(None, "blk", "red", None), P("red", "blk"), P("blk", "red"), P(), P(), P())
    return jax.shard_map(
        shards, mesh=mesh, in_specs=placed, out_specs=P(None, "red", "blk", None), check_vma=False
    )
```

profile of v0, /device:TPU:8, one launch (start us, length us, event | category | flops | bytes accessed | tf_op | source)
XLA Modules:
  0.0 577.9 jit_solution(12669226427983727070)
XLA Ops:
  6.5 0.0 all-gather.3.cloned.1.call-start
  6.5 0.7 all-gather.3.cloned.1.call-update
  7.3 0.0 all-gather.5.cloned.1.call-start
  7.3 0.7 all-gather.5.cloned.1.call-update
  8.0 0.0 reduce-scatter.3.cloned.1.call-start
  8.1 115.9 %all-gather.3.cloned.1.call-done = bf16[8,192,32,128]{3,2,1,0:T(8,128)(2,1)} async-done(((bf16[8,24,32,128]{3,2,1,0:T(8,128)(2,1)}), bf16[8,192,32,128]{3,2,1,0:T(8,128)(2,1)}) %all-gather.3.cloned.1.call-update) | async-done | bytes 12582928 | tf_op jit(solution)/shard_map/all_gather | solution.py:11
  123.9 19.6 %dot_general.10 = bf16[8,192,4096]{2,1,0:T(8,128)(2,1)} reshape(bf16[8,192,32,128]{3,2,1,0:T(8,128)(2,1)} %all-gather.3.cloned.1.call-done) | data formatting | bytes 25165824 | tf_op jit(solution)/shard_map/dot_general | solution.py:14
  143.5 34.5 %fusion.2 = f32[8,192,2048]{2,1,0:T(8,128)} fusion(bf16[8,192,4096]{2,1,0:T(8,128)(2,1)} %dot_general.10, bf16[4096,2048]{1,0:T(8,128)(2,1)} %param.7), kind=kOutput, calls=%fused_computation.2 | convolution fusion | flops 25769803776 | bytes 41943040 | tf_op jit(solution)/shard_map/dot_general | solution.py:14
  178.0 0.0 reduce-scatter.3.cloned.1.call-update
  178.0 0.0 reduce-scatter.5.cloned.1.call-start
  178.1 18.9 %all-gather.5.cloned.1.call-done = bf16[8,24,128,128]{3,2,1,0:T(8,128)(2,1)} async-done(((bf16[8,24,32,128]{3,2,1,0:T(8,128)(2,1)}), bf16[8,24,128,128]{3,2,1,0:T(8,128)(2,1)}) %all-gather.5.cloned.1.call-update) | async-done | bytes 6291472 | tf_op jit(solution)/shard_map/all_gather | solution.py:18
  197.0 46.6 %fusion = f32[8,128,6144]{2,1,0:T(8,128)} fusion(bf16[3072,6144]{1,0:T(8,128)(2,1)} %param.8, bf16[8,24,128,128]{3,2,1,0:T(8,128)(2,1)} %all-gather.5.cloned.1.call-done), kind=kOutput, calls=%fused_computation | convolution fusion | flops 38654705664 | bytes 69206016 | tf_op jit(solution)/shard_map/dot_general | solution.py:23
  243.6 0.0 copy-start
  243.6 0.0 copy-start.1
  243.6 0.0 copy-start.2
  243.6 0.0 reduce-scatter.5.cloned.1.call-update
  243.6 0.6 copy-done
  244.3 0.1 dynamic_slice.7
  244.4 0.0 copy-done.1
  244.4 0.1 dynamic_slice.6
  244.4 0.0 copy-done.2
  244.4 0.2 select_reduce_fusion
  244.6 0.1 broadcast_add_fusion
  244.7 0.1 broadcast_subtract_fusion
  244.8 76.0 %reduce-scatter.3.cloned.1.call-done = f32[8,48,2048]{2,1,0:T(8,128)} async-done(((f32[8,192,2048]{2,1,0:T(8,128)}), f32[8,48,2048]{2,1,0:T(8,128)}) %reduce-scatter.3.cloned.1.call-update) | async-done | bytes 3145744 | tf_op jit(solution)/shard_map/reduce_scatter | solution.py:16
  320.8 2.5 copy.13
  323.4 244.0 %reduce-scatter.5.cloned.1.call-done = f32[8,16,6144]{2,1,0:T(8,128)} async-done(((f32[8,128,6144]{2,1,0:T(8,128)}), f32[8,16,6144]{2,1,0:T(8,128)}) %reduce-scatter.5.cloned.1.call-update) | async-done | bytes 3145744 | tf_op jit(solution)/shard_map/reduce_scatter | solution.py:25
  567.4 4.0 fusion.6
Async XLA Ops:
  6.5 117.4 %all-gather.3.cloned.1.call-start = ((), (), s32[]{:S(2)}) async-start(), calls=%async_computation.2 | async-start | bytes 14155776 | tf_op jit(solution)/shard_map/all_gather | solution.py:11
  7.3 189.7 %all-gather.5.cloned.1.call-start = ((), (), s32[]{:S(2)}) async-start(), calls=%async_computation.4 | async-start | bytes 7864320 | tf_op jit(solution)/shard_map/all_gather | solution.py:18
  8.0 312.8 %reduce-scatter.3.cloned.1.call-start = ((), (), s32[]{:S(2)}) async-start(), calls=%async_computation.3 | async-start | bytes 15728640 | tf_op jit(solution)/shard_map/reduce_scatter | solution.py:16
  178.0 389.3 %reduce-scatter.5.cloned.1.call-start = ((), (), s32[]{:S(2)}) async-start(), calls=%async_computation.5 | async-start | bytes 28311552 | tf_op jit(solution)/shard_map/reduce_scatter | solution.py:25
  243.6 0.7 copy-start
  243.6 0.8 copy-start.1
  243.6 0.8 copy-start.2
Sparse Core Ops, SparseCore 0:
  9.0 114.8 all-gather.2
  125.7 71.1 all-gather.4
  200.1 120.7 reduce-scatter.2
  323.0 244.3 reduce-scatter.4
where the time goes:
time: 583 us; the launch traced here: 578 us
  waiting for transfers between devices  456 us (78%)
  matrix products  81.1 us (14%)
  local copies, waits for them, and re-layouts  23 us (4%)
  between operations  13.1 us (2%)
    reduce_scatter x1, waiting for transfers between devices, shards(): lax.psum_scatter(cycle_term, 'blk', scatter_dimension=1, tiled=True)  244 us
    all_gather x1, waiting for transfers between devices, shards(): shard_piece = lax.all_gather(amplitudes, 'blk', axis=1, tiled=True)  116 us
    reduce_scatter x1, waiting for transfers between devices, shards(): lax.psum_scatter(ladder, 'red', scatter_dimension=1, tiled=True)  76 us
    dot_general x1, matrix products, shards(): product = jnp.dot(operand, cycle_ints, preferred_element_type=jnp.float32)  46.6 us
    dot_general x1, matrix products, shards(): jnp.dot(flattened, ladder_ints, preferred_element_type=jnp.float32)  34.5 us
    dot_general x1, local copies, waits for them, and re-layouts, shards(): jnp.dot(flattened, ladder_ints, preferred_element_type=jnp.float32)  19.6 us
    all_gather x1, waiting for transfers between devices, shards(): shard_piece = lax.all_gather(amplitudes, 'red', axis=2, tiled=True)  18.9 us
  transfers between devices with their start and end apart: 4, of which 4 were waited for; matrix products, arithmetic and copies ran while one was open for 18% of the time, Pallas kernels for 0%

commit v1 on v0

v1 whole, which is shorter than its diff:
```python
import functools

import jax
import jax.numpy as jnp
from jax import lax
from jax.experimental import pallas as pl
from jax.experimental.pallas import tpu as pltpu
from jax.sharding import PartitionSpec as P

TRAILER = 16
STEPS = 64.0
TOP = 32000.0
VMEM = 56 * 2**20


def encode(groups):
    rows = lax.broadcasted_iota(jnp.int32, (TRAILER, groups[0].shape[1]), 0)
    trailer = jnp.zeros_like(rows)
    parts = []
    for index, group in enumerate(groups):
        largest = jnp.maximum(jnp.max(jnp.abs(group), axis=0, keepdims=True), 1e-35)
        level = jnp.ceil(jnp.log(largest) * (STEPS / 0.6931471805599453))
        scaled = group * (TOP * jnp.exp2(level * (-1.0 / STEPS)))
        parts.append(jnp.round(scaled).astype(jnp.int32).astype(jnp.int16))
        trailer = jnp.where(rows == index, level.astype(jnp.int32), trailer)
    return parts, trailer.astype(jnp.int16)


def put(ref, groups):
    parts, trailer = encode(groups)
    row = 0
    for part in parts:
        ref[row : row + part.shape[0], :] = part
        row += part.shape[0]
    ref[row : row + TRAILER, :] = trailer


def take(ref, groups, index):
    rows = (ref.shape[0] - TRAILER) // groups
    trailer = ref[groups * rows :, :].astype(jnp.int32).astype(jnp.float32)
    scale = jnp.exp2(trailer[index : index + 1, :] * (1.0 / STEPS)) * (1.0 / TOP)
    return ref[index * rows : (index + 1) * rows, :].astype(jnp.int32).astype(jnp.float32) * scale


def params():
    return pltpu.CompilerParams(vmem_limit_bytes=VMEM, dimension_semantics=("arbitrary",))


def light(flops=1000):
    return pl.CostEstimate(flops=flops, bytes_accessed=1000, transcendentals=0)


def bring(candidates, code, target, sem):
    def start(source):
        return lambda: pltpu.make_async_copy(source, target, sem).start()

    if len(candidates) == 1:
        start(candidates[0])()
    else:
        for number, source in enumerate(candidates):
            pl.when(code == number)(start(source))
    return pltpu.make_async_copy(candidates[0], target, sem)


ANY = pl.BlockSpec(memory_space=pl.ANY)


def forward_kernel(rx_ref, ry_ref, *refs, skip):
    on_y_ref, on_x_ref = refs[skip : skip + 2]
    on_y_ref[...], on_x_ref[...] = rx_ref[...], ry_ref[...]


def forward(rx, ry, through=(), after=()):
    rows, width = rx.shape[0] // 2, rx.shape[1]
    block = jax.ShapeDtypeStruct((rows, width), rx.dtype)
    return pl.pallas_call(
        functools.partial(forward_kernel, skip=len(through) + len(after)),
        grid=(1,),
        in_specs=[pl.BlockSpec((rows, width), lambda n: (0, 0)), pl.BlockSpec((rows, width), lambda n: (1, 0))]
        + [ANY] * (len(through) + len(after)),
        out_specs=[pl.BlockSpec((rows, width), lambda n: (0, 0))] * 2 + [ANY] * len(through),
        out_shape=[block, block] + [jax.ShapeDtypeStruct(t.shape, t.dtype) for t in through],
        input_output_aliases={2 + k: 2 + k for k in range(len(through))},
        compiler_params=params(),
        cost_estimate=light(),
    )(rx, ry, *through, *after)


BLOCKS = 4
SENT = 3


def cycle_kernel(at_ref, own_ref, rx_ref, ry_ref, ry2_ref, rx2_ref, left_ref, right_ref, *refs, keeps, skip):
    if keeps:
        got, refs = refs[:keeps], refs[keeps:]
        sums_ref, s0_ref, s1_ref, s2_ref = refs[skip : 4 + skip]
        x_ref, sems, got_ref = refs[-3:]
        for part, part_ref in enumerate(got):

            @pl.when(pl.program_id(0) // (pl.num_programs(0) // keeps) == part)
            def _(part_ref=part_ref):
                got_ref[...] = part_ref[...]

    else:
        out_ref, x_ref, sems = refs[skip:]
    rows = ry2_ref.shape[0]
    half = at_ref[0]

    @pl.when(pl.program_id(0) == 0)
    def _():
        waits = []
        place = pl.ds(pl.multiple_of(half * rows, rows), rows)
        for n in range(BLOCKS):
            target, sem = x_ref.at[pl.ds(n * rows, rows), :], sems.at[n]
            sources = [own_ref.at[place, :], rx_ref.at[place, :], ry_ref.at[place, :], ry2_ref, rx2_ref]
            code = at_ref[1 + n]
            waits.append(bring(sources, jnp.where(code == 3, 3 + half, code), target, sem))
        for copy in waits:
            copy.wait()

    products = [jnp.dot(x_ref[...], w[...], preferred_element_type=jnp.float32) for w in (left_ref, right_ref)]
    groups = [[p[rows * n : rows * (n + 1)] for p in products] for n in range(BLOCKS)]
    if not keeps:
        put(out_ref, [g for pair in groups for g in pair])
        return
    for n, pair in enumerate(groups):
        totals = [g + take(got_ref, 2 * BLOCKS, 2 * n + side) for side, g in enumerate(pair)]
        for side, total in enumerate(totals):
            sums_ref[n, rows * side : rows * (side + 1), :] = total
        if n < SENT:
            put((s0_ref, s1_ref, s2_ref)[n], totals)


def cycle_call(sources, w, at, part, parts, got=(), after=(), tile=512):
    own, depth = sources[0].shape
    rows, width = own // 2, w.shape[1] // 2
    tiles = width // tile // parts
    first = part * tiles
    operands = [*sources, w, w]
    specs = [ANY] * len(sources) + [
        pl.BlockSpec((depth, tile), lambda n, at: (0, first + n)),
        pl.BlockSpec((depth, tile), lambda n, at: (0, parts * tiles + first + n)),
    ]
    scratch = [pltpu.VMEM((BLOCKS * rows, depth), jnp.bfloat16), pltpu.SemaphoreType.DMA((BLOCKS,))]
    if not got:
        out_shape = jax.ShapeDtypeStruct((2 * BLOCKS * rows + TRAILER, width // parts), jnp.int16)
        out_specs = pl.BlockSpec((2 * BLOCKS * rows + TRAILER, tile), lambda n, at: (0, n))
    else:
        per = tiles // len(got)
        for k, array in enumerate(got):
            operands.append(array)
            shape = (2 * BLOCKS * rows + TRAILER, tile)
            specs.append(pl.BlockSpec(shape, lambda n, at, k=k: (0, jnp.clip(n - k * per, 0, per - 1))))
        scratch.append(pltpu.VMEM((2 * BLOCKS * rows + TRAILER, tile), jnp.int16))
        out_shape = [jax.ShapeDtypeStruct((BLOCKS, own, width), jnp.float32)]
        out_shape += [jax.ShapeDtypeStruct((own + TRAILER, width), jnp.int16)] * SENT
        out_specs = [pl.BlockSpec((BLOCKS, own, tile), lambda n, at: (0, 0, n))]
        out_specs += [pl.BlockSpec((own + TRAILER, tile), lambda n, at: (0, n))] * SENT
    skip = len(after)
    return pl.pallas_call(
        functools.partial(cycle_kernel, keeps=len(got), skip=skip),
        grid_spec=pltpu.PrefetchScalarGridSpec(
            num_scalar_prefetch=1,
            grid=(tiles,),
            in_specs=specs + [ANY] * skip,
            out_specs=out_specs,
            scratch_shapes=scratch,
        ),
        out_shape=out_shape,
        compiler_params=params(),
        cost_estimate=light(),
    )(at, *operands, *after)


def hop_kernel(base_ref, *refs, groups, joins, skip):
    rows = base_ref.shape[1] // groups

    def send(got_ref):
        put(refs[joins + skip], [base_ref[0, rows * g : rows * (g + 1), :] + take(got_ref, groups, g) for g in range(groups)])

    if joins == 1:
        send(refs[0])
    else:
        for part in range(joins):
            pl.when(pl.program_id(0) == part)(functools.partial(send, refs[part]))


def hop(sums, place, got, groups=1, after=(), through=(), parts=2):
    rows, width = sums.shape[1], sums.shape[2]
    tile = width // parts
    got = got if isinstance(got, list) else [got]
    index = (lambda n: (0, n)) if len(got) == 1 else (lambda n: (0, 0))
    skip = len(through) + len(after)
    out = pl.pallas_call(
        functools.partial(hop_kernel, groups=groups, joins=len(got), skip=skip),
        grid=(parts,),
        in_specs=[pl.BlockSpec((1, rows, tile), lambda n: (place, 0, n))]
        + [pl.BlockSpec((rows + TRAILER, tile), index)] * len(got)
        + [ANY] * skip,
        out_specs=[pl.BlockSpec((rows + TRAILER, tile), lambda n: (0, n))] + [ANY] * len(through),
        out_shape=[jax.ShapeDtypeStruct((rows + TRAILER, width), jnp.int16)]
        + [jax.ShapeDtypeStruct(t.shape, t.dtype) for t in through],
        input_output_aliases={1 + len(got) + k: 1 + k for k in range(len(through))},
        compiler_params=params(),
        cost_estimate=light(),
    )(sums, *got, *through, *after)
    return out if through else out[0]


def fill(at_ref, first_code, groups, refs, x_ref, sems):
    @pl.when(pl.program_id(0) == 0)
    def _():
        waits, row, used = [], 0, 0
        for index, count in enumerate(groups):
            rows = refs[used].shape[0]
            target = x_ref.at[pl.ds(row, rows), :]
            waits.append(bring(refs[used : used + count], at_ref[first_code + index], target, sems.at[index]))
            row, used = row + rows, used + count
        for copy in waits:
            copy.wait()


def ladder_one_kernel(at_ref, *refs, groups, after):
    sources, w_ref = refs[: sum(groups)], refs[sum(groups)]
    out_ref, x_ref, sems = refs[sum(groups) + 1 + after :]
    fill(at_ref, 2, groups, sources, x_ref, sems)
    out_ref[...] = jnp.dot(x_ref[...], w_ref[...], preferred_element_type=jnp.float32)


def ladder_pair_kernel(at_ref, *refs, groups, after, prior):
    sources, w_ref = refs[: sum(groups)], refs[sum(groups)]
    prior_ref = refs[sum(groups) + 1]
    keep_ref, message_ref, x_ref, sems, part_ref = refs[sum(groups) + 1 + prior + after :]
    fill(at_ref, 2, groups, sources, x_ref, sems)
    product = jnp.dot(x_ref[...], w_ref[...], preferred_element_type=jnp.float32)
    rows = keep_ref.shape[1]
    if prior:
        part_ref[0] = prior_ref[...]
        part_ref[1] = product
    else:
        part_ref[0] = product[:rows]
        part_ref[1] = product[rows:]
    keep_ref[0] = part_ref[at_ref[1]]
    put(message_ref, [part_ref[1 - at_ref[1]]])


def ladder_call(groups, w, at, pair, prior=None, after=(), columns=1, heavy=False, tile=512):
    depth = groups[0][0].shape[1]
    total = sum(g[0].shape[0] for g in groups)
    width = w.shape[1] // columns
    tiles = width // tile
    counts = tuple(len(g) for g in groups)
    operands = [a for g in groups for a in g] + [w]
    specs = [ANY] * sum(counts) + [pl.BlockSpec((depth, tile), lambda n, at: (0, at[0] * tiles + n))]
    scratch = [pltpu.VMEM((total, depth), jnp.bfloat16), pltpu.SemaphoreType.DMA((len(counts),))]
    if pair:
        rows = total if prior is not None else total // 2
        if prior is not None:
            operands.append(prior)
            specs.append(pl.BlockSpec((rows, tile), lambda n, at: (0, at[0] * tiles + n)))
        kernel = functools.partial(ladder_pair_kernel, groups=counts, after=len(after), prior=int(prior is not None))
        out_shape = [
            jax.ShapeDtypeStruct((1, rows, width), jnp.float32),
            jax.ShapeDtypeStruct((rows + TRAILER, width), jnp.int16),
        ]
        out_specs = [
            pl.BlockSpec((1, rows, tile), lambda n, at: (0, 0, n)),
            pl.BlockSpec((rows + TRAILER, tile), lambda n, at: (0, n)),
        ]
        scratch.append(pltpu.VMEM((2, rows, tile), jnp.float32))
    else:
        kernel = functools.partial(ladder_one_kernel, groups=counts, after=len(after))
        out_shape = jax.ShapeDtypeStruct((total, width), jnp.float32)
        out_specs = pl.BlockSpec((total, tile), lambda n, at: (0, n))
    return pl.pallas_call(
        kernel,
        grid_spec=pltpu.PrefetchScalarGridSpec(
            num_scalar_prefetch=1,
            grid=(tiles,),
            in_specs=specs + [ANY] * len(after),
            out_specs=out_specs,
            scratch_shapes=scratch,
        ),
        out_shape=out_shape,
        compiler_params=params(),
        cost_estimate=light(2 * total * depth * width if heavy else 1000),
    )(at, *operands, *after)


def finish_kernel(at_ref, slab_ref, pair_ref, base_ref, *refs):
    *refs, out_ref, cycle_ref, ladder_ref = refs
    near, core = at_ref[0], at_ref[1]
    refs = list(refs)

    def next_refs(count):
        return [refs.pop(0) for _ in range(count)]

    def scaled(data_ref, trailer_ref, group):
        trailer = trailer_ref[group : group + 1, :].astype(jnp.int32).astype(jnp.float32)
        scale = jnp.exp2(trailer * (1.0 / STEPS)) * (1.0 / TOP)
        return data_ref[...].astype(jnp.int32).astype(jnp.float32) * scale

    base = next_refs(2)
    messages = [next_refs(3) for _ in range(3)]
    for side in range(2):
        cycle_ref[side] = base[side][0] + sum(scaled(m[side], m[2], side) for m in messages)

    block, lanes = out_ref.shape[2:]
    keep0 = next_refs(2)
    chunk0 = [next_refs(3) for _ in range(2)]
    keep1 = next_refs(2)
    chunk1 = [next_refs(3) for _ in range(2)]
    rows = keep0[0].shape[1]

    def spread(keep, chunk):
        for side in range(2):
            total = keep[side][0] + sum(scaled(m[side], m[2], 0) for m in chunk)
            for a in range(block):
                row = (a * 2 + side) * rows
                ladder_ref[row : row + rows, :] = total[:, a * lanes : (a + 1) * lanes]

    pl.when(near == 1)(functools.partial(spread, keep0, chunk0))
    pl.when(near != 1)(functools.partial(spread, keep1, chunk1))

    slab, occ = out_ref.shape[:2]
    per = occ // 2
    step = pl.program_id(0)

    def row(i, carry):
        energy = base_ref[...] - slab_ref[step * slab + i]
        for side in range(2):
            first = jnp.where(core == side, 0, rows)
            for j in range(per):
                ladder = ladder_ref[pl.ds(first + i * per + j, block, stride=2 * rows), :]
                place = pl.ds(pl.multiple_of(i * block, block), block)
                cycle = cycle_ref[side, place, j * lanes : (j + 1) * lanes]
                out_ref[i, side * per + j] = (ladder + cycle) / (energy - pair_ref[side * per + j])
        return carry

    lax.fori_loop(0, slab, row, 0)


def finish(at, slab_energy, pair_energy, base, sums, cycle, chunk0, chunk1, slab, steps=4):
    vir, lanes = base.shape
    occ = pair_energy.shape[0]
    mine, wide = sums.shape[1] // 2 // steps, sums.shape[2]
    operands, specs = [], []

    def add(array, shape, index):
        operands.append(array)
        specs.append(pl.BlockSpec(shape, index))

    def message(array, near=None):
        rows = (array.shape[0] - TRAILER) // 2 // steps
        width = array.shape[1]
        for side in range(2):
            if near is None:
                add(array, (rows, width), lambda n, *_, side=side: (side * steps + n, 0))
            else:
                add(array, (rows, width), lambda n, at, *_, side=side: (jnp.where(at[0] == near, side * steps + n, 0), 0))
        last = (array.shape[0] - TRAILER) // TRAILER
        add(array, (TRAILER, width), lambda n, *_: (last, 0))

    def kept(array, near):
        rows, width = array.shape[1] // 2 // steps, array.shape[2]
        for side in range(2):
            add(array, (1, rows, width), lambda n, at, *_, side=side: (0, jnp.where(at[0] == near, side * steps + n, 0), 0))

    for side in range(2):
        add(sums, (1, mine, wide), lambda n, *_, side=side: (SENT, side * steps + n, 0))
    for array in cycle:
        message(array)
    for near, (keep, *messages) in ((1, chunk0), (0, chunk1)):
        kept(keep, near)
        for array in messages:
            message(array, near)
    rows = chunk0[0].shape[1] // 2 // steps
    return pl.pallas_call(
        finish_kernel,
        grid_spec=pltpu.PrefetchScalarGridSpec(
            num_scalar_prefetch=3,
            grid=(steps,),
            in_specs=[pl.BlockSpec((vir, lanes), lambda n, *_: (0, 0))] + specs,
            out_specs=pl.BlockSpec((slab // steps, occ, vir, lanes), lambda n, *_: (n, 0, 0, 0)),
            scratch_shapes=[
                pltpu.VMEM((2, mine, wide), jnp.float32),
                pltpu.VMEM((2 * vir * rows, lanes), jnp.float32),
            ],
        ),
        out_shape=jax.ShapeDtypeStruct((slab, occ, vir, lanes), jnp.float32),
        compiler_params=params(),
        cost_estimate=light(),
    )(at, slab_energy, pair_energy, base, *operands)


def denominators(occ_energy, vir_energy, slab_index, occ_red, vir_block):
    orbital_ids = jnp.arange(occ_energy.shape[0], dtype=jnp.int32)
    chosen = slab_index[:, None] == orbital_ids[None, :]
    slab_energy = jnp.sum(jnp.where(chosen, occ_energy[None, :], jnp.float32(0.0)), axis=1)
    pair_energy = lax.dynamic_slice_in_dim(occ_energy, lax.axis_index("red") * occ_red, occ_red)
    first_virtual = lax.dynamic_slice_in_dim(vir_energy, lax.axis_index("blk") * vir_block, vir_block)
    return (
        first_virtual[None, None, :, None]
        + vir_energy[None, None, None, :]
        - slab_energy[:, None, None, None]
        - pair_energy[None, :, None, None]
    )


ORDER = ((3, 2, 1, 0), (3, 2, 0, 1), (0, 1, 3, 2), (0, 1, 2, 3))


def paired_shards(amplitudes, ladder_ints, cycle_ints, occ_energy, vir_energy, slab_index):
    slab, occ_local, vir_local, virt = amplitudes.shape
    blk, red = lax.axis_index("blk"), lax.axis_index("red")
    chip, core = blk // 2, blk % 2
    x_place = red % 2
    along_x = [(r, r ^ 1) for r in range(4)]
    along_y = [(r, r ^ 2) for r in range(4)]
    across = [(b, b ^ 1) for b in range(8)]

    def line(*hops):
        return [(2 * a + c, 2 * b + c) for a, b in hops for c in range(2)]

    def trade(pair):
        return lax.all_to_all(pair, "blk", 0, 0, axis_index_groups=[[2 * z, 2 * z + 1] for z in range(4)])

    inward, middle, outward = line((0, 1), (3, 2)), line((1, 2), (2, 1)), line((1, 0), (2, 3))

    def ints(*values):
        return jnp.stack([jnp.asarray(v, jnp.int32) for v in values])

    occ_red, vir_block = 2 * occ_local, vir_local // 2
    zeros = jnp.zeros((8,), jnp.int32)

    mine = amplitudes.reshape(slab, occ_local, 2, vir_block, virt)
    mine = jnp.transpose(mine, (2, 0, 3, 1, 4)).reshape(2 * slab * vir_block, occ_local * virt)
    rx = lax.ppermute(mine, "red", along_x)
    ry = lax.ppermute(mine, "red", along_y)

    own = amplitudes.reshape(slab * occ_local, vir_local * virt)
    g1 = lax.ppermute(own, "blk", line((0, 1), (1, 0), (2, 3), (3, 2)))
    g2 = lax.ppermute(own, "blk", middle)
    own_s = lax.ppermute(own, "blk", across)
    p_own = ladder_call([[own], [own_s]], ladder_ints, zeros, False)

    on_y, on_x, g1, g2 = forward(rx, ry, through=(g1, g2), after=(p_own,))
    rx2 = lax.ppermute(on_x, "red", along_x)
    ry2 = lax.ppermute(on_y, "red", along_y)
    g3 = lax.ppermute(g1, "blk", middle)
    g4 = lax.ppermute(g2, "blk", outward)
    g1_s = lax.ppermute(g1, "blk", across)
    g2_s = lax.ppermute(g2, "blk", across)
    g3_s = lax.ppermute(g3, "blk", across)
    g4_s = lax.ppermute(g4, "blk", across)
    near_x = ints(0, jnp.where(x_place == chip % 2, 0, 1), 0, 0)
    keep0, to_x = ladder_call([[g1], [g1_s]], ladder_ints, near_x, True, prior=p_own)
    x0 = lax.ppermute(to_x, "red", along_x)

    blocks = [mine, rx, ry, ry2, rx2]
    places = jnp.array(ORDER, jnp.int32)[chip] ^ red
    at_give, at_keep = jnp.concatenate([ints(1 - core), places]), jnp.concatenate([ints(core), places])
    give_a = cycle_call(blocks, cycle_ints, at_give, 0, 2, after=(keep0, g2_s))
    got_a = lax.ppermute(give_a, "blk", across)
    give_b = cycle_call(blocks, cycle_ints, at_give, 1, 2, after=(give_a, g3, g4))
    got_b = lax.ppermute(give_b, "blk", across)
    sums, s0, s1, s2 = cycle_call(blocks, cycle_ints, at_keep, 0, 1, [got_a, got_b])
    g5 = lax.ppermute(g3, "blk", outward)
    g5_s = lax.ppermute(g5, "blk", across)
    r0 = lax.ppermute(s0, "blk", inward)
    r1 = lax.ppermute(s1, "blk", inward)
    r2 = lax.ppermute(s2, "blk", inward)

    end = jnp.where((chip == 0) | (chip == 3), 1, 0)
    stays = jnp.where(x_place == chip // 2, 0, 1)
    rest = [[g2, g4], [g2_s, g4_s], [g3, g5], [g3_s, g5_s]]
    keep1, to_x = ladder_call(rest, ladder_ints, ints(0, stays, end, end, end, end), True, after=(sums,))
    x1 = lax.ppermute(to_x, "red", along_x)
    to_mid = hop(sums, 0, r0, 2, after=(keep1,))
    mid = lax.ppermute(to_mid, "blk", middle)
    to_y = hop(keep0, 0, x0, after=(to_mid,))
    y0 = lax.ppermute(to_y, "red", along_y)
    to_inner = hop(sums, 1, r1, 2, after=(to_y,))
    inner = lax.ppermute(to_inner, "blk", middle)
    to_y1 = hop(keep1, 0, x1, after=(to_inner,))
    y1 = lax.ppermute(to_y1, "red", along_y)
    to_outer = hop(sums, 2, mid, 2, after=(to_y1, y0))
    outer = lax.ppermute(to_outer, "blk", outward)

    orbital_ids = jnp.arange(occ_energy.shape[0], dtype=jnp.int32)
    chosen = slab_index[:, None] == orbital_ids[None, :]
    slab_energy = jnp.sum(jnp.where(chosen, occ_energy[None, :], jnp.float32(0.0)), axis=1)
    pair_energy = lax.dynamic_slice_in_dim(occ_energy, red * occ_red, occ_red)
    first_virtual = lax.dynamic_slice_in_dim(vir_energy, blk * vir_block, vir_block)
    base = first_virtual[:, None] + vir_energy[None, :]
    near = jnp.where(red // 2 == chip // 2, 1, 0)
    chunk1 = (keep1, x1, y1)
    cycle = [r2, inner, outer]
    return finish(ints(near, core), slab_energy, pair_energy, base, sums, cycle, (keep0, x0, y0), chunk1, slab)


def plain_shards(amplitudes, ladder_ints, cycle_ints, occ_energy, vir_energy, slab_index):
    slab_rows, occ_local, vir_local, virt_width = amplitudes.shape
    occ_all = occ_local * lax.axis_size("blk")
    occ_red = occ_all // lax.axis_size("red")
    shard_piece = lax.all_gather(amplitudes, "blk", axis=1, tiled=True)
    row_count = shard_piece.shape[1]
    flattened = shard_piece.reshape(slab_rows * row_count, vir_local * virt_width)
    product = jnp.dot(flattened, ladder_ints, preferred_element_type=jnp.float32)
    ladder = product.reshape(slab_rows, row_count, ladder_ints.shape[1])
    ladder_own = lax.psum_scatter(ladder, "red", scatter_dimension=1, tiled=True)
    ladder_own = ladder_own.reshape(slab_rows, occ_red, -1, virt_width)
    shard_piece = lax.all_gather(amplitudes, "red", axis=2, tiled=True)
    vir_count = shard_piece.shape[2]
    operand = jnp.transpose(shard_piece, (0, 2, 1, 3)).reshape(slab_rows * vir_count, occ_local * virt_width)
    product = jnp.dot(operand, cycle_ints, preferred_element_type=jnp.float32)
    cycle_term = product.reshape(slab_rows, vir_count, cycle_ints.shape[1])
    cycle_own = lax.psum_scatter(cycle_term, "blk", scatter_dimension=1, tiled=True)
    vir_block = cycle_own.shape[1]
    cycle_own = jnp.transpose(cycle_own.reshape(slab_rows, vir_block, occ_red, virt_width), (0, 2, 1, 3))
    return (ladder_own + cycle_own) / denominators(occ_energy, vir_energy, slab_index, occ_red, vir_block)


def solution(mesh):
    placed = (P(None, "blk", "red", None), P("red", "blk"), P("blk", "red"), P(), P(), P())
    shards = paired_shards if (mesh.shape["blk"], mesh.shape["red"]) == (8, 4) else plain_shards
    return jax.shard_map(
        shards, mesh=mesh, in_specs=placed, out_specs=P(None, "red", "blk", None), check_vma=False
    )
```

time: 583 us -> 308 us (0.53)
  waiting for transfers between devices: 456 us -> 95.5 us
  Pallas kernels: 0 us -> 154 us
  matrix products: 81.1 us -> 0 us
  starting transfers between devices: 0.12 us -> 34.7 us
  between operations: 13.1 us -> 0.43 us
    reduce_scatter x2 -> x0, waiting for transfers between devices: 320 us -> none  [the longest x1 244 us: shards(): lax.psum_scatter(cycle_term, 'blk', scatter_dimension=1, tiled=True)]
    pallas_call x0 -> x13, Pallas kernels: none -> 154 us  [the longest x3 69.5 us: cycle_call(): pl.pallas_call(functools.partial(cycle_kernel, keeps=len(got), skip=skip)...]
    all_gather x2 -> x0, waiting for transfers between devices: 135 us -> none  [the longest x1 116 us: shards(): shard_piece = lax.all_gather(amplitudes, 'blk', axis=1, tiled=True)]
    ppermute x0 -> x27, waiting for transfers between devices: none -> 95.5 us  [the longest x1 21.1 us: paired_shards(): y1 = lax.ppermute(to_y1, 'red', along_y)]
    dot_general x2 -> x0, matrix products: 81.1 us -> none  [the longest x1 46.6 us: shards(): product = jnp.dot(operand, cycle_ints, preferred_element_type=jnp.float32)]
    ppermute x0 -> x27, starting transfers between devices: none -> 34.7 us  [the longest x1 4.6 us: paired_shards(): g2 = lax.ppermute(own, 'blk', middle)]
    dot_general x1 -> x0, local copies, waits for them, and re-layouts: 19.6 us -> none  [shards(): jnp.dot(flattened, ladder_ints, preferred_element_type=jnp.float32)]
    unnamed x7 -> x48, local copies, waits for them, and re-layouts: 3.19 us -> 16.5 us
  transfers between devices with their start and end apart: 4 -> 27, of which waited for: 4 -> 16; matrix products, arithmetic and copies ran while one was open for 18% -> 2% of each run, Pallas kernels for 0% -> 39%
where the time goes in v1:
time: 308 us; the launch traced here: 307 us
  Pallas kernels  154 us (50%)
  waiting for transfers between devices  95.5 us (31%)
  starting transfers between devices  34.7 us (11%)
  local copies, waits for them, and re-layouts  19 us (6%)
  other arithmetic  4.01 us (1%)
    pallas_call x3, Pallas kernels, cycle_call(): pl.pallas_call(functools.partial(cycle_kernel, keeps=len(got), skip=skip)...  69.5 us
    pallas_call x3, Pallas kernels, ladder_call(): pl.pallas_call(kernel, grid_spec=pltpu.PrefetchScalarGridSpec(num_scalar_...  51.4 us
    ppermute x1, waiting for transfers between devices, paired_shards(): y1 = lax.ppermute(to_y1, 'red', along_y)  21.1 us
    ppermute x1, waiting for transfers between devices, paired_shards(): r1 = lax.ppermute(s1, 'blk', inward)  20.2 us
    pallas_call x5, Pallas kernels, hop(): pl.pallas_call(functools.partial(hop_kernel, groups=groups, joins=len(got...  18.8 us
    unnamed x48, local copies, waits for them, and re-layouts  16.5 us
    ppermute x1, waiting for transfers between devices, paired_shards(): rx = lax.ppermute(mine, 'red', along_x)  14 us
    pallas_call x1, Pallas kernels, finish(): pl.pallas_call(finish_kernel, grid_spec=pltpu.PrefetchScalarGridSpec(num_...  11.4 us
  transfers between devices with their start and end apart: 27, of which 16 were waited for; matrix products, arithmetic and copies ran while one was open for 2% of the time, Pallas kernels for 39%

profile of v1, /device:TPU:8, one launch (start us, length us, event | category | flops | bytes accessed | tf_op | source)
XLA Modules:
  0.0 307.4 jit_solution(12329418473782017099)
XLA Ops:
  0.0 3.4 %copy.16 = bf16[24,8,32,128]{3,1,2,0:T(8,128)(2,1)} copy(bf16[24,8,32,128]{3,2,1,0:T(8,128)(2,1)} %bitcast.25) | data formatting | bytes 3145728
  4.3 1.6 collective-permute-start
  7.9 4.6 %collective-permute-start.3 = (bf16[192,4096]{1,0:T(8,128)(2,1)}, bf16[192,4096]{1,0:T(8,128)(2,1)S(1)}, u32[]{:S(2)}, u32[]{:S(2)}) collective-permute-start(bf16[192,4096]{1,0:T(8,128)(2,1)} %bitcast.18.refs_0_), channel_id=1, source_target_pairs={{8,16},{12,20},{16,8},{20,12},{9,17},{13,21},{17,9},{21,13},{10,18... | collective-permute-start | bytes 4718600 | tf_op jit(solution)/shard_map/ppermute | solution.py:443
  13.0 14.2 %shard_map.73.refs_2_.refs_3_ = f32[384,2048]{1,0:T(8,128)} custom-call(s32[8]{0:T(128)} %broadcast_3_at_ref.2.at_ref, bf16[192,4096]{1,0:T(8,128)(2,1)} %bitcast.18.refs_0_, bf16[192,4096]{1,0:T(8,128)(2,1)} %collective-permute-done.4.refs_1_, bf16[4096,2048]{1,0:T(8,128)(2,1)} %refs_8_.1), custom_call_target="tpu_custom_call" | custom-call | flops 1000 | bytes 1000 | tf_op jit(solution)/shard_map/pallas_call | solution.py:275
  27.2 14.0 %collective-permute-done.rx_ref = bf16[256,3072]{1,0:T(8,128)(2,1)S(1)} collective-permute-done((bf16[256,3072]{1,0:T(8,128)(2,1)S(1)}, bf16[256,3072]{1,0:T(8,128)(2,1)S(1)}, u32[]{:S(2)}, u32[]{:S(2)}) %collective-permute-start) | collective-permute-done | bytes 1572896 | tf_op jit(solution)/shard_map/ppermute | solution.py:438
  43.9 3.0 collective-permute-done.3.refs_1_
  48.1 2.6 shard_map.74
  51.2 3.6 %collective-permute-start.10 = (bf16[192,4096]{1,0:T(8,128)(2,1)}, bf16[192,4096]{1,0:T(8,128)(2,1)}, u32[]{:S(2)}, u32[]{:S(2)}) collective-permute-start(bf16[192,4096]{1,0:T(8,128)(2,1)} %get-tuple-element.19.refs_0_), channel_id=1, source_target_pairs={{8,16},{12,20},{16,8},{20,12},{9,17},{13,21},{17,9},{21,13},{10,18... | collective-permute-start | bytes 4718600 | tf_op jit(solution)/shard_map/ppermute | solution.py:450
  54.8 2.5 collective-permute-start.11
  61.5 15.6 %shard_map.75 = (f32[1,384,2048]{2,1,0:T(8,128)}, s16[400,2048]{1,0:T(8,128)(2,1)}) custom-call(s32[4]{0:T(128)} %pad_add_fusion.3.at_ref, bf16[192,4096]{1,0:T(8,128)(2,1)} %get-tuple-element.19.refs_0_, bf16[192,4096]{1,0:T(8,128)(2,1)} %copy-done.19, bf16[4096,2048]{1,0:T(8,128)(2,1)} %refs_8_.1, f32[384,2048]{1,0:T(8,128)} %shard_map.73.refs_2_.refs_3_), custom_call_target="tpu_custom_call" | custom-call | flops 1000 | bytes 1000 | tf_op jit(solution)/shard_map/pallas_call | solution.py:275
  79.5 18.4 %shard_map.76.refs_0_ = s16[1040,1536]{1,0:T(8,128)(2,1)} custom-call(s32[5]{0:T(128)} %get-tuple-element.29.at_ref, bf16[256,3072]{1,0:T(8,128)(2,1)} %bitcast.22, bf16[256,3072]{1,0:T(8,128)(2,1)} %copy-done.4, bf16[256,3072]{1,0:T(8,128)(2,1)} %copy-done.5, bf16[128,3072]{1,0:T(8,128)(2,1)} %copy-done.9, bf16[128,3072]{1,0:T(8,128)(2,1)} %copy-done.10, ...), custom_call_target="tpu_custom_call" | custom-call | flops 1000 | bytes 1000 | tf_op jit(solution)/shard_map/pallas_call | solution.py:160
  97.9 18.6 %shard_map.77 = s16[1040,1536]{1,0:T(8,128)(2,1)} custom-call(s32[5]{0:T(128)} %get-tuple-element.29.at_ref, bf16[256,3072]{1,0:T(8,128)(2,1)} %bitcast.23, bf16[256,3072]{1,0:T(8,128)(2,1)} %copy-done.4, bf16[256,3072]{1,0:T(8,128)(2,1)} %copy-done.5, bf16[128,3072]{1,0:T(8,128)(2,1)} %copy-done.9, bf16[128,3072]{1,0:T(8,128)(2,1)} %copy-done.10, ...), custom_call_target="tpu_custom_call" | custom-call | flops 1000 | bytes 1000 | tf_op jit(solution)/shard_map/pallas_call | solution.py:160
  117.1 2.5 collective-permute-start.18
  119.5 6.7 %collective-permute-done.12.refs_1_ = s16[1040,1536]{1,0:T(8,128)(2,1)S(1)} collective-permute-done((s16[1040,1536]{1,0:T(8,128)(2,1)}, s16[1040,1536]{1,0:T(8,128)(2,1)S(1)}, u32[]{:S(2)}, u32[]{:S(2)}) %collective-permute-start.12) | collective-permute-done | bytes 3194912 | tf_op jit(solution)/shard_map/ppermute | solution.py:466
  126.9 2.0 copy-done.16
  128.8 32.5 %shard_map.78 = (f32[4,256,3072]{2,1,0:T(8,128)}, s16[272,3072]{1,0:T(8,128)(2,1)}, s16[272,3072]{1,0:T(8,128)(2,1)}, s16[272,3072]{1,0:T(8,128)(2,1)}) custom-call(s32[5]{0:T(128)} %get-tuple-element.30.at_ref, bf16[256,3072]{1,0:T(8,128)(2,1)} %bitcast.24, bf16[256,3072]{1,0:T(8,128)(2,1)} %copy-done.4, bf16[256,3072]{1,0:T(8,128)(2,1)} %copy-done.5, ...), custom_call_target="tpu_custom_call" | custom-call | flops 1000 | bytes 1000 | tf_op jit(solution)/shard_map/pallas_call | solution.py:160
  164.7 2.6 collective-permute-done.19.refs_6_
  169.5 2.2 collective-permute-done.20.refs_7_
  171.8 21.7 %shard_map.79 = (f32[1,384,2048]{2,1,0:T(8,128)}, s16[400,2048]{1,0:T(8,128)(2,1)}) custom-call(s32[6]{0:T(128)} %stack.39.at_ref, bf16[192,4096]{1,0:T(8,128)(2,1)} %get-tuple-element.21.refs_0_, bf16[192,4096]{1,0:T(8,128)(2,1)} %collective-permute-done.11.refs_2_.refs_1_, bf16[192,4096]{1,0:T(8,128)(2,1)} %copy-done.12, ...), custom_call_target="tpu_custom_call" | custom-call | flops 1000 | bytes 1000 | tf_op jit(solution)/shard_map/pallas_call | solution.py:275
  193.5 9.3 %collective-permute-done.16.refs_0_ = s16[272,3072]{1,0:T(8,128)(2,1)S(1)} collective-permute-done((s16[272,3072]{1,0:T(8,128)(2,1)}, s16[272,3072]{1,0:T(8,128)(2,1)S(1)}, u32[]{:S(2)}, u32[]{:S(2)}) %collective-permute-start.16) | collective-permute-done | bytes 1671200 | tf_op jit(solution)/shard_map/ppermute | solution.py:470
  204.0 3.8 %shard_map.80.refs_1_ = s16[272,3072]{1,0:T(8,128)(2,1)} custom-call(f32[4,256,3072]{2,1,0:T(8,128)} %get-tuple-element.22.refs_9_.base_ref.refs_0_.refs_1_, s16[272,3072]{1,0:T(8,128)(2,1)} %copy-done.17, f32[1,384,2048]{2,1,0:T(8,128)} %get-tuple-element.27.refs_1_.base_ref.refs_19_.refs_20_), custom_call_target="tpu_custom_call" | custom-call | flops 1000 | bytes 1000 | tf_op jit(solution)/shard_map/pallas_call | solution.py:194
  207.8 2.2 collective-permute-start.22
  212.0 3.8 %shard_map.81.refs_1_ = s16[400,2048]{1,0:T(8,128)(2,1)} custom-call(f32[1,384,2048]{2,1,0:T(8,128)} %get-tuple-element.20.refs_0_.base_ref.refs_11_.refs_12_, s16[400,2048]{1,0:T(8,128)(2,1)} %copy-done.1, s16[272,3072]{1,0:T(8,128)(2,1)} %shard_map.80.refs_1_), custom_call_target="tpu_custom_call" | custom-call | flops 1000 | bytes 1000 | tf_op jit(solution)/shard_map/pallas_call | solution.py:194
  218.6 20.2 %collective-permute-done.14.refs_0_ = s16[272,3072]{1,0:T(8,128)(2,1)} collective-permute-done((s16[272,3072]{1,0:T(8,128)(2,1)}, s16[272,3072]{1,0:T(8,128)(2,1)}, u32[]{:S(2)}, u32[]{:S(2)}) %collective-permute-start.14) | collective-permute-done | bytes 1671200 | tf_op jit(solution)/shard_map/ppermute | solution.py:471
  238.8 3.7 %shard_map.82.refs_1_ = s16[272,3072]{1,0:T(8,128)(2,1)} custom-call(f32[4,256,3072]{2,1,0:T(8,128)} %get-tuple-element.22.refs_9_.base_ref.refs_0_.refs_1_, s16[272,3072]{1,0:T(8,128)(2,1)} %collective-permute-done.14.refs_0_, s16[400,2048]{1,0:T(8,128)(2,1)} %shard_map.81.refs_1_), custom_call_target="tpu_custom_call" | custom-call | flops 1000 | bytes 1000 | tf_op jit(solution)/shard_map/pallas_call | solution.py:194
  242.5 2.2 collective-permute-start.21
  247.1 3.8 %shard_map.83.refs_1_ = s16[400,2048]{1,0:T(8,128)(2,1)} custom-call(f32[1,384,2048]{2,1,0:T(8,128)} %get-tuple-element.27.refs_1_.base_ref.refs_19_.refs_20_, s16[400,2048]{1,0:T(8,128)(2,1)} %copy-done.2, s16[272,3072]{1,0:T(8,128)(2,1)} %shard_map.82.refs_1_), custom_call_target="tpu_custom_call" | custom-call | flops 1000 | bytes 1000 | tf_op jit(solution)/shard_map/pallas_call | solution.py:194
  253.8 3.8 %shard_map.84 = s16[272,3072]{1,0:T(8,128)(2,1)} custom-call(f32[4,256,3072]{2,1,0:T(8,128)} %get-tuple-element.22.refs_9_.base_ref.refs_0_.refs_1_, s16[272,3072]{1,0:T(8,128)(2,1)} %copy-done.18, s16[400,2048]{1,0:T(8,128)(2,1)} %shard_map.83.refs_1_, s16[400,2048]{1,0:T(8,128)(2,1)} %copy-done), custom_call_target="tpu_custom_call" | custom-call | flops 1000 | bytes 1000 | tf_op jit(solution)/shard_map/pallas_call | solution.py:194
  257.5 2.5 collective-permute-start.25
  264.2 9.3 %collective-permute-done.13.refs_2_.refs_3_.refs_4_ = s16[272,3072]{1,0:T(8,128)(2,1)S(1)} collective-permute-done((s16[272,3072]{1,0:T(8,128)(2,1)}, s16[272,3072]{1,0:T(8,128)(2,1)S(1)}, u32[]{:S(2)}, u32[]{:S(2)}) %collective-permute-start.13) | collective-permute-done | bytes 1671200 | tf_op jit(solution)/shard_map/ppermute | solution.py:472
  273.6 21.1 %collective-permute-done.26.refs_24_.refs_25_.refs_26_ = s16[400,2048]{1,0:T(8,128)(2,1)S(1)} collective-permute-done((s16[400,2048]{1,0:T(8,128)(2,1)}, s16[400,2048]{1,0:T(8,128)(2,1)S(1)}, u32[]{:S(2)}, u32[]{:S(2)}) %collective-permute-start.26) | collective-permute-done | bytes 1638432 | tf_op jit(solution)/shard_map/ppermute | solution.py:486
  295.9 11.4 %shard_map.85 = f32[8,48,16,128]{3,2,1,0:T(8,128)} custom-call(s32[2]{0:T(128)} %pad_add_fusion.at_ref, f32[8]{0:T(128)} %select_reduce_fusion.slab_ref, f32[48]{0:T(128)} %dynamic_slice.9.pair_ref, f32[16,128]{1,0:T(8,128)} %broadcast_add_fusion.base_ref, f32[4,256,3072]{2,1,0:T(8,128)} %get-tuple-element.22.refs_9_.base_ref.refs_0_.refs_1_, ...), custom_call_target="tpu_custom_call" | custom-call | flops 1000 | bytes 1000 | tf_op jit(solution)/shard_map/pallas_call | solution.py:378
  (95 shorter events, 37.8 us)
Async XLA Ops:
  3.4 9.1 %collective-permute-start.4 = (bf16[192,4096]{1,0:T(8,128)(2,1)}, bf16[192,4096]{1,0:T(8,128)(2,1)}, u32[]{:S(2)}, u32[]{:S(2)}) collective-permute-start(bf16[192,4096]{1,0:T(8,128)(2,1)} %bitcast.18.refs_0_), channel_id=1, source_target_pairs={{0,4},{4,0},{8,12},{12,8},{16,20},{20,16},{24,28},{28,24},{1,5},{5... | collective-permute-start | bytes 4718600 | tf_op jit(solution)/shard_map/ppermute | solution.py:444
  4.3 22.8 %copy-start.3 = (bf16[32,8,24,128]{3,1,2,0:T(8,128)(2,1)}, bf16[32,8,24,128]{3,1,2,0:T(8,128)(2,1)S(1)}, u32[]{:S(2)}) copy-start(bf16[32,8,24,128]{3,1,2,0:T(8,128)(2,1)S(1)} %copy.17) | copy-start | bytes 4718596
  4.3 36.9 %collective-permute-start = (bf16[256,3072]{1,0:T(8,128)(2,1)S(1)}, bf16[256,3072]{1,0:T(8,128)(2,1)S(1)}, u32[]{:S(2)}, u32[]{:S(2)}) collective-permute-start(bf16[256,3072]{1,0:T(8,128)(2,1)S(1)} %bitcast.20), channel_id=1, source_target_pairs={{0,1},{1,0},{2,3},{3,2},{4,5},{5,4},{6,7},{7,6},{8,9},{9,8},{10,11... | collective-permute-start | bytes 4718600 | tf_op jit(solution)/shard_map/ppermute | solution.py:438
  5.9 36.5 %collective-permute-start.1 = (bf16[256,3072]{1,0:T(8,128)(2,1)S(1)}, bf16[256,3072]{1,0:T(8,128)(2,1)S(1)}, u32[]{:S(2)}, u32[]{:S(2)}) collective-permute-start(bf16[256,3072]{1,0:T(8,128)(2,1)S(1)} %bitcast.21), channel_id=1, source_target_pairs={{0,2},{1,3},{2,0},{3,1},{4,6},{5,7},{6,4},{7,5},{8,10},{9,11},{10,... | collective-permute-start | bytes 4718600 | tf_op jit(solution)/shard_map/ppermute | solution.py:439
  7.4 36.5 %collective-permute-start.2 = (bf16[192,4096]{1,0:T(8,128)(2,1)}, bf16[192,4096]{1,0:T(8,128)(2,1)S(1)}, u32[]{:S(2)}, u32[]{:S(2)}) collective-permute-start(bf16[192,4096]{1,0:T(8,128)(2,1)} %bitcast.18.refs_0_), channel_id=1, source_target_pairs={{0,8},{4,12},{8,0},{12,4},{16,24},{20,28},{24,16},{28,20},{1,9},{5... | collective-permute-start | bytes 4718600 | tf_op jit(solution)/shard_map/ppermute | solution.py:442
  7.9 39.0 %collective-permute-start.3 = (bf16[192,4096]{1,0:T(8,128)(2,1)}, bf16[192,4096]{1,0:T(8,128)(2,1)S(1)}, u32[]{:S(2)}, u32[]{:S(2)}) collective-permute-start(bf16[192,4096]{1,0:T(8,128)(2,1)} %bitcast.18.refs_0_), channel_id=1, source_target_pairs={{8,16},{12,20},{16,8},{20,12},{9,17},{13,21},{17,9},{21,13},{10,18... | collective-permute-start | bytes 4718600 | tf_op jit(solution)/shard_map/ppermute | solution.py:443
  50.7 7.1 %collective-permute-start.7 = (bf16[192,4096]{1,0:T(8,128)(2,1)}, bf16[192,4096]{1,0:T(8,128)(2,1)S(1)}, u32[]{:S(2)}, u32[]{:S(2)}) collective-permute-start(bf16[192,4096]{1,0:T(8,128)(2,1)} %get-tuple-element.19.refs_0_), channel_id=1, source_target_pairs={{0,4},{4,0},{8,12},{12,8},{16,20},{20,16},{24,28},{28,24},{1,5},{5... | collective-permute-start | bytes 4718600 | tf_op jit(solution)/shard_map/ppermute | solution.py:452
  50.7 27.4 %collective-permute-start.8 = (bf16[192,4096]{1,0:T(8,128)(2,1)}, bf16[192,4096]{1,0:T(8,128)(2,1)S(1)}, u32[]{:S(2)}, u32[]{:S(2)}) collective-permute-start(bf16[192,4096]{1,0:T(8,128)(2,1)} %get-tuple-element.21.refs_0_), channel_id=1, source_target_pairs={{0,4},{4,0},{8,12},{12,8},{16,20},{20,16},{24,28},{28,24},{1,5},{5... | collective-permute-start | bytes 4718600 | tf_op jit(solution)/shard_map/ppermute | solution.py:453
  51.2 46.7 %collective-permute-start.10 = (bf16[192,4096]{1,0:T(8,128)(2,1)}, bf16[192,4096]{1,0:T(8,128)(2,1)}, u32[]{:S(2)}, u32[]{:S(2)}) collective-permute-start(bf16[192,4096]{1,0:T(8,128)(2,1)} %get-tuple-element.19.refs_0_), channel_id=1, source_target_pairs={{8,16},{12,20},{16,8},{20,12},{9,17},{13,21},{17,9},{21,13},{10,18... | collective-permute-start | bytes 4718600 | tf_op jit(solution)/shard_map/ppermute | solution.py:450
  54.8 43.0 %collective-permute-start.11 = (bf16[192,4096]{1,0:T(8,128)(2,1)}, bf16[192,4096]{1,0:T(8,128)(2,1)}, u32[]{:S(2)}, u32[]{:S(2)}) collective-permute-start(bf16[192,4096]{1,0:T(8,128)(2,1)} %get-tuple-element.21.refs_0_), channel_id=1, source_target_pairs={{8,0},{12,4},{16,24},{20,28},{9,1},{13,5},{17,25},{21,29},{10,2},{... | collective-permute-start | bytes 4718600 | tf_op jit(solution)/shard_map/ppermute | solution.py:451
  57.3 19.8 %collective-permute-start.5 = (bf16[128,3072]{1,0:T(8,128)(2,1)}, bf16[128,3072]{1,0:T(8,128)(2,1)S(1)}, u32[]{:S(2)}, u32[]{:S(2)}) collective-permute-start(bf16[128,3072]{1,0:T(8,128)(2,1)} %get-tuple-element.17), channel_id=1, source_target_pairs={{0,2},{1,3},{2,0},{3,1},{4,6},{5,7},{6,4},{7,5},{8,10},{9,11},{10,... | collective-permute-start | bytes 2359304 | tf_op jit(solution)/shard_map/ppermute | solution.py:449
  59.0 19.1 %collective-permute-start.6 = (bf16[128,3072]{1,0:T(8,128)(2,1)}, bf16[128,3072]{1,0:T(8,128)(2,1)S(1)}, u32[]{:S(2)}, u32[]{:S(2)}) collective-permute-start(bf16[128,3072]{1,0:T(8,128)(2,1)} %get-tuple-element.18), channel_id=1, source_target_pairs={{0,1},{1,0},{2,3},{3,2},{4,5},{5,4},{6,7},{7,6},{8,9},{9,8},{10,11... | collective-permute-start | bytes 2359304 | tf_op jit(solution)/shard_map/ppermute | solution.py:448
  97.8 18.7 %copy-start.8 = (s16[1040,1536]{1,0:T(8,128)(2,1)S(1)}, s16[1040,1536]{1,0:T(8,128)(2,1)}, u32[]{:S(2)}) copy-start(s16[1040,1536]{1,0:T(8,128)(2,1)} %shard_map.76.refs_0_) | copy-start | bytes 9584644
  116.5 9.7 %collective-permute-start.12 = (s16[1040,1536]{1,0:T(8,128)(2,1)}, s16[1040,1536]{1,0:T(8,128)(2,1)S(1)}, u32[]{:S(2)}, u32[]{:S(2)}) collective-permute-start(s16[1040,1536]{1,0:T(8,128)(2,1)} %shard_map.77), channel_id=1, source_target_pairs={{0,4},{4,0},{8,12},{12,8},{16,20},{20,16},{24,28},{28,24},{1,5},{5... | collective-permute-start | bytes 9584648 | tf_op jit(solution)/shard_map/ppermute | solution.py:466
  116.6 10.3 %collective-permute-start.9 = (s16[1040,1536]{1,0:T(8,128)(2,1)S(1)}, s16[1040,1536]{1,0:T(8,128)(2,1)S(1)}, u32[]{:S(2)}, u32[]{:S(2)}) collective-permute-start(s16[1040,1536]{1,0:T(8,128)(2,1)S(1)} %copy-done.8), channel_id=1, source_target_pairs={{0,4},{4,0},{8,12},{12,8},{16,20},{20,16},{24,28},{28,24},{1,5},{5... | collective-permute-start | bytes 9584648 | tf_op jit(solution)/shard_map/ppermute | solution.py:464
  117.1 47.0 %collective-permute-start.18 = (bf16[192,4096]{1,0:T(8,128)(2,1)}, bf16[192,4096]{1,0:T(8,128)(2,1)}, u32[]{:S(2)}, u32[]{:S(2)}) collective-permute-start(bf16[192,4096]{1,0:T(8,128)(2,1)} %collective-permute-done.10.refs_1_.refs_4_), channel_id=1, source_target_pairs={{8,0},{12,4},{16,24},{20,28},{9,1},{13,5},{17,25},{21,29},{10,2},{... | collective-permute-start | bytes 4718600 | tf_op jit(solution)/shard_map/ppermute | solution.py:468
  161.4 41.5 %collective-permute-start.16 = (s16[272,3072]{1,0:T(8,128)(2,1)}, s16[272,3072]{1,0:T(8,128)(2,1)S(1)}, u32[]{:S(2)}, u32[]{:S(2)}) collective-permute-start(s16[272,3072]{1,0:T(8,128)(2,1)} %get-tuple-element.26), channel_id=1, source_target_pairs={{0,8},{4,12},{24,16},{28,20},{1,9},{5,13},{25,17},{29,21},{2,10},{... | collective-permute-start | bytes 5013512 | tf_op jit(solution)/shard_map/ppermute | solution.py:470
  162.7 48.2 %collective-permute-start.15 = (s16[400,2048]{1,0:T(8,128)(2,1)}, s16[400,2048]{1,0:T(8,128)(2,1)S(1)}, u32[]{:S(2)}, u32[]{:S(2)}) collective-permute-start(s16[400,2048]{1,0:T(8,128)(2,1)} %get-tuple-element.25), channel_id=1, source_target_pairs={{0,1},{1,0},{2,3},{3,2},{4,5},{5,4},{6,7},{7,6},{8,9},{9,8},{10,11... | collective-permute-start | bytes 4915208 | tf_op jit(solution)/shard_map/ppermute | solution.py:458
  163.5 3.8 %collective-permute-start.19 = (bf16[192,4096]{1,0:T(8,128)(2,1)}, bf16[192,4096]{1,0:T(8,128)(2,1)}, u32[]{:S(2)}, u32[]{:S(2)}) collective-permute-start(bf16[192,4096]{1,0:T(8,128)(2,1)} %collective-permute-done.10.refs_1_.refs_4_), channel_id=1, source_target_pairs={{0,4},{4,0},{8,12},{12,8},{16,20},{20,16},{24,28},{28,24},{1,5},{5... | collective-permute-start | bytes 4718600 | tf_op jit(solution)/shard_map/ppermute | solution.py:454
  163.5 6.0 %collective-permute-start.17 = (bf16[192,4096]{1,0:T(8,128)(2,1)}, bf16[192,4096]{1,0:T(8,128)(2,1)}, u32[]{:S(2)}, u32[]{:S(2)}) collective-permute-start(bf16[192,4096]{1,0:T(8,128)(2,1)} %collective-permute-done.11.refs_2_.refs_1_), channel_id=1, source_target_pairs={{0,4},{4,0},{8,12},{12,8},{16,20},{20,16},{24,28},{28,24},{1,5},{5... | collective-permute-start | bytes 4718600 | tf_op jit(solution)/shard_map/ppermute | solution.py:455
  164.0 7.7 %collective-permute-start.20 = (bf16[192,4096]{1,0:T(8,128)(2,1)}, bf16[192,4096]{1,0:T(8,128)(2,1)}, u32[]{:S(2)}, u32[]{:S(2)}) collective-permute-start(bf16[192,4096]{1,0:T(8,128)(2,1)} %collective-permute-done.18.refs_5_), channel_id=1, source_target_pairs={{0,4},{4,0},{8,12},{12,8},{16,20},{20,16},{24,28},{28,24},{1,5},{5... | collective-permute-start | bytes 4718600 | tf_op jit(solution)/shard_map/ppermute | solution.py:469
  167.3 71.5 %collective-permute-start.14 = (s16[272,3072]{1,0:T(8,128)(2,1)}, s16[272,3072]{1,0:T(8,128)(2,1)}, u32[]{:S(2)}, u32[]{:S(2)}) collective-permute-start(s16[272,3072]{1,0:T(8,128)(2,1)} %get-tuple-element.24), channel_id=1, source_target_pairs={{0,8},{4,12},{24,16},{28,20},{1,9},{5,13},{25,17},{29,21},{2,10},{... | collective-permute-start | bytes 5013512 | tf_op jit(solution)/shard_map/ppermute | solution.py:471
  207.8 43.6 %collective-permute-start.22 = (s16[272,3072]{1,0:T(8,128)(2,1)}, s16[272,3072]{1,0:T(8,128)(2,1)S(1)}, u32[]{:S(2)}, u32[]{:S(2)}) collective-permute-start(s16[272,3072]{1,0:T(8,128)(2,1)} %shard_map.80.refs_1_), channel_id=1, source_target_pairs={{8,16},{12,20},{16,8},{20,12},{9,17},{13,21},{17,9},{21,13},{10,18... | collective-permute-start | bytes 5013512 | tf_op jit(solution)/shard_map/ppermute | solution.py:480
  210.0 36.0 %collective-permute-start.23 = (s16[400,2048]{1,0:T(8,128)(2,1)}, s16[400,2048]{1,0:T(8,128)(2,1)S(1)}, u32[]{:S(2)}, u32[]{:S(2)}) collective-permute-start(s16[400,2048]{1,0:T(8,128)(2,1)} %get-tuple-element.28), channel_id=1, source_target_pairs={{0,1},{1,0},{2,3},{3,2},{4,5},{5,4},{6,7},{7,6},{8,9},{9,8},{10,11... | collective-permute-start | bytes 4915208 | tf_op jit(solution)/shard_map/ppermute | solution.py:478
  215.8 35.6 %collective-permute-start.24 = (s16[400,2048]{1,0:T(8,128)(2,1)}, s16[400,2048]{1,0:T(8,128)(2,1)S(1)}, u32[]{:S(2)}, u32[]{:S(2)}) collective-permute-start(s16[400,2048]{1,0:T(8,128)(2,1)} %shard_map.81.refs_1_), channel_id=1, source_target_pairs={{0,2},{1,3},{2,0},{3,1},{4,6},{5,7},{6,4},{7,5},{8,10},{9,11},{10,... | collective-permute-start | bytes 4915208 | tf_op jit(solution)/shard_map/ppermute | solution.py:482
  217.3 56.3 %collective-permute-start.13 = (s16[272,3072]{1,0:T(8,128)(2,1)}, s16[272,3072]{1,0:T(8,128)(2,1)S(1)}, u32[]{:S(2)}, u32[]{:S(2)}) collective-permute-start(s16[272,3072]{1,0:T(8,128)(2,1)} %get-tuple-element.23), channel_id=1, source_target_pairs={{0,8},{4,12},{24,16},{28,20},{1,9},{5,13},{25,17},{29,21},{2,10},{... | collective-permute-start | bytes 5013512 | tf_op jit(solution)/shard_map/ppermute | solution.py:472
  242.5 52.2 %collective-permute-start.21 = (s16[272,3072]{1,0:T(8,128)(2,1)}, s16[272,3072]{1,0:T(8,128)(2,1)}, u32[]{:S(2)}, u32[]{:S(2)}) collective-permute-start(s16[272,3072]{1,0:T(8,128)(2,1)} %shard_map.82.refs_1_), channel_id=1, source_target_pairs={{8,16},{12,20},{16,8},{20,12},{9,17},{13,21},{17,9},{21,13},{10,18... | collective-permute-start | bytes 5013512 | tf_op jit(solution)/shard_map/ppermute | solution.py:484
  250.9 11.2 %copy-start.21 = (f32[128]{0:T(128)S(1)}, f32[128]{0:T(128)}, u32[]{:S(2)}) copy-start(f32[128]{0:T(128)} %param.11) | copy-start | bytes 1540
  250.9 11.9 %copy-start.22 = (s32[8]{0:T(128)S(1)}, s32[8]{0:T(128)}, u32[]{:S(2)}) copy-start(s32[8]{0:T(128)} %param.12) | copy-start | bytes 100
  257.5 37.2 %collective-permute-start.25 = (s16[272,3072]{1,0:T(8,128)(2,1)}, s16[272,3072]{1,0:T(8,128)(2,1)}, u32[]{:S(2)}, u32[]{:S(2)}) collective-permute-start(s16[272,3072]{1,0:T(8,128)(2,1)} %shard_map.84), channel_id=1, source_target_pairs={{8,0},{12,4},{16,24},{20,28},{9,1},{13,5},{17,25},{21,29},{10,2},{... | collective-permute-start | bytes 5013512 | tf_op jit(solution)/shard_map/ppermute | solution.py:488
  260.0 34.7 %collective-permute-start.26 = (s16[400,2048]{1,0:T(8,128)(2,1)}, s16[400,2048]{1,0:T(8,128)(2,1)S(1)}, u32[]{:S(2)}, u32[]{:S(2)}) collective-permute-start(s16[400,2048]{1,0:T(8,128)(2,1)} %shard_map.83.refs_1_), channel_id=1, source_target_pairs={{0,2},{1,3},{2,0},{3,1},{4,6},{5,7},{6,4},{7,5},{8,10},{9,11},{10,... | collective-permute-start | bytes 4915208 | tf_op jit(solution)/shard_map/ppermute | solution.py:486
  273.5 21.2 %copy-start.6 = (s16[272,3072]{1,0:T(8,128)(2,1)}, s16[272,3072]{1,0:T(8,128)(2,1)S(1)}, u32[]{:S(2)}) copy-start(s16[272,3072]{1,0:T(8,128)(2,1)S(1)} %collective-permute-done.13.refs_2_.refs_3_.refs_4_) | copy-start | bytes 5013508
  (18 other events, 44.5 us)

commit v2 on v1

--- a/solution.py
+++ b/solution.py
@@ -8,13 +8,14 @@
 from jax.sharding import PartitionSpec as P
 
 TRAILER = 16
+WIDE = 32
 STEPS = 64.0
 TOP = 32000.0
 VMEM = 56 * 2**20
 
 
-def encode(groups):
-    rows = lax.broadcasted_iota(jnp.int32, (TRAILER, groups[0].shape[1]), 0)
+def encode(groups, last):
+    rows = lax.broadcasted_iota(jnp.int32, (last, groups[0].shape[1]), 0)
     trailer = jnp.zeros_like(rows)
     parts = []
     for index, group in enumerate(groups):
@@ -26,17 +27,17 @@
     return parts, trailer.astype(jnp.int16)
 
 
-def put(ref, groups):
-    parts, trailer = encode(groups)
+def put(ref, groups, last=TRAILER):
+    parts, trailer = encode(groups, last)
     row = 0
     for part in parts:
         ref[row : row + part.shape[0], :] = part
         row += part.shape[0]
-    ref[row : row + TRAILER, :] = trailer
-
-
-def take(ref, groups, index):
-    rows = (ref.shape[0] - TRAILER) // groups
+    ref[row : row + last, :] = trailer
+
+
+def take(ref, groups, index, last=TRAILER):
+    rows = (ref.shape[0] - last) // groups
     trailer = ref[groups * rows :, :].astype(jnp.int32).astype(jnp.float32)
     scale = jnp.exp2(trailer[index : index + 1, :] * (1.0 / STEPS)) * (1.0 / TOP)
     return ref[index * rows : (index + 1) * rows, :].astype(jnp.int32).astype(jnp.float32) * scale
@@ -46,8 +47,8 @@
     return pltpu.CompilerParams(vmem_limit_bytes=VMEM, dimension_semantics=("arbitrary",))
 
 
-def light(flops=1000):
-    return pl.CostEstimate(flops=flops, bytes_accessed=1000, transcendentals=0)
+def light(weight=0):
+    return pl.CostEstimate(flops=weight * 1150000000 + 1000, bytes_accessed=1000, transcendentals=0)
 
 
 def bring(candidates, code, target, sem):
@@ -88,19 +89,13 @@
 
 BLOCKS = 4
 SENT = 3
+PARTS = 2
 
 
 def cycle_kernel(at_ref, own_ref, rx_ref, ry_ref, ry2_ref, rx2_ref, left_ref, right_ref, *refs, keeps, skip):
     if keeps:
-        got, refs = refs[:keeps], refs[keeps:]
-        sums_ref, s0_ref, s1_ref, s2_ref = refs[skip : 4 + skip]
-        x_ref, sems, got_ref = refs[-3:]
-        for part, part_ref in enumerate(got):
-
-            @pl.when(pl.program_id(0) // (pl.num_programs(0) // keeps) == part)
-            def _(part_ref=part_ref):
-                got_ref[...] = part_ref[...]
-
+        got_ref = refs[0]
+        sums_ref, s0_ref, s1_ref, s2_ref, x_ref, sems = refs[1 + skip :]
     else:
         out_ref, x_ref, sems = refs[skip:]
     rows = ry2_ref.shape[0]
@@ -131,52 +126,59 @@
             put((s0_ref, s1_ref, s2_ref)[n], totals)
 
 
-def cycle_call(sources, w, at, part, parts, got=(), after=(), tile=512):
+def cycle_call(sources, w, at, part, got=None, before=(), after=(), tile=512):
     own, depth = sources[0].shape
     rows, width = own // 2, w.shape[1] // 2
-    tiles = width // tile // parts
+    tiles = width // tile // PARTS
     first = part * tiles
     operands = [*sources, w, w]
     specs = [ANY] * len(sources) + [
         pl.BlockSpec((depth, tile), lambda n, at: (0, first + n)),
-        pl.BlockSpec((depth, tile), lambda n, at: (0, parts * tiles + first + n)),
+        pl.BlockSpec((depth, tile), lambda n, at: (0, PARTS * tiles + first + n)),
     ]
-    scratch = [pltpu.VMEM((BLOCKS * rows, depth), jnp.bfloat16), pltpu.SemaphoreType.DMA((BLOCKS,))]
-    if not got:
-        out_shape = jax.ShapeDtypeStruct((2 * BLOCKS * rows + TRAILER, width // parts), jnp.int16)
-        out_specs = pl.BlockSpec((2 * BLOCKS * rows + TRAILER, tile), lambda n, at: (0, n))
+    given = pl.BlockSpec((2 * BLOCKS * rows + TRAILER, tile), lambda n, at: (0, n))
+    aliases = {}
+    if got is None:
+        out_shape = jax.ShapeDtypeStruct((2 * BLOCKS * rows + TRAILER, width // PARTS), jnp.int16)
+        out_specs = given
     else:
-        per = tiles // len(got)
-        for k, array in enumerate(got):
-            operands.append(array)
-            shape = (2 * BLOCKS * rows + TRAILER, tile)
-            specs.append(pl.BlockSpec(shape, lambda n, at, k=k: (0, jnp.clip(n - k * per, 0, per - 1))))
-        scratch.append(pltpu.VMEM((2 * BLOCKS * rows + TRAILER, tile), jnp.int16))
-        out_shape = [jax.ShapeDtypeStruct((BLOCKS, own, width), jnp.float32)]
-        out_shape += [jax.ShapeDtypeStruct((own + TRAILER, width), jnp.int16)] * SENT
-        out_specs = [pl.BlockSpec((BLOCKS, own, tile), lambda n, at: (0, 0, n))]
-        out_specs += [pl.BlockSpec((own + TRAILER, tile), lambda n, at: (0, n))] * SENT
-    skip = len(after)
+        operands.append(got)
+        specs.append(given)
+        if before:
+            aliases = {1 + len(operands): 0, 2 + len(operands): 2, 3 + len(operands): 3}
+        message = jax.ShapeDtypeStruct((own + TRAILER, width), jnp.int16)
+        out_shape = [
+            jax.ShapeDtypeStruct((BLOCKS, own, width), jnp.float32),
+            jax.ShapeDtypeStruct((own + TRAILER, width // PARTS), jnp.int16),
+            message,
+            message,
+        ]
+        out_specs = [
+            pl.BlockSpec((BLOCKS, own, tile), lambda n, at: (0, 0, first + n)),
+            pl.BlockSpec((own + TRAILER, tile), lambda n, at: (0, n)),
+        ] + [pl.BlockSpec((own + TRAILER, tile), lambda n, at: (0, first + n))] * 2
+    skip = len(before) + len(after)
     return pl.pallas_call(
-        functools.partial(cycle_kernel, keeps=len(got), skip=skip),
+        functools.partial(cycle_kernel, keeps=got is not None, skip=skip),
         grid_spec=pltpu.PrefetchScalarGridSpec(
             num_scalar_prefetch=1,
             grid=(tiles,),
             in_specs=specs + [ANY] * skip,
             out_specs=out_specs,
-            scratch_shapes=scratch,
+            scratch_shapes=[pltpu.VMEM((BLOCKS * rows, depth), jnp.bfloat16), pltpu.SemaphoreType.DMA((BLOCKS,))],
         ),
         out_shape=out_shape,
+        input_output_aliases=aliases,
         compiler_params=params(),
-        cost_estimate=light(),
-    )(at, *operands, *after)
-
-
-def hop_kernel(base_ref, *refs, groups, joins, skip):
-    rows = base_ref.shape[1] // groups
+        cost_estimate=light(19),
+    )(at, *operands, *before, *after)
+
+
+def hop_kernel(base_ref, *refs, joins, skip, trailer):
+    rows = base_ref.shape[1] // 2
 
     def send(got_ref):
-        put(refs[joins + skip], [base_ref[0, rows * g : rows * (g + 1), :] + take(got_ref, groups, g) for g in range(groups)])
+        put(refs[joins + skip], [base_ref[0, rows * g : rows * (g + 1), :] + take(got_ref, 2, g) for g in range(2)], trailer)
 
     if joins == 1:
         send(refs[0])
@@ -185,24 +187,23 @@
             pl.when(pl.program_id(0) == part)(functools.partial(send, refs[part]))
 
 
-def hop(sums, place, got, groups=1, after=(), through=(), parts=2):
-    rows, width = sums.shape[1], sums.shape[2]
-    tile = width // parts
-    got = got if isinstance(got, list) else [got]
-    index = (lambda n: (0, n)) if len(got) == 1 else (lambda n: (0, 0))
+def hop(sums, place, got, part=0, parts=1, through=(), after=(), weight=4, trailer=TRAILER):
+    rows, tile = sums.shape[1], sums.shape[2] // 2
+    joins = len(got)
     skip = len(through) + len(after)
+    index = (lambda n: (0, n)) if joins == 1 else (lambda n: (0, 0))
     out = pl.pallas_call(
-        functools.partial(hop_kernel, groups=groups, joins=len(got), skip=skip),
+        functools.partial(hop_kernel, joins=joins, skip=skip, trailer=trailer),
         grid=(parts,),
-        in_specs=[pl.BlockSpec((1, rows, tile), lambda n: (place, 0, n))]
-        + [pl.BlockSpec((rows + TRAILER, tile), index)] * len(got)
+        in_specs=[pl.BlockSpec((1, rows, tile), lambda n: (place, 0, part + n))]
+        + [pl.BlockSpec((rows + TRAILER, tile), index)] * joins
         + [ANY] * skip,
-        out_specs=[pl.BlockSpec((rows + TRAILER, tile), lambda n: (0, n))] + [ANY] * len(through),
-        out_shape=[jax.ShapeDtypeStruct((rows + TRAILER, width), jnp.int16)]
+        out_specs=[pl.BlockSpec((rows + trailer, tile), lambda n: (0, n))] + [ANY] * len(through),
+        out_shape=[jax.ShapeDtypeStruct((rows + trailer, parts * tile), jnp.int16)]
         + [jax.ShapeDtypeStruct(t.shape, t.dtype) for t in through],
-        input_output_aliases={1 + len(got) + k: 1 + k for k in range(len(through))},
+        input_output_aliases={1 + joins + k: 1 + k for k in range(len(through))},
         compiler_params=params(),
-        cost_estimate=light(),
+        cost_estimate=light(weight),
     )(sums, *got, *through, *after)
     return out if through else out[0]
 
@@ -227,7 +228,7 @@
     out_ref[...] = jnp.dot(x_ref[...], w_ref[...], preferred_element_type=jnp.float32)
 
 
-def ladder_pair_kernel(at_ref, *refs, groups, after, prior):
+def ladder_pair_kernel(at_ref, *refs, groups, after, prior, trailer):
     sources, w_ref = refs[: sum(groups)], refs[sum(groups)]
     prior_ref = refs[sum(groups) + 1]
     keep_ref, message_ref, x_ref, sems, part_ref = refs[sum(groups) + 1 + prior + after :]
@@ -241,10 +242,10 @@
         part_ref[0] = product[:rows]
         part_ref[1] = product[rows:]
     keep_ref[0] = part_ref[at_ref[1]]
-    put(message_ref, [part_ref[1 - at_ref[1]]])
-
-
-def ladder_call(groups, w, at, pair, prior=None, after=(), columns=1, heavy=False, tile=512):
+    put(message_ref, [part_ref[1 - at_ref[1]]], trailer)
+
+
+def ladder_call(groups, w, at, pair, prior=None, after=(), columns=1, trailer=TRAILER, tile=512):
     depth = groups[0][0].shape[1]
     total = sum(g[0].shape[0] for g in groups)
     width = w.shape[1] // columns
@@ -258,14 +259,14 @@
         if prior is not None:
             operands.append(prior)
             specs.append(pl.BlockSpec((rows, tile), lambda n, at: (0, at[0] * tiles + n)))
-        kernel = functools.partial(ladder_pair_kernel, groups=counts, after=len(after), prior=int(prior is not None))
+        kernel = functools.partial(ladder_pair_kernel, groups=counts, after=len(after), prior=int(prior is not None), trailer=trailer)
         out_shape = [
             jax.ShapeDtypeStruct((1, rows, width), jnp.float32),
-            jax.ShapeDtypeStruct((rows + TRAILER, width), jnp.int16),
+            jax.ShapeDtypeStruct((rows + trailer, width), jnp.int16),
         ]
         out_specs = [
             pl.BlockSpec((1, rows, tile), lambda n, at: (0, 0, n)),
-            pl.BlockSpec((rows + TRAILER, tile), lambda n, at: (0, n)),
+            pl.BlockSpec((rows + trailer, tile), lambda n, at: (0, n)),
         ]
         scratch.append(pltpu.VMEM((2, rows, tile), jnp.float32))
     else:
@@ -283,7 +284,36 @@
         ),
         out_shape=out_shape,
         compiler_params=params(),
-        cost_estimate=light(2 * total * depth * width if heavy else 1000),
+        cost_estimate=light(),
+    )(at, *operands, *after)
+
+
+def turn_kernel(at_ref, *refs, trailer):
+    for near, (base_ref, got_ref) in enumerate((refs[2:4], refs[0:2])):
+
+        @pl.when(at_ref[0] == near)
+        def _(near=near, base_ref=base_ref, got_ref=got_ref):
+            put(refs[-1], [base_ref[0] + take(got_ref, 1, 0, WIDE if near else TRAILER)], trailer)
+
+
+def turn(at, chunk0, chunk1, part, after=(), weight=4, trailer=TRAILER):
+    _, rows, width = chunk1[0].shape
+    operands, specs = [], []
+    for (keep, got), index in ((chunk0, part), (chunk1, 0)):
+        operands += [keep, got]
+        specs.append(pl.BlockSpec((1, rows, width), lambda n, at, index=index: (0, 0, index)))
+        specs.append(pl.BlockSpec((got.shape[0], width), lambda n, at, index=index: (0, index)))
+    return pl.pallas_call(
+        functools.partial(turn_kernel, trailer=trailer),
+        grid_spec=pltpu.PrefetchScalarGridSpec(
+            num_scalar_prefetch=1,
+            grid=(1,),
+            in_specs=specs + [ANY] * len(after),
+            out_specs=pl.BlockSpec((rows + trailer, width), lambda n, at: (0, n)),
+        ),
+        out_shape=jax.ShapeDtypeStruct((rows + trailer, width), jnp.int16),
+        compiler_params=params(),
+        cost_estimate=light(weight),
     )(at, *operands, *after)
 
 
@@ -306,21 +336,30 @@
         cycle_ref[side] = base[side][0] + sum(scaled(m[side], m[2], side) for m in messages)
 
     block, lanes = out_ref.shape[2:]
-    keep0 = next_refs(2)
-    chunk0 = [next_refs(3) for _ in range(2)]
-    keep1 = next_refs(2)
-    chunk1 = [next_refs(3) for _ in range(2)]
+    keep0, x0 = next_refs(2), next_refs(3)
+    chunk1 = [(next_refs(2), next_refs(3)) for _ in range(2)]
+    came = [next_refs(3) for _ in range(2)]
     rows = keep0[0].shape[1]
 
-    def spread(keep, chunk):
+    def spread(part, side, total):
+        total = total + scaled(came[part][side], came[part][2], 0)
+        for a in range(block // 2):
+            row = ((part * (block // 2) + a) * 2 + side) * rows
+            ladder_ref[row : row + rows, :] = total[:, a * lanes : (a + 1) * lanes]
+
+    @pl.when(near == 1)
+    def _():
         for side in range(2):
-            total = keep[side][0] + sum(scaled(m[side], m[2], 0) for m in chunk)
-            for a in range(block):
-                row = (a * 2 + side) * rows
-                ladder_ref[row : row + rows, :] = total[:, a * lanes : (a + 1) * lanes]
-
-    pl.when(near == 1)(functools.partial(spread, keep0, chunk0))
-    pl.when(near != 1)(functools.partial(spread, keep1, chunk1))
+            total = keep0[side][0] + scaled(x0[side], x0[2], 0)
+            half = total.shape[1] // 2
+            for part in range(2):
+                spread(part, side, total[:, part * half : (part + 1) * half])
+
+    @pl.when(near != 1)
+    def _():
+        for part, (keep, got) in enumerate(chunk1):
+            for side in range(2):
+                spread(part, side, keep[side][0] + scaled(got[side], got[2], 0))
 
     slab, occ = out_ref.shape[:2]
     per = occ // 2
@@ -340,7 +379,7 @@
     lax.fori_loop(0, slab, row, 0)
 
 
-def finish(at, slab_energy, pair_energy, base, sums, cycle, chunk0, chunk1, slab, steps=4):
+def finish(at, slab_energy, pair_energy, base, sums, cycle, chunk0, chunk1, came, slab, steps=4):
     vir, lanes = base.shape
     occ = pair_energy.shape[0]
     mine, wide = sums.shape[1] // 2 // steps, sums.shape[2]
@@ -350,16 +389,16 @@
         operands.append(array)
         specs.append(pl.BlockSpec(shape, index))
 
-    def message(array, near=None):
-        rows = (array.shape[0] - TRAILER) // 2 // steps
+    def message(array, trailer, near=None):
+        rows = (array.shape[0] - trailer) // 2 // steps
         width = array.shape[1]
         for side in range(2):
             if near is None:
                 add(array, (rows, width), lambda n, *_, side=side: (side * steps + n, 0))
             else:
                 add(array, (rows, width), lambda n, at, *_, side=side: (jnp.where(at[0] == near, side * steps + n, 0), 0))
-        last = (array.shape[0] - TRAILER) // TRAILER
-        add(array, (TRAILER, width), lambda n, *_: (last, 0))
+        last = (array.shape[0] - trailer) // trailer
+        add(array, (trailer, width), lambda n, *_: (last, 0))
 
     def kept(array, near):
         rows, width = array.shape[1] // 2 // steps, array.shape[2]
@@ -369,11 +408,14 @@
     for side in range(2):
         add(sums, (1, mine, wide), lambda n, *_, side=side: (SENT, side * steps + n, 0))
     for array in cycle:
-        message(array)
-    for near, (keep, *messages) in ((1, chunk0), (0, chunk1)):
-        kept(keep, near)
-        for array in messages:
-            message(array, near)
+        message(array, array.shape[0] - sums.shape[1])
+    kept(chunk0[0], 1)
+    message(chunk0[1], WIDE, 1)
+    for keep, got in chunk1:
+        kept(keep, 0)
+        message(got, TRAILER, 0)
+    for array in came:
+        message(array, array.shape[0] - chunk0[0].shape[1])
     rows = chunk0[0].shape[1] // 2 // steps
     return pl.pallas_call(
         finish_kernel,
@@ -454,38 +496,47 @@
     g3_s = lax.ppermute(g3, "blk", across)
     g4_s = lax.ppermute(g4, "blk", across)
     near_x = ints(0, jnp.where(x_place == chip % 2, 0, 1), 0, 0)
-    keep0, to_x = ladder_call([[g1], [g1_s]], ladder_ints, near_x, True, prior=p_own)
+    keep0, to_x = ladder_call([[g1], [g1_s]], ladder_ints, near_x, True, prior=p_own, trailer=WIDE)
     x0 = lax.ppermute(to_x, "red", along_x)
 
     blocks = [mine, rx, ry, ry2, rx2]
     places = jnp.array(ORDER, jnp.int32)[chip] ^ red
     at_give, at_keep = jnp.concatenate([ints(1 - core), places]), jnp.concatenate([ints(core), places])
-    give_a = cycle_call(blocks, cycle_ints, at_give, 0, 2, after=(keep0, g2_s))
+    give_a = cycle_call(blocks, cycle_ints, at_give, 0, after=(keep0, g2_s))
     got_a = lax.ppermute(give_a, "blk", across)
-    give_b = cycle_call(blocks, cycle_ints, at_give, 1, 2, after=(give_a, g3, g4))
+    give_b = cycle_call(blocks, cycle_ints, at_give, 1, after=(give_a, g3, g4))
     got_b = lax.ppermute(give_b, "blk", across)
-    sums, s0, s1, s2 = cycle_call(blocks, cycle_ints, at_keep, 0, 1, [got_a, got_b])
+    sums, s0a, s1, s2 = cycle_call(blocks, cycle_ints, at_keep, 0, got_a, after=(give_b,))
+    r0a = lax.ppermute(s0a, "blk", inward)
+    sums, s0b, s1, s2 = cycle_call(blocks, cycle_ints, at_keep, 1, got_b, (sums, s1, s2))
+    r0b = lax.ppermute(s0b, "blk", inward)
     g5 = lax.ppermute(g3, "blk", outward)
+
+    to_mid, s1, s2, g5 = hop(sums, 0, [r0a], 0, through=(s1, s2, g5))
     g5_s = lax.ppermute(g5, "blk", across)
-    r0 = lax.ppermute(s0, "blk", inward)
+    mid_a = lax.ppermute(to_mid, "blk", middle)
     r1 = lax.ppermute(s1, "blk", inward)
-    r2 = lax.ppermute(s2, "blk", inward)
-
     end = jnp.where((chip == 0) | (chip == 3), 1, 0)
     stays = jnp.where(x_place == chip // 2, 0, 1)
     rest = [[g2, g4], [g2_s, g4_s], [g3, g5], [g3_s, g5_s]]
-    keep1, to_x = ladder_call(rest, ladder_ints, ints(0, stays, end, end, end, end), True, after=(sums,))
+    at = ints(0, stays, end, end, end, end)
+    keep1, to_x = ladder_call(rest, ladder_ints, at, True, after=(to_mid, x0), columns=2)
     x1 = lax.ppermute(to_x, "red", along_x)
-    to_mid = hop(sums, 0, r0, 2, after=(keep1,))
-    mid = lax.ppermute(to_mid, "blk", middle)
-    to_y = hop(keep0, 0, x0, after=(to_mid,))
-    y0 = lax.ppermute(to_y, "red", along_y)
-    to_inner = hop(sums, 1, r1, 2, after=(to_y,))
+    to_mid = hop(sums, 0, [r0b], 1, after=(keep1,))
+    mid_b = lax.ppermute(to_mid, "blk", middle)
+    at = ints(1, stays, end, end, end, end)
+    keep2, to_x = ladder_call(rest, ladder_ints, at, True, after=(to_mid,), columns=2)
+    x2 = lax.ppermute(to_x, "red", along_x)
+    to_outer = hop(sums, 2, [mid_a, mid_b], parts=2, after=(keep2,), weight=0, trailer=WIDE)
+    outer = lax.ppermute(to_outer, "blk", outward)
+    near = jnp.where(red // 2 == chip // 2, 1, 0)
+    to_y1 = turn(ints(1 - near), (keep0, x0), (keep1, x1), 0, after=(to_outer,), weight=0, trailer=WIDE)
+    y1 = lax.ppermute(to_y1, "red", along_y)
+    to_inner, s2 = hop(sums, 1, [r1], parts=2, through=(s2,), after=(to_y1,), weight=8)
+    r2 = lax.ppermute(s2, "blk", inward)
     inner = lax.ppermute(to_inner, "blk", middle)
-    to_y1 = hop(keep1, 0, x1, after=(to_inner,))
-    y1 = lax.ppermute(to_y1, "red", along_y)
-    to_outer = hop(sums, 2, mid, 2, after=(to_y1, y0))
-    outer = lax.ppermute(to_outer, "blk", outward)
+    to_y2 = turn(ints(1 - near), (keep0, x0), (keep2, x2), 1, after=(to_inner,), weight=4)
+    y2 = lax.ppermute(to_y2, "red", along_y)
 
     orbital_ids = jnp.arange(occ_energy.shape[0], dtype=jnp.int32)
     chosen = slab_index[:, None] == orbital_ids[None, :]
@@ -493,10 +544,10 @@
     pair_energy = lax.dynamic_slice_in_dim(occ_energy, red * occ_red, occ_red)
     first_virtual = lax.dynamic_slice_in_dim(vir_energy, blk * vir_block, vir_block)
     base = first_virtual[:, None] + vir_energy[None, :]
-    near = jnp.where(red // 2 == chip // 2, 1, 0)
-    chunk1 = (keep1, x1, y1)
     cycle = [r2, inner, outer]
-    return finish(ints(near, core), slab_energy, pair_energy, base, sums, cycle, (keep0, x0, y0), chunk1, slab)
+    at = ints(near, core)
+    chunk1 = [(keep1, x1), (keep2, x2)]
+    return finish(at, slab_energy, pair_energy, base, sums, cycle, (keep0, x0), chunk1, [y1, y2], slab)
 
 
 def plain_shards(amplitudes, ladder_ints, cycle_ints, occ_energy, vir_energy, slab_index):

time: 308 us -> 290 us (0.942)
  waiting for transfers between devices: 95.5 us -> 55.7 us
  Pallas kernels: 154 us -> 171 us
    ppermute x3 -> x6, waiting for transfers between devices: 9.81 us -> 34.9 us  [the longest x1 28.1 us: paired_shards(): y2 = lax.ppermute(to_y2, 'red', along_y)]
    ppermute x1, waiting for transfers between devices: 21.1 us -> 0.01 us  [paired_shards(): y1 = lax.ppermute(to_y1, 'red', along_y)]
    ppermute x1, waiting for transfers between devices: 20.2 us -> 0.01 us  [paired_shards(): r1 = lax.ppermute(s1, 'blk', inward)]
    pallas_call x8 -> x10, Pallas kernels: 88.3 us -> 98.6 us  [the longest x4 77.5 us: cycle_call(): pl.pallas_call(functools.partial(cycle_kernel, keeps=got is not None, ski...]
    ppermute x1, waiting for transfers between devices: 9.33 us -> 0.01 us  [paired_shards(): r2 = lax.ppermute(s2, 'blk', inward)]
    pallas_call x3 -> x4, Pallas kernels: 51.4 us -> 58.6 us  [ladder_call(): pl.pallas_call(kernel, grid_spec=pltpu.PrefetchScalarGridSpec(num_scalar_...]
    ppermute x1, waiting for transfers between devices: 6.66 us -> 0.01 us  [paired_shards(): got_b = lax.ppermute(give_b, 'blk', across)]
    ppermute x3 -> x6, starting transfers between devices: 4.99 us -> 7.85 us  [the longest x1 2.05 us: paired_shards(): mid_a = lax.ppermute(to_mid, 'blk', middle)]
  transfers between devices with their start and end apart: 27 -> 30, of which waited for: 16 -> 9; matrix products, arithmetic and copies ran while one was open for 2% -> 3% of each run, Pallas kernels for 39% -> 55%
where the time goes in v2:
time: 290 us; the launch traced here: 286 us
  Pallas kernels  171 us (59%)
  waiting for transfers between devices  55.7 us (19%)
  starting transfers between devices  35.6 us (12%)
  local copies, waits for them, and re-layouts  19.3 us (7%)
  other arithmetic  4.03 us (1%)
    pallas_call x4, Pallas kernels, cycle_call(): pl.pallas_call(functools.partial(cycle_kernel, keeps=got is not None, ski...  77.5 us
    pallas_call x4, Pallas kernels, ladder_call(): pl.pallas_call(kernel, grid_spec=pltpu.PrefetchScalarGridSpec(num_scalar_...  58.6 us
    ppermute x1, waiting for transfers between devices, paired_shards(): y2 = lax.ppermute(to_y2, 'red', along_y)  28.1 us
    unnamed x50, local copies, waits for them, and re-layouts  16 us
    ppermute x1, waiting for transfers between devices, paired_shards(): rx = lax.ppermute(mine, 'red', along_x)  14 us
    pallas_call x4, Pallas kernels, hop(): pl.pallas_call(functools.partial(hop_kernel, joins=joins, skip=skip, trai...  13.6 us
    pallas_call x1, Pallas kernels, finish(): pl.pallas_call(finish_kernel, grid_spec=pltpu.PrefetchScalarGridSpec(num_...  11.4 us
    pallas_call x2, Pallas kernels, turn(): pl.pallas_call(functools.partial(turn_kernel, trailer=trailer), grid_spec...  7.47 us
  transfers between devices with their start and end apart: 30, of which 9 were waited for; matrix products, arithmetic and copies ran while one was open for 3% of the time, Pallas kernels for 55%

profile of v2, /device:TPU:8, one launch (start us, length us, event | category | flops | bytes accessed | tf_op | source)
XLA Modules:
  0.0 286.4 jit_solution(10261880480285499809)
XLA Ops:
  0.0 3.4 %copy.23 = bf16[24,8,32,128]{3,1,2,0:T(8,128)(2,1)} copy(bf16[24,8,32,128]{3,2,1,0:T(8,128)(2,1)} %bitcast.27) | data formatting | bytes 3145728
  4.4 1.6 collective-permute-start
  5.9 1.5 collective-permute-start.1
  7.9 4.6 %collective-permute-start.3 = (bf16[192,4096]{1,0:T(8,128)(2,1)}, bf16[192,4096]{1,0:T(8,128)(2,1)S(1)}, u32[]{:S(2)}, u32[]{:S(2)}) collective-permute-start(bf16[192,4096]{1,0:T(8,128)(2,1)} %bitcast.19.refs_0_), channel_id=1, source_target_pairs={{8,16},{12,20},{16,8},{20,12},{9,17},{13,21},{17,9},{21,13},{10,18... | collective-permute-start | bytes 4718600 | tf_op jit(solution)/shard_map/ppermute | solution.py:485
  13.1 14.2 %shard_map.73.refs_2_.refs_3_ = f32[384,2048]{1,0:T(8,128)} custom-call(s32[8]{0:T(128)} %broadcast_3_at_ref.2.at_ref, bf16[192,4096]{1,0:T(8,128)(2,1)} %bitcast.19.refs_0_, bf16[192,4096]{1,0:T(8,128)(2,1)} %collective-permute-done.4.refs_1_, bf16[4096,2048]{1,0:T(8,128)(2,1)} %refs_8_.3), custom_call_target="tpu_custom_call" | custom-call | flops 1000 | bytes 1000 | tf_op jit(solution)/shard_map/pallas_call | solution.py:276
  27.3 14.0 %collective-permute-done.rx_ref = bf16[256,3072]{1,0:T(8,128)(2,1)S(1)} collective-permute-done((bf16[256,3072]{1,0:T(8,128)(2,1)S(1)}, bf16[256,3072]{1,0:T(8,128)(2,1)S(1)}, u32[]{:S(2)}, u32[]{:S(2)}) %collective-permute-start) | collective-permute-done | bytes 1572896 | tf_op jit(solution)/shard_map/ppermute | solution.py:480
  43.9 3.0 %collective-permute-done.3.refs_1_ = bf16[192,4096]{1,0:T(8,128)(2,1)S(1)} collective-permute-done((bf16[192,4096]{1,0:T(8,128)(2,1)}, bf16[192,4096]{1,0:T(8,128)(2,1)S(1)}, u32[]{:S(2)}, u32[]{:S(2)}) %collective-permute-start.3) | collective-permute-done | bytes 1572896 | tf_op jit(solution)/shard_map/ppermute | solution.py:485
  48.1 2.6 shard_map.74
  56.6 3.6 %collective-permute-start.9 = (bf16[192,4096]{1,0:T(8,128)(2,1)}, bf16[192,4096]{1,0:T(8,128)(2,1)S(1)}, u32[]{:S(2)}, u32[]{:S(2)}) collective-permute-start(bf16[192,4096]{1,0:T(8,128)(2,1)} %get-tuple-element.31.refs_0_), channel_id=1, source_target_pairs={{8,16},{12,20},{16,8},{20,12},{9,17},{13,21},{17,9},{21,13},{10,18... | collective-permute-start | bytes 4718600 | tf_op jit(solution)/shard_map/ppermute | solution.py:492
  60.3 15.6 %shard_map.75 = (f32[1,384,2048]{2,1,0:T(8,128)}, s16[416,2048]{1,0:T(8,128)(2,1)}) custom-call(s32[4]{0:T(128)} %pad_add_fusion.3.at_ref, bf16[192,4096]{1,0:T(8,128)(2,1)} %get-tuple-element.31.refs_0_, bf16[192,4096]{1,0:T(8,128)(2,1)} %collective-permute-done.7.refs_1_, bf16[4096,2048]{1,0:T(8,128)(2,1)} %refs_8_.3, f32[384,2048]{1,0:T(8,128)} %shard_map.73.refs_2_.refs_3_), custom_call_target="tpu_custom_call" | custom-call | flops 1000 | bytes 1000 | tf_op jit(solution)/shard_map/pallas_call | solution.py:276
  77.5 18.4 %shard_map.76.refs_0_ = s16[1040,1536]{1,0:T(8,128)(2,1)} custom-call(s32[5]{0:T(128)} %get-tuple-element.53.at_ref, bf16[256,3072]{1,0:T(8,128)(2,1)} %bitcast.23, bf16[256,3072]{1,0:T(8,128)(2,1)} %copy-done.2, bf16[256,3072]{1,0:T(8,128)(2,1)} %copy-done.3, bf16[128,3072]{1,0:T(8,128)(2,1)} %copy-done.12, bf16[128,3072]{1,0:T(8,128)(2,1)} %copy-done.13, ...), custom_call_target="tpu_custom_call" | custom-call | flops 21850001408 | bytes 1000 | tf_op jit(solution)/shard_map/pallas_call | solution.py:161
  98.3 18.6 %shard_map.77.refs_1_ = s16[1040,1536]{1,0:T(8,128)(2,1)} custom-call(s32[5]{0:T(128)} %get-tuple-element.53.at_ref, bf16[256,3072]{1,0:T(8,128)(2,1)} %bitcast.24, bf16[256,3072]{1,0:T(8,128)(2,1)} %copy-done.2, bf16[256,3072]{1,0:T(8,128)(2,1)} %copy-done.3, bf16[128,3072]{1,0:T(8,128)(2,1)} %copy-done.12, bf16[128,3072]{1,0:T(8,128)(2,1)} %copy-done.13, ...), custom_call_target="tpu_custom_call" | custom-call | flops 21850001408 | bytes 1000 | tf_op jit(solution)/shard_map/pallas_call | solution.py:161
  118.0 1.6 collective-permute-start.14
  120.2 20.3 %shard_map.78 = (f32[4,256,3072]{2,1,0:T(8,128)}, s16[272,1536]{1,0:T(8,128)(2,1)}, s16[272,3072]{1,0:T(8,128)(2,1)}, s16[272,3072]{1,0:T(8,128)(2,1)}) custom-call(s32[5]{0:T(128)} %get-tuple-element.54.at_ref, bf16[256,3072]{1,0:T(8,128)(2,1)} %bitcast.25, bf16[256,3072]{1,0:T(8,128)(2,1)} %copy-done.2, bf16[256,3072]{1,0:T(8,128)(2,1)} %copy-done.3, ...), custom_call_target="tpu_custom_call" | custom-call | flops 21850001408 | bytes 1000 | tf_op jit(solution)/shard_map/pallas_call | solution.py:161
  142.1 20.3 %shard_map.79 = (f32[4,256,3072]{2,1,0:T(8,128)}, s16[272,1536]{1,0:T(8,128)(2,1)}, s16[272,3072]{1,0:T(8,128)(2,1)}, s16[272,3072]{1,0:T(8,128)(2,1)}) custom-call(s32[5]{0:T(128)} %get-tuple-element.54.at_ref, bf16[256,3072]{1,0:T(8,128)(2,1)} %bitcast.26, ...), custom_call_target="tpu_custom_call", output_to_operand_aliasing={{0}: (9, {}), {2}: (10, {}), {3}: (11, {})} | custom-call | flops 21850001408 | bytes 1000 | tf_op jit(solution)/shard_map/pallas_call | solution.py:161
  163.6 3.0 %shard_map.80 = (s16[272,1536]{1,0:T(8,128)(2,1)}, s16[272,3072]{1,0:T(8,128)(2,1)}, s16[272,3072]{1,0:T(8,128)(2,1)}, bf16[192,4096]{1,0:T(8,128)(2,1)}) custom-call(f32[4,256,3072]{2,1,0:T(8,128)} %get-tuple-element.37.base_ref.refs_0_.refs_1_, ...), custom_call_target="tpu_custom_call", output_to_operand_aliasing={{1}: (2, {}), {2}: (3, {}), {3}: (4, {})} | custom-call | flops 4600001024 | bytes 1000 | tf_op jit(solution)/shard_map/pallas_call | solution.py:195
  170.1 2.1 collective-permute-start.21
  173.4 14.5 %shard_map.81 = (f32[1,384,1024]{2,1,0:T(8,128)}, s16[400,1024]{1,0:T(8,128)(2,1)}) custom-call(s32[6]{0:T(128)} %stack.52.at_ref, bf16[192,4096]{1,0:T(8,128)(2,1)} %get-tuple-element.33.refs_0_, bf16[192,4096]{1,0:T(8,128)(2,1)} %copy-done.8, bf16[192,4096]{1,0:T(8,128)(2,1)} %copy-done.7, bf16[192,4096]{1,0:T(8,128)(2,1)} %copy-done.15, ...), custom_call_target="tpu_custom_call" | custom-call | flops 1000 | bytes 1000 | tf_op jit(solution)/shard_map/pallas_call | solution.py:276
  187.8 3.0 %collective-permute-done.22.refs_0_ = s16[272,1536]{1,0:T(8,128)(2,1)} collective-permute-done((s16[272,1536]{1,0:T(8,128)(2,1)}, s16[272,1536]{1,0:T(8,128)(2,1)}, u32[]{:S(2)}, u32[]{:S(2)}) %collective-permute-start.22) | collective-permute-done | bytes 835616 | tf_op jit(solution)/shard_map/ppermute | solution.py:512
  190.9 3.1 %shard_map.82.refs_9_ = s16[272,1536]{1,0:T(8,128)(2,1)} custom-call(f32[4,256,3072]{2,1,0:T(8,128)} %get-tuple-element.37.base_ref.refs_0_.refs_1_, s16[272,1536]{1,0:T(8,128)(2,1)} %collective-permute-done.22.refs_0_, f32[1,384,1024]{2,1,0:T(8,128)} %get-tuple-element.46.refs_1_.refs_2_.refs_16_.refs_17_), custom_call_target="tpu_custom_call" | custom-call | flops 4600001024 | bytes 1000 | tf_op jit(solution)/shard_map/pallas_call | solution.py:195
  193.9 2.0 collective-permute-start.23
  196.0 1.6 collective-permute-start.20
  198.2 14.4 %shard_map.83 = (f32[1,384,1024]{2,1,0:T(8,128)}, s16[400,1024]{1,0:T(8,128)(2,1)}) custom-call(s32[6]{0:T(128)} %stack.53.at_ref, bf16[192,4096]{1,0:T(8,128)(2,1)} %get-tuple-element.33.refs_0_, bf16[192,4096]{1,0:T(8,128)(2,1)} %copy-done.8, bf16[192,4096]{1,0:T(8,128)(2,1)} %copy-done.7, bf16[192,4096]{1,0:T(8,128)(2,1)} %copy-done.15, ...), custom_call_target="tpu_custom_call" | custom-call | flops 1000 | bytes 1000 | tf_op jit(solution)/shard_map/pallas_call | solution.py:276
  213.2 3.1 %collective-permute-done.23.refs_1_ = s16[272,1536]{1,0:T(8,128)(2,1)S(1)} collective-permute-done((s16[272,1536]{1,0:T(8,128)(2,1)}, s16[272,1536]{1,0:T(8,128)(2,1)S(1)}, u32[]{:S(2)}, u32[]{:S(2)}) %collective-permute-start.23) | collective-permute-done | bytes 835616 | tf_op jit(solution)/shard_map/ppermute | solution.py:526
  217.2 3.8 %shard_map.84.refs_4_ = s16[288,3072]{1,0:T(8,128)(2,1)} custom-call(f32[4,256,3072]{2,1,0:T(8,128)} %get-tuple-element.37.base_ref.refs_0_.refs_1_, s16[272,1536]{1,0:T(8,128)(2,1)} %collective-permute-done.21.refs_0_, s16[272,1536]{1,0:T(8,128)(2,1)} %copy-done.19, f32[1,384,1024]{2,1,0:T(8,128)} %get-tuple-element.49.refs_2_.refs_21_.refs_22_), custom_call_target="tpu_custom_call" | custom-call | flops 1000 | bytes 1000 | tf_op jit(solution)/shard_map/pallas_call | solution.py:195
  220.9 1.6 collective-permute-start.26
  223.5 3.7 %shard_map.85.refs_2_ = s16[416,1024]{1,0:T(8,128)(2,1)} custom-call(s32[1]{0:T(128)} %bitcast.7.at_ref, f32[1,384,2048]{2,1,0:T(8,128)} %get-tuple-element.32.refs_0_.refs_11_.refs_12_, s16[416,2048]{1,0:T(8,128)(2,1)} %copy-done, f32[1,384,1024]{2,1,0:T(8,128)} %get-tuple-element.46.refs_1_.refs_2_.refs_16_.refs_17_, s16[400,1024]{1,0:T(8,128)(2,1)} %copy-done.11, ...), custom_call_target="tpu_custom_call" | custom-call | flops 1000 | bytes 1000 | tf_op jit(solution)/shard_map/pallas_call | solution.py:306
  227.2 3.8 %shard_map.86 = (s16[272,3072]{1,0:T(8,128)(2,1)}, s16[272,3072]{1,0:T(8,128)(2,1)}) custom-call(f32[4,256,3072]{2,1,0:T(8,128)} %get-tuple-element.37.base_ref.refs_0_.refs_1_, s16[272,3072]{1,0:T(8,128)(2,1)} %collective-permute-done.15.refs_0_, s16[272,3072]{1,0:T(8,128)(2,1)} %get-tuple-element.42.refs_1_, ...), custom_call_target="tpu_custom_call", output_to_operand_aliasing={{1}: (2, {})} | custom-call | flops 9200001024 | bytes 1000 | tf_op jit(solution)/shard_map/pallas_call | solution.py:195
  232.3 2.3 collective-permute-start.25
  237.1 3.7 %shard_map.87 = s16[400,1024]{1,0:T(8,128)(2,1)} custom-call(s32[1]{0:T(128)} %bitcast.7.at_ref, f32[1,384,2048]{2,1,0:T(8,128)} %get-tuple-element.32.refs_0_.refs_11_.refs_12_, s16[416,2048]{1,0:T(8,128)(2,1)} %copy-done, f32[1,384,1024]{2,1,0:T(8,128)} %get-tuple-element.49.refs_2_.refs_21_.refs_22_, s16[400,1024]{1,0:T(8,128)(2,1)} %copy-done.14, ...), custom_call_target="tpu_custom_call" | custom-call | flops 4600001024 | bytes 1000 | tf_op jit(solution)/shard_map/pallas_call | solution.py:306
  244.3 28.1 %collective-permute-done.29.refs_29_.refs_30_.refs_31_ = s16[400,1024]{1,0:T(8,128)(2,1)} collective-permute-done((s16[400,1024]{1,0:T(8,128)(2,1)}, s16[400,1024]{1,0:T(8,128)(2,1)}, u32[]{:S(2)}, u32[]{:S(2)}) %collective-permute-start.29) | collective-permute-done | bytes 819232 | tf_op jit(solution)/shard_map/ppermute | solution.py:539
  274.9 11.4 %shard_map.88 = f32[8,48,16,128]{3,2,1,0:T(8,128)} custom-call(s32[2]{0:T(128)} %pad_add_fusion.at_ref, f32[8]{0:T(128)} %select_reduce_fusion.slab_ref, f32[48]{0:T(128)} %dynamic_slice.9.pair_ref, f32[16,128]{1,0:T(8,128)} %broadcast_add_fusion.base_ref, f32[4,256,3072]{2,1,0:T(8,128)} %get-tuple-element.37.base_ref.refs_0_.refs_1_, ...), custom_call_target="tpu_custom_call" | custom-call | flops 1000 | bytes 1000 | tf_op jit(solution)/shard_map/pallas_call | solution.py:420
  (107 shorter events, 37.5 us)
Async XLA Ops:
  3.4 9.1 %collective-permute-start.4 = (bf16[192,4096]{1,0:T(8,128)(2,1)}, bf16[192,4096]{1,0:T(8,128)(2,1)}, u32[]{:S(2)}, u32[]{:S(2)}) collective-permute-start(bf16[192,4096]{1,0:T(8,128)(2,1)} %bitcast.19.refs_0_), channel_id=1, source_target_pairs={{0,4},{4,0},{8,12},{12,8},{16,20},{20,16},{24,28},{28,24},{1,5},{5... | collective-permute-start | bytes 4718600 | tf_op jit(solution)/shard_map/ppermute | solution.py:486
  4.4 22.9 %copy-start.1 = (bf16[32,8,24,128]{3,1,2,0:T(8,128)(2,1)}, bf16[32,8,24,128]{3,1,2,0:T(8,128)(2,1)S(1)}, u32[]{:S(2)}) copy-start(bf16[32,8,24,128]{3,1,2,0:T(8,128)(2,1)S(1)} %copy.24) | copy-start | bytes 4718596
  4.4 36.9 %collective-permute-start = (bf16[256,3072]{1,0:T(8,128)(2,1)S(1)}, bf16[256,3072]{1,0:T(8,128)(2,1)S(1)}, u32[]{:S(2)}, u32[]{:S(2)}) collective-permute-start(bf16[256,3072]{1,0:T(8,128)(2,1)S(1)} %bitcast.21), channel_id=1, source_target_pairs={{0,1},{1,0},{2,3},{3,2},{4,5},{5,4},{6,7},{7,6},{8,9},{9,8},{10,11... | collective-permute-start | bytes 4718600 | tf_op jit(solution)/shard_map/ppermute | solution.py:480
  5.9 36.5 %collective-permute-start.1 = (bf16[256,3072]{1,0:T(8,128)(2,1)S(1)}, bf16[256,3072]{1,0:T(8,128)(2,1)S(1)}, u32[]{:S(2)}, u32[]{:S(2)}) collective-permute-start(bf16[256,3072]{1,0:T(8,128)(2,1)S(1)} %bitcast.22), channel_id=1, source_target_pairs={{0,2},{1,3},{2,0},{3,1},{4,6},{5,7},{6,4},{7,5},{8,10},{9,11},{10,... | collective-permute-start | bytes 4718600 | tf_op jit(solution)/shard_map/ppermute | solution.py:481
  7.4 36.5 %collective-permute-start.2 = (bf16[192,4096]{1,0:T(8,128)(2,1)}, bf16[192,4096]{1,0:T(8,128)(2,1)S(1)}, u32[]{:S(2)}, u32[]{:S(2)}) collective-permute-start(bf16[192,4096]{1,0:T(8,128)(2,1)} %bitcast.19.refs_0_), channel_id=1, source_target_pairs={{0,8},{4,12},{8,0},{12,4},{16,24},{20,28},{24,16},{28,20},{1,9},{5... | collective-permute-start | bytes 4718600 | tf_op jit(solution)/shard_map/ppermute | solution.py:484
  7.9 39.0 %collective-permute-start.3 = (bf16[192,4096]{1,0:T(8,128)(2,1)}, bf16[192,4096]{1,0:T(8,128)(2,1)S(1)}, u32[]{:S(2)}, u32[]{:S(2)}) collective-permute-start(bf16[192,4096]{1,0:T(8,128)(2,1)} %bitcast.19.refs_0_), channel_id=1, source_target_pairs={{8,16},{12,20},{16,8},{20,12},{9,17},{13,21},{17,9},{21,13},{10,18... | collective-permute-start | bytes 4718600 | tf_op jit(solution)/shard_map/ppermute | solution.py:485
  50.7 6.0 %collective-permute-start.7 = (bf16[192,4096]{1,0:T(8,128)(2,1)}, bf16[192,4096]{1,0:T(8,128)(2,1)}, u32[]{:S(2)}, u32[]{:S(2)}) collective-permute-start(bf16[192,4096]{1,0:T(8,128)(2,1)} %get-tuple-element.31.refs_0_), channel_id=1, source_target_pairs={{0,4},{4,0},{8,12},{12,8},{16,20},{20,16},{24,28},{28,24},{1,5},{5... | collective-permute-start | bytes 4718600 | tf_op jit(solution)/shard_map/ppermute | solution.py:494
  50.7 25.2 %collective-permute-start.8 = (bf16[192,4096]{1,0:T(8,128)(2,1)}, bf16[192,4096]{1,0:T(8,128)(2,1)S(1)}, u32[]{:S(2)}, u32[]{:S(2)}) collective-permute-start(bf16[192,4096]{1,0:T(8,128)(2,1)} %get-tuple-element.33.refs_0_), channel_id=1, source_target_pairs={{0,4},{4,0},{8,12},{12,8},{16,20},{20,16},{24,28},{28,24},{1,5},{5... | collective-permute-start | bytes 4718600 | tf_op jit(solution)/shard_map/ppermute | solution.py:495
  51.2 24.7 %collective-permute-start.5 = (bf16[128,3072]{1,0:T(8,128)(2,1)}, bf16[128,3072]{1,0:T(8,128)(2,1)S(1)}, u32[]{:S(2)}, u32[]{:S(2)}) collective-permute-start(bf16[128,3072]{1,0:T(8,128)(2,1)} %get-tuple-element.29), channel_id=1, source_target_pairs={{0,2},{1,3},{2,0},{3,1},{4,6},{5,7},{6,4},{7,5},{8,10},{9,11},{10,... | collective-permute-start | bytes 2359304 | tf_op jit(solution)/shard_map/ppermute | solution.py:491
  51.7 24.2 %collective-permute-start.6 = (bf16[128,3072]{1,0:T(8,128)(2,1)}, bf16[128,3072]{1,0:T(8,128)(2,1)S(1)}, u32[]{:S(2)}, u32[]{:S(2)}) collective-permute-start(bf16[128,3072]{1,0:T(8,128)(2,1)} %get-tuple-element.30), channel_id=1, source_target_pairs={{0,1},{1,0},{2,3},{3,2},{4,5},{5,4},{6,7},{7,6},{8,9},{9,8},{10,11... | collective-permute-start | bytes 2359304 | tf_op jit(solution)/shard_map/ppermute | solution.py:490
  54.2 41.8 %collective-permute-start.10 = (bf16[192,4096]{1,0:T(8,128)(2,1)}, bf16[192,4096]{1,0:T(8,128)(2,1)S(1)}, u32[]{:S(2)}, u32[]{:S(2)}) collective-permute-start(bf16[192,4096]{1,0:T(8,128)(2,1)} %get-tuple-element.33.refs_0_), channel_id=1, source_target_pairs={{8,0},{12,4},{16,24},{20,28},{9,1},{13,5},{17,25},{21,29},{10,2},{... | collective-permute-start | bytes 4718600 | tf_op jit(solution)/shard_map/ppermute | solution.py:493
  56.6 39.4 %collective-permute-start.9 = (bf16[192,4096]{1,0:T(8,128)(2,1)}, bf16[192,4096]{1,0:T(8,128)(2,1)S(1)}, u32[]{:S(2)}, u32[]{:S(2)}) collective-permute-start(bf16[192,4096]{1,0:T(8,128)(2,1)} %get-tuple-element.31.refs_0_), channel_id=1, source_target_pairs={{8,16},{12,20},{16,8},{20,12},{9,17},{13,21},{17,9},{21,13},{10,18... | collective-permute-start | bytes 4718600 | tf_op jit(solution)/shard_map/ppermute | solution.py:492
  95.9 23.8 %collective-permute-start.12 = (s16[1040,1536]{1,0:T(8,128)(2,1)}, s16[1040,1536]{1,0:T(8,128)(2,1)}, u32[]{:S(2)}, u32[]{:S(2)}) collective-permute-start(s16[1040,1536]{1,0:T(8,128)(2,1)} %shard_map.76.refs_0_), channel_id=1, source_target_pairs={{0,4},{4,0},{8,12},{12,8},{16,20},{20,16},{24,28},{28,24},{1,5},{5... | collective-permute-start | bytes 9584648 | tf_op jit(solution)/shard_map/ppermute | solution.py:506
  116.9 23.6 %collective-permute-start.11 = (s16[1040,1536]{1,0:T(8,128)(2,1)}, s16[1040,1536]{1,0:T(8,128)(2,1)S(1)}, u32[]{:S(2)}, u32[]{:S(2)}) collective-permute-start(s16[1040,1536]{1,0:T(8,128)(2,1)} %shard_map.77.refs_1_), channel_id=1, source_target_pairs={{0,4},{4,0},{8,12},{12,8},{16,20},{20,16},{24,28},{28,24},{1,5},{5... | collective-permute-start | bytes 9584648 | tf_op jit(solution)/shard_map/ppermute | solution.py:508
  117.3 54.8 %collective-permute-start.16 = (s16[416,2048]{1,0:T(8,128)(2,1)}, s16[416,2048]{1,0:T(8,128)(2,1)S(1)}, u32[]{:S(2)}, u32[]{:S(2)}) collective-permute-start(s16[416,2048]{1,0:T(8,128)(2,1)} %get-tuple-element.43), channel_id=1, source_target_pairs={{0,1},{1,0},{2,3},{3,2},{4,5},{5,4},{6,7},{7,6},{8,9},{9,8},{10,11... | collective-permute-start | bytes 5111816 | tf_op jit(solution)/shard_map/ppermute | solution.py:500
  118.0 44.4 %collective-permute-start.14 = (bf16[192,4096]{1,0:T(8,128)(2,1)}, bf16[192,4096]{1,0:T(8,128)(2,1)S(1)}, u32[]{:S(2)}, u32[]{:S(2)}) collective-permute-start(bf16[192,4096]{1,0:T(8,128)(2,1)} %copy-done.9), channel_id=1, source_target_pairs={{8,0},{12,4},{16,24},{20,28},{9,1},{13,5},{17,25},{21,29},{10,2},{... | collective-permute-start | bytes 4718600 | tf_op jit(solution)/shard_map/ppermute | solution.py:513
  119.6 48.5 %collective-permute-start.17 = (bf16[192,4096]{1,0:T(8,128)(2,1)}, bf16[192,4096]{1,0:T(8,128)(2,1)S(1)}, u32[]{:S(2)}, u32[]{:S(2)}) collective-permute-start(bf16[192,4096]{1,0:T(8,128)(2,1)} %copy-done.8), channel_id=1, source_target_pairs={{0,4},{4,0},{8,12},{12,8},{16,20},{20,16},{24,28},{28,24},{1,5},{5... | collective-permute-start | bytes 4718600 | tf_op jit(solution)/shard_map/ppermute | solution.py:497
  119.7 50.4 %collective-permute-start.18 = (bf16[192,4096]{1,0:T(8,128)(2,1)}, bf16[192,4096]{1,0:T(8,128)(2,1)}, u32[]{:S(2)}, u32[]{:S(2)}) collective-permute-start(bf16[192,4096]{1,0:T(8,128)(2,1)} %copy-done.9), channel_id=1, source_target_pairs={{0,4},{4,0},{8,12},{12,8},{16,20},{20,16},{24,28},{28,24},{1,5},{5... | collective-permute-start | bytes 4718600 | tf_op jit(solution)/shard_map/ppermute | solution.py:496
  140.5 22.7 %collective-permute-start.13 = (s16[272,1536]{1,0:T(8,128)(2,1)}, s16[272,1536]{1,0:T(8,128)(2,1)}, u32[]{:S(2)}, u32[]{:S(2)}) collective-permute-start(s16[272,1536]{1,0:T(8,128)(2,1)} %get-tuple-element.38), channel_id=1, source_target_pairs={{0,8},{4,12},{24,16},{28,20},{1,9},{5,13},{25,17},{29,21},{2,10},{... | collective-permute-start | bytes 2506760 | tf_op jit(solution)/shard_map/ppermute | solution.py:510
  166.6 5.6 %collective-permute-start.19 = (bf16[192,4096]{1,0:T(8,128)(2,1)}, bf16[192,4096]{1,0:T(8,128)(2,1)}, u32[]{:S(2)}, u32[]{:S(2)}) collective-permute-start(bf16[192,4096]{1,0:T(8,128)(2,1)} %get-tuple-element.44.refs_5_), channel_id=1, source_target_pairs={{0,4},{4,0},{8,12},{12,8},{16,20},{20,16},{24,28},{28,24},{1,5},{5... | collective-permute-start | bytes 4718600 | tf_op jit(solution)/shard_map/ppermute | solution.py:516
  166.8 24.1 %collective-permute-start.22 = (s16[272,1536]{1,0:T(8,128)(2,1)}, s16[272,1536]{1,0:T(8,128)(2,1)}, u32[]{:S(2)}, u32[]{:S(2)}) collective-permute-start(s16[272,1536]{1,0:T(8,128)(2,1)} %get-tuple-element.48), channel_id=1, source_target_pairs={{0,8},{4,12},{24,16},{28,20},{1,9},{5,13},{25,17},{29,21},{2,10},{... | collective-permute-start | bytes 2506760 | tf_op jit(solution)/shard_map/ppermute | solution.py:512
  168.1 59.1 %collective-permute-start.15 = (s16[272,3072]{1,0:T(8,128)(2,1)}, s16[272,3072]{1,0:T(8,128)(2,1)}, u32[]{:S(2)}, u32[]{:S(2)}) collective-permute-start(s16[272,3072]{1,0:T(8,128)(2,1)} %get-tuple-element.41), channel_id=1, source_target_pairs={{0,8},{4,12},{24,16},{28,20},{1,9},{5,13},{25,17},{29,21},{2,10},{... | collective-permute-start | bytes 5013512 | tf_op jit(solution)/shard_map/ppermute | solution.py:518
  170.1 43.1 %collective-permute-start.21 = (s16[272,1536]{1,0:T(8,128)(2,1)}, s16[272,1536]{1,0:T(8,128)(2,1)}, u32[]{:S(2)}, u32[]{:S(2)}) collective-permute-start(s16[272,1536]{1,0:T(8,128)(2,1)} %get-tuple-element.45.refs_9_), channel_id=1, source_target_pairs={{8,16},{12,20},{16,8},{20,12},{9,17},{13,21},{17,9},{21,13},{10,18... | collective-permute-start | bytes 2506760 | tf_op jit(solution)/shard_map/ppermute | solution.py:517
  193.9 22.3 %collective-permute-start.23 = (s16[272,1536]{1,0:T(8,128)(2,1)}, s16[272,1536]{1,0:T(8,128)(2,1)S(1)}, u32[]{:S(2)}, u32[]{:S(2)}) collective-permute-start(s16[272,1536]{1,0:T(8,128)(2,1)} %shard_map.82.refs_9_), channel_id=1, source_target_pairs={{8,16},{12,20},{16,8},{20,12},{9,17},{13,21},{17,9},{21,13},{10,18... | collective-permute-start | bytes 2506760 | tf_op jit(solution)/shard_map/ppermute | solution.py:526
  196.0 26.6 %collective-permute-start.20 = (s16[400,1024]{1,0:T(8,128)(2,1)S(1)}, s16[400,1024]{1,0:T(8,128)(2,1)S(1)}, u32[]{:S(2)}, u32[]{:S(2)}) collective-permute-start(s16[400,1024]{1,0:T(8,128)(2,1)S(1)} %copy-done.23), channel_id=1, source_target_pairs={{0,1},{1,0},{2,3},{3,2},{4,5},{5,4},{6,7},{7,6},{8,9},{9,8},{10,11... | collective-permute-start | bytes 2457608 | tf_op jit(solution)/shard_map/ppermute | solution.py:524
  212.6 23.6 %collective-permute-start.27 = (s16[400,1024]{1,0:T(8,128)(2,1)}, s16[400,1024]{1,0:T(8,128)(2,1)S(1)}, u32[]{:S(2)}, u32[]{:S(2)}) collective-permute-start(s16[400,1024]{1,0:T(8,128)(2,1)} %get-tuple-element.52), channel_id=1, source_target_pairs={{0,1},{1,0},{2,3},{3,2},{4,5},{5,4},{6,7},{7,6},{8,9},{9,8},{10,11... | collective-permute-start | bytes 2457608 | tf_op jit(solution)/shard_map/ppermute | solution.py:529
  220.9 51.4 %collective-permute-start.26 = (s16[288,3072]{1,0:T(8,128)(2,1)}, s16[288,3072]{1,0:T(8,128)(2,1)S(1)}, u32[]{:S(2)}, u32[]{:S(2)}) collective-permute-start(s16[288,3072]{1,0:T(8,128)(2,1)} %shard_map.84.refs_4_), channel_id=1, source_target_pairs={{8,0},{12,4},{16,24},{20,28},{9,1},{13,5},{17,25},{21,29},{10,2},{... | collective-permute-start | bytes 5308424 | tf_op jit(solution)/shard_map/ppermute | solution.py:531
  231.0 41.4 %collective-permute-start.24 = (s16[272,3072]{1,0:T(8,128)(2,1)}, s16[272,3072]{1,0:T(8,128)(2,1)S(1)}, u32[]{:S(2)}, u32[]{:S(2)}) collective-permute-start(s16[272,3072]{1,0:T(8,128)(2,1)} %get-tuple-element.50), channel_id=1, source_target_pairs={{0,8},{4,12},{24,16},{28,20},{1,9},{5,13},{25,17},{29,21},{2,10},{... | collective-permute-start | bytes 5013512 | tf_op jit(solution)/shard_map/ppermute | solution.py:536
  232.3 10.5 %copy-start.22 = (s32[8]{0:T(128)S(1)}, s32[8]{0:T(128)}, u32[]{:S(2)}) copy-start(s32[8]{0:T(128)} %param.12) | copy-start | bytes 100
  232.3 40.1 %collective-permute-start.25 = (s16[272,3072]{1,0:T(8,128)(2,1)}, s16[272,3072]{1,0:T(8,128)(2,1)}, u32[]{:S(2)}, u32[]{:S(2)}) collective-permute-start(s16[272,3072]{1,0:T(8,128)(2,1)} %get-tuple-element.51.refs_4_), channel_id=1, source_target_pairs={{8,16},{12,20},{16,8},{20,12},{9,17},{13,21},{17,9},{21,13},{10,18... | collective-permute-start | bytes 5013512 | tf_op jit(solution)/shard_map/ppermute | solution.py:537
  234.7 37.7 %collective-permute-start.28 = (s16[416,1024]{1,0:T(8,128)(2,1)}, s16[416,1024]{1,0:T(8,128)(2,1)}, u32[]{:S(2)}, u32[]{:S(2)}) collective-permute-start(s16[416,1024]{1,0:T(8,128)(2,1)} %shard_map.85.refs_2_), channel_id=1, source_target_pairs={{0,2},{1,3},{2,0},{3,1},{4,6},{5,7},{6,4},{7,5},{8,10},{9,11},{10,... | collective-permute-start | bytes 2555912 | tf_op jit(solution)/shard_map/ppermute | solution.py:534
  240.9 31.5 %collective-permute-start.29 = (s16[400,1024]{1,0:T(8,128)(2,1)}, s16[400,1024]{1,0:T(8,128)(2,1)}, u32[]{:S(2)}, u32[]{:S(2)}) collective-permute-start(s16[400,1024]{1,0:T(8,128)(2,1)} %shard_map.87), channel_id=1, source_target_pairs={{0,2},{1,3},{2,0},{3,1},{4,6},{5,7},{6,4},{7,5},{8,10},{9,11},{10,... | collective-permute-start | bytes 2457608 | tf_op jit(solution)/shard_map/ppermute | solution.py:539
  (22 other events, 61.3 us)

commit v3 on v2

--- a/solution.py
+++ b/solution.py
@@ -67,8 +67,16 @@
 
 
 def forward_kernel(rx_ref, ry_ref, *refs, skip):
-    on_y_ref, on_x_ref = refs[skip : skip + 2]
-    on_y_ref[...], on_x_ref[...] = rx_ref[...], ry_ref[...]
+    on_y_ref, on_x_ref, sems = refs[skip], refs[skip + 1], refs[-1]
+    rows = on_y_ref.shape[0]
+    copies = [
+        pltpu.make_async_copy(rx_ref.at[pl.ds(0, rows), :], on_y_ref, sems.at[0]),
+        pltpu.make_async_copy(ry_ref.at[pl.ds(rows, rows), :], on_x_ref, sems.at[1]),
+    ]
+    for copy in copies:
+        copy.start()
+    for copy in copies:
+        copy.wait()
 
 
 def forward(rx, ry, through=(), after=()):
@@ -77,9 +85,9 @@
     return pl.pallas_call(
         functools.partial(forward_kernel, skip=len(through) + len(after)),
         grid=(1,),
-        in_specs=[pl.BlockSpec((rows, width), lambda n: (0, 0)), pl.BlockSpec((rows, width), lambda n: (1, 0))]
-        + [ANY] * (len(through) + len(after)),
+        in_specs=[ANY] * (2 + len(through) + len(after)),
         out_specs=[pl.BlockSpec((rows, width), lambda n: (0, 0))] * 2 + [ANY] * len(through),
+        scratch_shapes=[pltpu.SemaphoreType.DMA((2,))],
         out_shape=[block, block] + [jax.ShapeDtypeStruct(t.shape, t.dtype) for t in through],
         input_output_aliases={2 + k: 2 + k for k in range(len(through))},
         compiler_params=params(),
@@ -123,10 +131,10 @@
         for side, total in enumerate(totals):
             sums_ref[n, rows * side : rows * (side + 1), :] = total
         if n < SENT:
-            put((s0_ref, s1_ref, s2_ref)[n], totals)
-
-
-def cycle_call(sources, w, at, part, got=None, before=(), after=(), tile=512):
+            put((s0_ref, s1_ref, s2_ref)[n], totals, WIDE if n == SENT - 1 else TRAILER)
+
+
+def cycle_call(sources, w, at, part, got=None, before=(), after=(), tile=256):
     own, depth = sources[0].shape
     rows, width = own // 2, w.shape[1] // 2
     tiles = width // tile // PARTS
@@ -146,17 +154,18 @@
         specs.append(given)
         if before:
             aliases = {1 + len(operands): 0, 2 + len(operands): 2, 3 + len(operands): 3}
-        message = jax.ShapeDtypeStruct((own + TRAILER, width), jnp.int16)
         out_shape = [
             jax.ShapeDtypeStruct((BLOCKS, own, width), jnp.float32),
             jax.ShapeDtypeStruct((own + TRAILER, width // PARTS), jnp.int16),
-            message,
-            message,
+            jax.ShapeDtypeStruct((own + TRAILER, width), jnp.int16),
+            jax.ShapeDtypeStruct((own + WIDE, width), jnp.int16),
         ]
         out_specs = [
             pl.BlockSpec((BLOCKS, own, tile), lambda n, at: (0, 0, first + n)),
             pl.BlockSpec((own + TRAILER, tile), lambda n, at: (0, n)),
-        ] + [pl.BlockSpec((own + TRAILER, tile), lambda n, at: (0, first + n))] * 2
+            pl.BlockSpec((own + TRAILER, tile), lambda n, at: (0, first + n)),
+            pl.BlockSpec((own + WIDE, tile), lambda n, at: (0, first + n)),
+        ]
     skip = len(before) + len(after)
     return pl.pallas_call(
         functools.partial(cycle_kernel, keeps=got is not None, skip=skip),
@@ -172,6 +181,22 @@
         compiler_params=params(),
         cost_estimate=light(19),
     )(at, *operands, *before, *after)
+
+
+def gate_kernel(*refs):
+    refs[-1][...] = jnp.zeros_like(refs[-1])
+
+
+def gate(*through, after=()):
+    out = pl.pallas_call(
+        gate_kernel,
+        in_specs=[ANY] * (len(through) + len(after)),
+        out_specs=[ANY] * len(through) + [pl.BlockSpec(memory_space=pltpu.VMEM)],
+        out_shape=[jax.ShapeDtypeStruct(t.shape, t.dtype) for t in through] + [jax.ShapeDtypeStruct((8, 128), jnp.float32)],
+        input_output_aliases={k: k for k in range(len(through))},
+        cost_estimate=light(),
+    )(*through, *after)
+    return out[:-1]
 
 
 def hop_kernel(base_ref, *refs, joins, skip, trailer):
@@ -317,7 +342,38 @@
     )(at, *operands, *after)
 
 
-def finish_kernel(at_ref, slab_ref, pair_ref, base_ref, *refs):
+def scaled(message, side, group):
+    trailer = message[2][group : group + 1, :].astype(jnp.int32).astype(jnp.float32)
+    scale = jnp.exp2(trailer * (1.0 / STEPS)) * (1.0 / TOP)
+    return message[side][...].astype(jnp.int32).astype(jnp.float32) * scale
+
+
+class Blocks:
+    def __init__(self, steps):
+        self.steps, self.operands, self.specs = steps, [], []
+
+    def add(self, array, shape, index):
+        self.operands.append(array)
+        self.specs.append(pl.BlockSpec(shape, index))
+
+    def place(self, at, side, n, near):
+        place = side * self.steps + n
+        return place if near is None else jnp.where(at[0] == near, place, 0)
+
+    def message(self, array, trailer, near=None):
+        rows, width = (array.shape[0] - trailer) // 2 // self.steps, array.shape[1]
+        for side in range(2):
+            self.add(array, (rows, width), lambda n, at, *_, side=side: (self.place(at, side, n, near), 0))
+        last = (array.shape[0] - trailer) // trailer
+        self.add(array, (trailer, width), lambda n, *_: (last, 0))
+
+    def sides(self, array, first, near=None):
+        rows, width = array.shape[1] // 2 // self.steps, array.shape[2]
+        for side in range(2):
+            self.add(array, (1, rows, width), lambda n, at, *_, side=side: (first, self.place(at, side, n, near), 0))
+
+
+def settle_kernel(at_ref, *refs):
     *refs, out_ref, cycle_ref, ladder_ref = refs
     near, core = at_ref[0], at_ref[1]
     refs = list(refs)
@@ -325,24 +381,18 @@
     def next_refs(count):
         return [refs.pop(0) for _ in range(count)]
 
-    def scaled(data_ref, trailer_ref, group):
-        trailer = trailer_ref[group : group + 1, :].astype(jnp.int32).astype(jnp.float32)
-        scale = jnp.exp2(trailer * (1.0 / STEPS)) * (1.0 / TOP)
-        return data_ref[...].astype(jnp.int32).astype(jnp.float32) * scale
-
-    base = next_refs(2)
-    messages = [next_refs(3) for _ in range(3)]
+    base, chain = next_refs(2), next_refs(3)
     for side in range(2):
-        cycle_ref[side] = base[side][0] + sum(scaled(m[side], m[2], side) for m in messages)
-
-    block, lanes = out_ref.shape[2:]
+        cycle_ref[side] = base[side][0] + scaled(chain, side, side)
+
+    slab, occ, block, lanes = out_ref.shape
     keep0, x0 = next_refs(2), next_refs(3)
     chunk1 = [(next_refs(2), next_refs(3)) for _ in range(2)]
     came = [next_refs(3) for _ in range(2)]
     rows = keep0[0].shape[1]
 
     def spread(part, side, total):
-        total = total + scaled(came[part][side], came[part][2], 0)
+        total = total + scaled(came[part], side, 0)
         for a in range(block // 2):
             row = ((part * (block // 2) + a) * 2 + side) * rows
             ladder_ref[row : row + rows, :] = total[:, a * lanes : (a + 1) * lanes]
@@ -350,7 +400,7 @@
     @pl.when(near == 1)
     def _():
         for side in range(2):
-            total = keep0[side][0] + scaled(x0[side], x0[2], 0)
+            total = keep0[side][0] + scaled(x0, side, 0)
             half = total.shape[1] // 2
             for part in range(2):
                 spread(part, side, total[:, part * half : (part + 1) * half])
@@ -359,80 +409,96 @@
     def _():
         for part, (keep, got) in enumerate(chunk1):
             for side in range(2):
-                spread(part, side, keep[side][0] + scaled(got[side], got[2], 0))
-
-    slab, occ = out_ref.shape[:2]
+                spread(part, side, keep[side][0] + scaled(got, side, 0))
+
     per = occ // 2
-    step = pl.program_id(0)
 
     def row(i, carry):
-        energy = base_ref[...] - slab_ref[step * slab + i]
         for side in range(2):
             first = jnp.where(core == side, 0, rows)
             for j in range(per):
                 ladder = ladder_ref[pl.ds(first + i * per + j, block, stride=2 * rows), :]
                 place = pl.ds(pl.multiple_of(i * block, block), block)
-                cycle = cycle_ref[side, place, j * lanes : (j + 1) * lanes]
-                out_ref[i, side * per + j] = (ladder + cycle) / (energy - pair_ref[side * per + j])
+                out_ref[i, side * per + j] = ladder + cycle_ref[side, place, j * lanes : (j + 1) * lanes]
         return carry
 
     lax.fori_loop(0, slab, row, 0)
 
 
-def finish(at, slab_energy, pair_energy, base, sums, cycle, chunk0, chunk1, came, slab, steps=4):
-    vir, lanes = base.shape
-    occ = pair_energy.shape[0]
+def settle(at, shape, sums, outer, chunk0, chunk1, came, steps=4):
+    slab, occ, vir, lanes = shape
     mine, wide = sums.shape[1] // 2 // steps, sums.shape[2]
-    operands, specs = [], []
-
-    def add(array, shape, index):
-        operands.append(array)
-        specs.append(pl.BlockSpec(shape, index))
-
-    def message(array, trailer, near=None):
-        rows = (array.shape[0] - trailer) // 2 // steps
-        width = array.shape[1]
-        for side in range(2):
-            if near is None:
-                add(array, (rows, width), lambda n, *_, side=side: (side * steps + n, 0))
-            else:
-                add(array, (rows, width), lambda n, at, *_, side=side: (jnp.where(at[0] == near, side * steps + n, 0), 0))
-        last = (array.shape[0] - trailer) // trailer
-        add(array, (trailer, width), lambda n, *_: (last, 0))
-
-    def kept(array, near):
-        rows, width = array.shape[1] // 2 // steps, array.shape[2]
-        for side in range(2):
-            add(array, (1, rows, width), lambda n, at, *_, side=side: (0, jnp.where(at[0] == near, side * steps + n, 0), 0))
-
-    for side in range(2):
-        add(sums, (1, mine, wide), lambda n, *_, side=side: (SENT, side * steps + n, 0))
-    for array in cycle:
-        message(array, array.shape[0] - sums.shape[1])
-    kept(chunk0[0], 1)
-    message(chunk0[1], WIDE, 1)
+    blocks = Blocks(steps)
+    blocks.sides(sums, SENT)
+    blocks.message(outer, WIDE)
+    blocks.sides(chunk0[0], 0, 1)
+    blocks.message(chunk0[1], WIDE, 1)
     for keep, got in chunk1:
-        kept(keep, 0)
-        message(got, TRAILER, 0)
+        blocks.sides(keep, 0, 0)
+        blocks.message(got, TRAILER, 0)
     for array in came:
-        message(array, array.shape[0] - chunk0[0].shape[1])
+        blocks.message(array, array.shape[0] - chunk0[0].shape[1])
     rows = chunk0[0].shape[1] // 2 // steps
     return pl.pallas_call(
-        finish_kernel,
+        settle_kernel,
         grid_spec=pltpu.PrefetchScalarGridSpec(
-            num_scalar_prefetch=3,
+            num_scalar_prefetch=1,
             grid=(steps,),
-            in_specs=[pl.BlockSpec((vir, lanes), lambda n, *_: (0, 0))] + specs,
+            in_specs=blocks.specs,
             out_specs=pl.BlockSpec((slab // steps, occ, vir, lanes), lambda n, *_: (n, 0, 0, 0)),
             scratch_shapes=[
                 pltpu.VMEM((2, mine, wide), jnp.float32),
                 pltpu.VMEM((2 * vir * rows, lanes), jnp.float32),
             ],
         ),
-        out_shape=jax.ShapeDtypeStruct((slab, occ, vir, lanes), jnp.float32),
+        out_shape=jax.ShapeDtypeStruct(shape, jnp.float32),
+        compiler_params=params(),
+        cost_estimate=light(7),
+    )(at, *blocks.operands)
+
+
+def finish_kernel(at_ref, slab_ref, pair_ref, base_ref, settled_ref, *refs):
+    first, second = refs[0:3], refs[3:6]
+    out_ref, cycle_ref = refs[6:]
+    for side in range(2):
+        cycle_ref[side] = scaled(first, side, side) + scaled(second, side, side)
+    slab, occ, block, lanes = out_ref.shape
+    per = occ // 2
+    step = pl.program_id(0)
+
+    def row(i, carry):
+        energy = base_ref[...] - slab_ref[step * slab + i]
+        place = pl.ds(pl.multiple_of(i * block, block), block)
+        for side in range(2):
+            for j in range(per):
+                total = settled_ref[i, side * per + j] + cycle_ref[side, place, j * lanes : (j + 1) * lanes]
+                out_ref[i, side * per + j] = total / (energy - pair_ref[side * per + j])
+        return carry
+
+    lax.fori_loop(0, slab, row, 0)
+
+
+def finish(at, slab_energy, pair_energy, base, settled, cycle, steps=2):
+    slab, occ, vir, lanes = settled.shape
+    blocks = Blocks(steps)
+    blocks.add(base, base.shape, lambda n, *_: (0, 0))
+    blocks.add(settled, (slab // steps, occ, vir, lanes), lambda n, *_: (n, 0, 0, 0))
+    for array, trailer in zip(cycle, (WIDE, TRAILER)):
+        blocks.message(array, trailer)
+    wide = cycle[0].shape[1]
+    return pl.pallas_call(
+        finish_kernel,
+        grid_spec=pltpu.PrefetchScalarGridSpec(
+            num_scalar_prefetch=3,
+            grid=(steps,),
+            in_specs=blocks.specs,
+            out_specs=pl.BlockSpec((slab // steps, occ, vir, lanes), lambda n, *_: (n, 0, 0, 0)),
+            scratch_shapes=[pltpu.VMEM((2, slab * vir // steps, wide), jnp.float32)],
+        ),
+        out_shape=jax.ShapeDtypeStruct(settled.shape, jnp.float32),
         compiler_params=params(),
         cost_estimate=light(),
-    )(at, slab_energy, pair_energy, base, *operands)
+    )(at, slab_energy, pair_energy, *blocks.operands)
 
 
 def denominators(occ_energy, vir_energy, slab_index, occ_red, vir_block):
@@ -512,7 +578,8 @@
     r0b = lax.ppermute(s0b, "blk", inward)
     g5 = lax.ppermute(g3, "blk", outward)
 
-    to_mid, s1, s2, g5 = hop(sums, 0, [r0a], 0, through=(s1, s2, g5))
+    s1, s2, g5 = gate(s1, s2, g5, after=(sums, r0a))
+    to_mid = hop(sums, 0, [r0a], 0, after=(s1,))
     g5_s = lax.ppermute(g5, "blk", across)
     mid_a = lax.ppermute(to_mid, "blk", middle)
     r1 = lax.ppermute(s1, "blk", inward)
@@ -527,15 +594,15 @@
     at = ints(1, stays, end, end, end, end)
     keep2, to_x = ladder_call(rest, ladder_ints, at, True, after=(to_mid,), columns=2)
     x2 = lax.ppermute(to_x, "red", along_x)
-    to_outer = hop(sums, 2, [mid_a, mid_b], parts=2, after=(keep2,), weight=0, trailer=WIDE)
+    to_outer, s2 = hop(sums, 2, [mid_a, mid_b], parts=2, through=(s2,), after=(keep2,), weight=0, trailer=WIDE)
+    r2 = lax.ppermute(s2, "blk", inward)
     outer = lax.ppermute(to_outer, "blk", outward)
     near = jnp.where(red // 2 == chip // 2, 1, 0)
-    to_y1 = turn(ints(1 - near), (keep0, x0), (keep1, x1), 0, after=(to_outer,), weight=0, trailer=WIDE)
+    to_y1 = turn(ints(1 - near), (keep0, x0), (keep1, x1), 0, after=(to_outer,), weight=0, trailer=6 * TRAILER)
     y1 = lax.ppermute(to_y1, "red", along_y)
-    to_inner, s2 = hop(sums, 1, [r1], parts=2, through=(s2,), after=(to_y1,), weight=8)
-    r2 = lax.ppermute(s2, "blk", inward)
+    to_inner = hop(sums, 1, [r1], parts=2, after=(to_y1,), weight=8)
     inner = lax.ppermute(to_inner, "blk", middle)
-    to_y2 = turn(ints(1 - near), (keep0, x0), (keep2, x2), 1, after=(to_inner,), weight=4)
+    to_y2 = turn(ints(1 - near), (keep0, x0), (keep2, x2), 1, after=(to_inner,), weight=0)
     y2 = lax.ppermute(to_y2, "red", along_y)
 
     orbital_ids = jnp.arange(occ_energy.shape[0], dtype=jnp.int32)
@@ -544,10 +611,10 @@
     pair_energy = lax.dynamic_slice_in_dim(occ_energy, red * occ_red, occ_red)
     first_virtual = lax.dynamic_slice_in_dim(vir_energy, blk * vir_block, vir_block)
     base = first_virtual[:, None] + vir_energy[None, :]
-    cycle = [r2, inner, outer]
     at = ints(near, core)
-    chunk1 = [(keep1, x1), (keep2, x2)]
-    return finish(at, slab_energy, pair_energy, base, sums, cycle, (keep0, x0), chunk1, [y1, y2], slab)
+    shape = (slab, occ_red, vir_block, virt)
+    settled = settle(at, shape, sums, outer, (keep0, x0), [(keep1, x1), (keep2, x2)], [y1, y2])
+    return finish(at, slab_energy, pair_energy, base, settled, [r2, inner])
 
 
 def plain_shards(amplitudes, ladder_ints, cycle_ints, occ_energy, vir_energy, slab_index):

time: 290 us -> 283 us (0.976)
  waiting for transfers between devices: 55.7 us -> 47 us
  starting transfers between devices: 35.6 us -> 40.3 us
    pallas_call x0 -> x2, Pallas kernels: none -> 10.3 us  [the longest x1 9.72 us: settle(): pl.pallas_call(settle_kernel, grid_spec=pltpu.PrefetchScalarGridSpec(num_...]
    pallas_call x1, Pallas kernels: 11.4 us -> 5.47 us  [finish(): pl.pallas_call(finish_kernel, grid_spec=pltpu.PrefetchScalarGridSpec(num_...]
    ppermute x1, waiting for transfers between devices: 28.1 us -> 23 us  [paired_shards(): y2 = lax.ppermute(to_y2, 'red', along_y)]
    pallas_call x4, Pallas kernels: 77.5 us -> 73.2 us  [cycle_call(): pl.pallas_call(functools.partial(cycle_kernel, keeps=got is not None, ski...]
    ppermute x1, waiting for transfers between devices: 3.02 us -> 0.01 us  [paired_shards(): r0b = lax.ppermute(s0b, 'blk', inward)]
  transfers between devices with their start and end apart: 30 -> 30, of which waited for: 9 -> 8; matrix products, arithmetic and copies ran while one was open for 3% -> 3% of each run, Pallas kernels for 55% -> 58%
where the time goes in v3:
time: 283 us; the launch traced here: 282 us
  Pallas kernels  171 us (60%)
  waiting for transfers between devices  47 us (17%)
  starting transfers between devices  40.3 us (14%)
  local copies, waits for them, and re-layouts  18.5 us (7%)
  other arithmetic  4.02 us (1%)
    pallas_call x4, Pallas kernels, cycle_call(): pl.pallas_call(functools.partial(cycle_kernel, keeps=got is not None, ski...  73.2 us
    pallas_call x4, Pallas kernels, ladder_call(): pl.pallas_call(kernel, grid_spec=pltpu.PrefetchScalarGridSpec(num_scalar_...  58.6 us
    ppermute x1, waiting for transfers between devices, paired_shards(): y2 = lax.ppermute(to_y2, 'red', along_y)  23 us
    unnamed x50, local copies, waits for them, and re-layouts  15.4 us
    ppermute x1, waiting for transfers between devices, paired_shards(): rx = lax.ppermute(mine, 'red', along_x)  14 us
    pallas_call x4, Pallas kernels, hop(): pl.pallas_call(functools.partial(hop_kernel, joins=joins, skip=skip, trai...  13.6 us
    pallas_call x1, Pallas kernels, settle(): pl.pallas_call(settle_kernel, grid_spec=pltpu.PrefetchScalarGridSpec(num_...  9.72 us
    pallas_call x2, Pallas kernels, turn(): pl.pallas_call(functools.partial(turn_kernel, trailer=trailer), grid_spec...  7.66 us
  transfers between devices with their start and end apart: 30, of which 8 were waited for; matrix products, arithmetic and copies ran while one was open for 3% of the time, Pallas kernels for 58%

profile of v3, /device:TPU:8, one launch (start us, length us, event | category | flops | bytes accessed | tf_op | source)
XLA Modules:
  0.0 281.7 jit_solution(14122890083410743772)
XLA Ops:
  0.0 3.4 %copy.23 = bf16[24,8,32,128]{3,1,2,0:T(8,128)(2,1)} copy(bf16[24,8,32,128]{3,2,1,0:T(8,128)(2,1)} %bitcast.27) | data formatting | bytes 3145728
  4.3 1.6 collective-permute-start
  5.9 1.5 collective-permute-start.1
  7.9 4.6 %collective-permute-start.3 = (bf16[192,4096]{1,0:T(8,128)(2,1)}, bf16[192,4096]{1,0:T(8,128)(2,1)S(1)}, u32[]{:S(2)}, u32[]{:S(2)}) collective-permute-start(bf16[192,4096]{1,0:T(8,128)(2,1)} %bitcast.19.refs_0_), channel_id=1, source_target_pairs={{8,16},{12,20},{16,8},{20,12},{9,17},{13,21},{17,9},{21,13},{10,18... | collective-permute-start | bytes 4718600 | tf_op jit(solution)/shard_map/ppermute | solution.py:551
  13.0 14.2 %shard_map.73.refs_2_.refs_3_ = f32[384,2048]{1,0:T(8,128)} custom-call(s32[8]{0:T(128)} %broadcast_3_at_ref.2.at_ref, bf16[192,4096]{1,0:T(8,128)(2,1)} %bitcast.19.refs_0_, bf16[192,4096]{1,0:T(8,128)(2,1)} %collective-permute-done.4.refs_1_, bf16[4096,2048]{1,0:T(8,128)(2,1)} %refs_8_.3), custom_call_target="tpu_custom_call" | custom-call | flops 1000 | bytes 1000 | tf_op jit(solution)/shard_map/pallas_call | solution.py:301
  27.2 14.0 %collective-permute-done.rx_ref = bf16[256,3072]{1,0:T(8,128)(2,1)S(1)} collective-permute-done((bf16[256,3072]{1,0:T(8,128)(2,1)S(1)}, bf16[256,3072]{1,0:T(8,128)(2,1)S(1)}, u32[]{:S(2)}, u32[]{:S(2)}) %collective-permute-start) | collective-permute-done | bytes 1572896 | tf_op jit(solution)/shard_map/ppermute | solution.py:546
  43.9 3.0 %collective-permute-done.3.refs_1_ = bf16[192,4096]{1,0:T(8,128)(2,1)S(1)} collective-permute-done((bf16[192,4096]{1,0:T(8,128)(2,1)}, bf16[192,4096]{1,0:T(8,128)(2,1)S(1)}, u32[]{:S(2)}, u32[]{:S(2)}) %collective-permute-start.3) | collective-permute-done | bytes 1572896 | tf_op jit(solution)/shard_map/ppermute | solution.py:551
  48.1 2.5 shard_map.74
  55.9 3.8 %collective-permute-start.9 = (bf16[192,4096]{1,0:T(8,128)(2,1)}, bf16[192,4096]{1,0:T(8,128)(2,1)S(1)}, u32[]{:S(2)}, u32[]{:S(2)}) collective-permute-start(bf16[192,4096]{1,0:T(8,128)(2,1)} %get-tuple-element.30.refs_0_), channel_id=1, source_target_pairs={{8,16},{12,20},{16,8},{20,12},{9,17},{13,21},{17,9},{21,13},{10,18... | collective-permute-start | bytes 4718600 | tf_op jit(solution)/shard_map/ppermute | solution.py:558
  59.7 15.6 %shard_map.75 = (f32[1,384,2048]{2,1,0:T(8,128)}, s16[416,2048]{1,0:T(8,128)(2,1)}) custom-call(s32[4]{0:T(128)} %pad_add_fusion.3.at_ref, bf16[192,4096]{1,0:T(8,128)(2,1)} %get-tuple-element.30.refs_0_, bf16[192,4096]{1,0:T(8,128)(2,1)} %collective-permute-done.7.refs_1_, bf16[4096,2048]{1,0:T(8,128)(2,1)} %refs_8_.3, f32[384,2048]{1,0:T(8,128)} %shard_map.73.refs_2_.refs_3_), custom_call_target="tpu_custom_call" | custom-call | flops 1000 | bytes 1000 | tf_op jit(solution)/shard_map/pallas_call | solution.py:301
  76.9 17.4 %shard_map.76.refs_0_ = s16[1040,1536]{1,0:T(8,128)(2,1)} custom-call(s32[5]{0:T(128)} %get-tuple-element.51.at_ref, bf16[256,3072]{1,0:T(8,128)(2,1)} %bitcast.23, bf16[256,3072]{1,0:T(8,128)(2,1)} %copy-done.2, bf16[256,3072]{1,0:T(8,128)(2,1)} %copy-done.3, bf16[128,3072]{1,0:T(8,128)(2,1)} %copy-done.13, bf16[128,3072]{1,0:T(8,128)(2,1)} %copy-done.14, ...), custom_call_target="tpu_custom_call" | custom-call | flops 21850001408 | bytes 1000 | tf_op jit(solution)/shard_map/pallas_call | solution.py:170
  96.8 17.4 %shard_map.77.refs_1_ = s16[1040,1536]{1,0:T(8,128)(2,1)} custom-call(s32[5]{0:T(128)} %get-tuple-element.51.at_ref, bf16[256,3072]{1,0:T(8,128)(2,1)} %bitcast.24, bf16[256,3072]{1,0:T(8,128)(2,1)} %copy-done.2, bf16[256,3072]{1,0:T(8,128)(2,1)} %copy-done.3, bf16[128,3072]{1,0:T(8,128)(2,1)} %copy-done.13, bf16[128,3072]{1,0:T(8,128)(2,1)} %copy-done.14, ...), custom_call_target="tpu_custom_call" | custom-call | flops 21850001408 | bytes 1000 | tf_op jit(solution)/shard_map/pallas_call | solution.py:170
  117.9 19.2 %shard_map.78 = (f32[4,256,3072]{2,1,0:T(8,128)}, s16[272,1536]{1,0:T(8,128)(2,1)}, s16[272,3072]{1,0:T(8,128)(2,1)}, s16[288,3072]{1,0:T(8,128)(2,1)}) custom-call(s32[5]{0:T(128)} %get-tuple-element.52.at_ref, bf16[256,3072]{1,0:T(8,128)(2,1)} %bitcast.25, bf16[256,3072]{1,0:T(8,128)(2,1)} %copy-done.2, bf16[256,3072]{1,0:T(8,128)(2,1)} %copy-done.3, ...), custom_call_target="tpu_custom_call" | custom-call | flops 21850001408 | bytes 1000 | tf_op jit(solution)/shard_map/pallas_call | solution.py:170
  138.8 19.2 %shard_map.79 = (f32[4,256,3072]{2,1,0:T(8,128)}, s16[272,1536]{1,0:T(8,128)(2,1)}, s16[272,3072]{1,0:T(8,128)(2,1)}, s16[288,3072]{1,0:T(8,128)(2,1)}) custom-call(s32[5]{0:T(128)} %get-tuple-element.52.at_ref, bf16[256,3072]{1,0:T(8,128)(2,1)} %bitcast.26, ...), custom_call_target="tpu_custom_call", output_to_operand_aliasing={{0}: (9, {}), {2}: (10, {}), {3}: (11, {})} | custom-call | flops 21850001408 | bytes 1000 | tf_op jit(solution)/shard_map/pallas_call | solution.py:170
  158.0 1.9 collective-permute-done.13.refs_4_.refs_0_
  162.6 1.5 collective-permute-start.26
  164.0 3.0 %shard_map.81.refs_9_ = s16[272,1536]{1,0:T(8,128)(2,1)} custom-call(f32[4,256,3072]{2,1,0:T(8,128)} %get-tuple-element.36.refs_3_.base_ref.refs_0_.refs_1_, s16[272,1536]{1,0:T(8,128)(2,1)} %collective-permute-done.13.refs_4_.refs_0_, s16[272,3072]{1,0:T(8,128)(2,1)} %get-tuple-element.40.refs_1_), custom_call_target="tpu_custom_call" | custom-call | flops 4600001024 | bytes 1000 | tf_op jit(solution)/shard_map/pallas_call | solution.py:220
  167.0 2.0 collective-permute-start.15
  171.4 14.4 %shard_map.82 = (f32[1,384,1024]{2,1,0:T(8,128)}, s16[400,1024]{1,0:T(8,128)(2,1)}) custom-call(s32[6]{0:T(128)} %stack.51.at_ref, bf16[192,4096]{1,0:T(8,128)(2,1)} %get-tuple-element.32.refs_0_, bf16[192,4096]{1,0:T(8,128)(2,1)} %copy-done.8, bf16[192,4096]{1,0:T(8,128)(2,1)} %copy-done.7, bf16[192,4096]{1,0:T(8,128)(2,1)} %collective-permute-done.17.refs_3_, ...), custom_call_target="tpu_custom_call" | custom-call | flops 1000 | bytes 1000 | tf_op jit(solution)/shard_map/pallas_call | solution.py:301
  185.8 3.1 %shard_map.83.refs_9_ = s16[272,1536]{1,0:T(8,128)(2,1)} custom-call(f32[4,256,3072]{2,1,0:T(8,128)} %get-tuple-element.36.refs_3_.base_ref.refs_0_.refs_1_, s16[272,1536]{1,0:T(8,128)(2,1)} %collective-permute-done.16.refs_0_, f32[1,384,1024]{2,1,0:T(8,128)} %get-tuple-element.44.refs_1_.refs_2_.refs_10_.refs_11_), custom_call_target="tpu_custom_call" | custom-call | flops 4600001024 | bytes 1000 | tf_op jit(solution)/shard_map/pallas_call | solution.py:220
  188.9 3.8 %collective-permute-start.21 = (s16[272,1536]{1,0:T(8,128)(2,1)}, s16[272,1536]{1,0:T(8,128)(2,1)S(1)}, u32[]{:S(2)}, u32[]{:S(2)}) collective-permute-start(s16[272,1536]{1,0:T(8,128)(2,1)} %shard_map.83.refs_9_), channel_id=1, source_target_pairs={{8,16},{12,20},{16,8},{20,12},{9,17},{13,21},{17,9},{21,13},{10,18... | collective-permute-start | bytes 2506760 | tf_op jit(solution)/shard_map/ppermute | solution.py:593
  194.2 14.4 %shard_map.84 = (f32[1,384,1024]{2,1,0:T(8,128)}, s16[400,1024]{1,0:T(8,128)(2,1)}) custom-call(s32[6]{0:T(128)} %stack.52.at_ref, bf16[192,4096]{1,0:T(8,128)(2,1)} %get-tuple-element.32.refs_0_, bf16[192,4096]{1,0:T(8,128)(2,1)} %copy-done.8, bf16[192,4096]{1,0:T(8,128)(2,1)} %copy-done.7, bf16[192,4096]{1,0:T(8,128)(2,1)} %collective-permute-done.17.refs_3_, ...), custom_call_target="tpu_custom_call" | custom-call | flops 1000 | bytes 1000 | tf_op jit(solution)/shard_map/pallas_call | solution.py:301
  209.9 2.0 collective-permute-done.21.refs_1_
  212.8 3.8 %shard_map.85 = (s16[288,3072]{1,0:T(8,128)(2,1)}, s16[288,3072]{1,0:T(8,128)(2,1)}) custom-call(f32[4,256,3072]{2,1,0:T(8,128)} %get-tuple-element.36.refs_3_.base_ref.refs_0_.refs_1_, s16[272,1536]{1,0:T(8,128)(2,1)} %collective-permute-done.15.refs_0_, s16[272,1536]{1,0:T(8,128)(2,1)} %copy-done.19, ...), custom_call_target="tpu_custom_call", output_to_operand_aliasing={{1}: (3, {})} | custom-call | flops 1000 | bytes 1000 | tf_op jit(solution)/shard_map/pallas_call | solution.py:220
  216.6 2.5 collective-permute-start.22
  220.0 3.9 %shard_map.86.refs_1_ = s16[480,1024]{1,0:T(8,128)(2,1)} custom-call(s32[1]{0:T(128)} %bitcast.9.at_ref, f32[1,384,2048]{2,1,0:T(8,128)} %get-tuple-element.31.refs_0_.refs_5_.refs_6_, s16[416,2048]{1,0:T(8,128)(2,1)} %copy-done, f32[1,384,1024]{2,1,0:T(8,128)} %get-tuple-element.44.refs_1_.refs_2_.refs_10_.refs_11_, s16[400,1024]{1,0:T(8,128)(2,1)} %copy-done.11, ...), custom_call_target="tpu_custom_call" | custom-call | flops 1000 | bytes 1000 | tf_op jit(solution)/shard_map/pallas_call | solution.py:331
  226.7 3.8 %shard_map.87.refs_4_ = s16[272,3072]{1,0:T(8,128)(2,1)} custom-call(f32[4,256,3072]{2,1,0:T(8,128)} %get-tuple-element.36.refs_3_.base_ref.refs_0_.refs_1_, s16[272,3072]{1,0:T(8,128)(2,1)} %collective-permute-done.26.refs_0_, s16[480,1024]{1,0:T(8,128)(2,1)} %shard_map.86.refs_1_), custom_call_target="tpu_custom_call" | custom-call | flops 9200001024 | bytes 1000 | tf_op jit(solution)/shard_map/pallas_call | solution.py:220
  230.5 3.8 %collective-permute-start.29 = (s16[272,3072]{1,0:T(8,128)(2,1)}, s16[272,3072]{1,0:T(8,128)(2,1)}, u32[]{:S(2)}, u32[]{:S(2)}) collective-permute-start(s16[272,3072]{1,0:T(8,128)(2,1)} %shard_map.87.refs_4_), channel_id=1, source_target_pairs={{8,16},{12,20},{16,8},{20,12},{9,17},{13,21},{17,9},{21,13},{10,18... | collective-permute-start | bytes 5013512 | tf_op jit(solution)/shard_map/ppermute | solution.py:604
  235.2 3.7 %shard_map.88 = s16[400,1024]{1,0:T(8,128)(2,1)} custom-call(s32[1]{0:T(128)} %bitcast.9.at_ref, f32[1,384,2048]{2,1,0:T(8,128)} %get-tuple-element.31.refs_0_.refs_5_.refs_6_, s16[416,2048]{1,0:T(8,128)(2,1)} %copy-done, f32[1,384,1024]{2,1,0:T(8,128)} %get-tuple-element.46.refs_3_.refs_2_.refs_15_.refs_16_, s16[400,1024]{1,0:T(8,128)(2,1)} %copy-done.12, ...), custom_call_target="tpu_custom_call" | custom-call | flops 1000 | bytes 1000 | tf_op jit(solution)/shard_map/pallas_call | solution.py:331
  242.3 23.0 %collective-permute-done.27.refs_23_.refs_24_.refs_25_ = s16[400,1024]{1,0:T(8,128)(2,1)} collective-permute-done((s16[400,1024]{1,0:T(8,128)(2,1)}, s16[400,1024]{1,0:T(8,128)(2,1)}, u32[]{:S(2)}, u32[]{:S(2)}) %collective-permute-start.27) | collective-permute-done | bytes 819232 | tf_op jit(solution)/shard_map/ppermute | solution.py:606
  265.3 9.7 %shard_map.89.settled_ref = f32[8,48,16,128]{3,2,1,0:T(8,128)} custom-call(s32[2]{0:T(128)} %pad_add_fusion.at_ref, f32[4,256,3072]{2,1,0:T(8,128)} %get-tuple-element.36.refs_3_.base_ref.refs_0_.refs_1_, f32[4,256,3072]{2,1,0:T(8,128)} %get-tuple-element.36.refs_3_.base_ref.refs_0_.refs_1_, ...), custom_call_target="tpu_custom_call" | custom-call | flops 8050000896 | bytes 1000 | tf_op jit(solution)/shard_map/pallas_call | solution.py:442
  276.3 5.5 %shard_map.90 = f32[8,48,16,128]{3,2,1,0:T(8,128)} custom-call(s32[2]{0:T(128)} %pad_add_fusion.at_ref, f32[8]{0:T(128)} %select_reduce_fusion.slab_ref, f32[48]{0:T(128)} %dynamic_slice.9.pair_ref, f32[16,128]{1,0:T(8,128)} %broadcast_add_fusion.base_ref, f32[8,48,16,128]{3,2,1,0:T(8,128)} %shard_map.89.settled_ref, s16[288,3072]{1,0:T(8,128)(2,1)} %copy-done.4, ...), custom_call_target="tpu_custom_call" | custom-call | flops 1000 | bytes 1000 | tf_op jit(solution)/shard_map/pallas_call | solution.py:489
  (109 shorter events, 38.0 us)
Async XLA Ops:
  3.4 9.1 %collective-permute-start.4 = (bf16[192,4096]{1,0:T(8,128)(2,1)}, bf16[192,4096]{1,0:T(8,128)(2,1)}, u32[]{:S(2)}, u32[]{:S(2)}) collective-permute-start(bf16[192,4096]{1,0:T(8,128)(2,1)} %bitcast.19.refs_0_), channel_id=1, source_target_pairs={{0,4},{4,0},{8,12},{12,8},{16,20},{20,16},{24,28},{28,24},{1,5},{5... | collective-permute-start | bytes 4718600 | tf_op jit(solution)/shard_map/ppermute | solution.py:552
  4.3 22.8 %copy-start.1 = (bf16[32,8,24,128]{3,1,2,0:T(8,128)(2,1)}, bf16[32,8,24,128]{3,1,2,0:T(8,128)(2,1)S(1)}, u32[]{:S(2)}) copy-start(bf16[32,8,24,128]{3,1,2,0:T(8,128)(2,1)S(1)} %copy.24) | copy-start | bytes 4718596
  4.3 36.9 %collective-permute-start = (bf16[256,3072]{1,0:T(8,128)(2,1)S(1)}, bf16[256,3072]{1,0:T(8,128)(2,1)S(1)}, u32[]{:S(2)}, u32[]{:S(2)}) collective-permute-start(bf16[256,3072]{1,0:T(8,128)(2,1)S(1)} %bitcast.21), channel_id=1, source_target_pairs={{0,1},{1,0},{2,3},{3,2},{4,5},{5,4},{6,7},{7,6},{8,9},{9,8},{10,11... | collective-permute-start | bytes 4718600 | tf_op jit(solution)/shard_map/ppermute | solution.py:546
  5.9 36.5 %collective-permute-start.1 = (bf16[256,3072]{1,0:T(8,128)(2,1)S(1)}, bf16[256,3072]{1,0:T(8,128)(2,1)S(1)}, u32[]{:S(2)}, u32[]{:S(2)}) collective-permute-start(bf16[256,3072]{1,0:T(8,128)(2,1)S(1)} %bitcast.22), channel_id=1, source_target_pairs={{0,2},{1,3},{2,0},{3,1},{4,6},{5,7},{6,4},{7,5},{8,10},{9,11},{10,... | collective-permute-start | bytes 4718600 | tf_op jit(solution)/shard_map/ppermute | solution.py:547
  7.4 36.5 %collective-permute-start.2 = (bf16[192,4096]{1,0:T(8,128)(2,1)}, bf16[192,4096]{1,0:T(8,128)(2,1)S(1)}, u32[]{:S(2)}, u32[]{:S(2)}) collective-permute-start(bf16[192,4096]{1,0:T(8,128)(2,1)} %bitcast.19.refs_0_), channel_id=1, source_target_pairs={{0,8},{4,12},{8,0},{12,4},{16,24},{20,28},{24,16},{28,20},{1,9},{5... | collective-permute-start | bytes 4718600 | tf_op jit(solution)/shard_map/ppermute | solution.py:550
  7.9 39.0 %collective-permute-start.3 = (bf16[192,4096]{1,0:T(8,128)(2,1)}, bf16[192,4096]{1,0:T(8,128)(2,1)S(1)}, u32[]{:S(2)}, u32[]{:S(2)}) collective-permute-start(bf16[192,4096]{1,0:T(8,128)(2,1)} %bitcast.19.refs_0_), channel_id=1, source_target_pairs={{8,16},{12,20},{16,8},{20,12},{9,17},{13,21},{17,9},{21,13},{10,18... | collective-permute-start | bytes 4718600 | tf_op jit(solution)/shard_map/ppermute | solution.py:551
  50.6 5.3 %collective-permute-start.7 = (bf16[192,4096]{1,0:T(8,128)(2,1)}, bf16[192,4096]{1,0:T(8,128)(2,1)}, u32[]{:S(2)}, u32[]{:S(2)}) collective-permute-start(bf16[192,4096]{1,0:T(8,128)(2,1)} %get-tuple-element.30.refs_0_), channel_id=1, source_target_pairs={{0,4},{4,0},{8,12},{12,8},{16,20},{20,16},{24,28},{28,24},{1,5},{5... | collective-permute-start | bytes 4718600 | tf_op jit(solution)/shard_map/ppermute | solution.py:560
  50.7 24.6 %collective-permute-start.8 = (bf16[192,4096]{1,0:T(8,128)(2,1)}, bf16[192,4096]{1,0:T(8,128)(2,1)S(1)}, u32[]{:S(2)}, u32[]{:S(2)}) collective-permute-start(bf16[192,4096]{1,0:T(8,128)(2,1)} %get-tuple-element.32.refs_0_), channel_id=1, source_target_pairs={{0,4},{4,0},{8,12},{12,8},{16,20},{20,16},{24,28},{28,24},{1,5},{5... | collective-permute-start | bytes 4718600 | tf_op jit(solution)/shard_map/ppermute | solution.py:561
  51.2 24.1 %collective-permute-start.5 = (bf16[128,3072]{1,0:T(8,128)(2,1)}, bf16[128,3072]{1,0:T(8,128)(2,1)S(1)}, u32[]{:S(2)}, u32[]{:S(2)}) collective-permute-start(bf16[128,3072]{1,0:T(8,128)(2,1)} %get-tuple-element.28), channel_id=1, source_target_pairs={{0,2},{1,3},{2,0},{3,1},{4,6},{5,7},{6,4},{7,5},{8,10},{9,11},{10,... | collective-permute-start | bytes 2359304 | tf_op jit(solution)/shard_map/ppermute | solution.py:557
  51.7 23.6 %collective-permute-start.6 = (bf16[128,3072]{1,0:T(8,128)(2,1)}, bf16[128,3072]{1,0:T(8,128)(2,1)S(1)}, u32[]{:S(2)}, u32[]{:S(2)}) collective-permute-start(bf16[128,3072]{1,0:T(8,128)(2,1)} %get-tuple-element.29), channel_id=1, source_target_pairs={{0,1},{1,0},{2,3},{3,2},{4,5},{5,4},{6,7},{7,6},{8,9},{9,8},{10,11... | collective-permute-start | bytes 2359304 | tf_op jit(solution)/shard_map/ppermute | solution.py:556
  54.2 40.3 %collective-permute-start.10 = (bf16[192,4096]{1,0:T(8,128)(2,1)}, bf16[192,4096]{1,0:T(8,128)(2,1)S(1)}, u32[]{:S(2)}, u32[]{:S(2)}) collective-permute-start(bf16[192,4096]{1,0:T(8,128)(2,1)} %get-tuple-element.32.refs_0_), channel_id=1, source_target_pairs={{8,0},{12,4},{16,24},{20,28},{9,1},{13,5},{17,25},{21,29},{10,2},{... | collective-permute-start | bytes 4718600 | tf_op jit(solution)/shard_map/ppermute | solution.py:559
  55.9 38.6 %collective-permute-start.9 = (bf16[192,4096]{1,0:T(8,128)(2,1)}, bf16[192,4096]{1,0:T(8,128)(2,1)S(1)}, u32[]{:S(2)}, u32[]{:S(2)}) collective-permute-start(bf16[192,4096]{1,0:T(8,128)(2,1)} %get-tuple-element.30.refs_0_), channel_id=1, source_target_pairs={{8,16},{12,20},{16,8},{20,12},{9,17},{13,21},{17,9},{21,13},{10,18... | collective-permute-start | bytes 4718600 | tf_op jit(solution)/shard_map/ppermute | solution.py:558
  94.3 23.1 %collective-permute-start.12 = (s16[1040,1536]{1,0:T(8,128)(2,1)}, s16[1040,1536]{1,0:T(8,128)(2,1)}, u32[]{:S(2)}, u32[]{:S(2)}) collective-permute-start(s16[1040,1536]{1,0:T(8,128)(2,1)} %shard_map.76.refs_0_), channel_id=1, source_target_pairs={{0,4},{4,0},{8,12},{12,8},{16,20},{20,16},{24,28},{28,24},{1,5},{5... | collective-permute-start | bytes 9584648 | tf_op jit(solution)/shard_map/ppermute | solution.py:572
  114.1 23.0 %collective-permute-start.11 = (s16[1040,1536]{1,0:T(8,128)(2,1)}, s16[1040,1536]{1,0:T(8,128)(2,1)S(1)}, u32[]{:S(2)}, u32[]{:S(2)}) collective-permute-start(s16[1040,1536]{1,0:T(8,128)(2,1)} %shard_map.77.refs_1_), channel_id=1, source_target_pairs={{0,4},{4,0},{8,12},{12,8},{16,20},{20,16},{24,28},{28,24},{1,5},{5... | collective-permute-start | bytes 9584648 | tf_op jit(solution)/shard_map/ppermute | solution.py:574
  114.7 54.3 %collective-permute-start.20 = (s16[416,2048]{1,0:T(8,128)(2,1)}, s16[416,2048]{1,0:T(8,128)(2,1)S(1)}, u32[]{:S(2)}, u32[]{:S(2)}) collective-permute-start(s16[416,2048]{1,0:T(8,128)(2,1)} %get-tuple-element.43), channel_id=1, source_target_pairs={{0,1},{1,0},{2,3},{3,2},{4,5},{5,4},{6,7},{7,6},{8,9},{9,8},{10,11... | collective-permute-start | bytes 5111816 | tf_op jit(solution)/shard_map/ppermute | solution.py:566
  115.9 42.1 %collective-permute-start.14 = (bf16[192,4096]{1,0:T(8,128)(2,1)}, bf16[192,4096]{1,0:T(8,128)(2,1)S(1)}, u32[]{:S(2)}, u32[]{:S(2)}) collective-permute-start(bf16[192,4096]{1,0:T(8,128)(2,1)} %copy-done.9), channel_id=1, source_target_pairs={{8,0},{12,4},{16,24},{20,28},{9,1},{13,5},{17,25},{21,29},{10,2},{... | collective-permute-start | bytes 4718600 | tf_op jit(solution)/shard_map/ppermute | solution.py:579
  117.3 45.2 %collective-permute-start.17 = (bf16[192,4096]{1,0:T(8,128)(2,1)}, bf16[192,4096]{1,0:T(8,128)(2,1)}, u32[]{:S(2)}, u32[]{:S(2)}) collective-permute-start(bf16[192,4096]{1,0:T(8,128)(2,1)} %copy-done.8), channel_id=1, source_target_pairs={{0,4},{4,0},{8,12},{12,8},{16,20},{20,16},{24,28},{28,24},{1,5},{5... | collective-permute-start | bytes 4718600 | tf_op jit(solution)/shard_map/ppermute | solution.py:563
  117.4 49.6 %collective-permute-start.18 = (bf16[192,4096]{1,0:T(8,128)(2,1)}, bf16[192,4096]{1,0:T(8,128)(2,1)}, u32[]{:S(2)}, u32[]{:S(2)}) collective-permute-start(bf16[192,4096]{1,0:T(8,128)(2,1)} %copy-done.9), channel_id=1, source_target_pairs={{0,4},{4,0},{8,12},{12,8},{16,20},{20,16},{24,28},{28,24},{1,5},{5... | collective-permute-start | bytes 4718600 | tf_op jit(solution)/shard_map/ppermute | solution.py:562
  137.2 22.8 %collective-permute-start.13 = (s16[272,1536]{1,0:T(8,128)(2,1)}, s16[272,1536]{1,0:T(8,128)(2,1)}, u32[]{:S(2)}, u32[]{:S(2)}) collective-permute-start(s16[272,1536]{1,0:T(8,128)(2,1)} %get-tuple-element.37), channel_id=1, source_target_pairs={{0,8},{4,12},{24,16},{28,20},{1,9},{5,13},{25,17},{29,21},{2,10},{... | collective-permute-start | bytes 2506760 | tf_op jit(solution)/shard_map/ppermute | solution.py:576
  160.5 8.5 %collective-permute-start.19 = (bf16[192,4096]{1,0:T(8,128)(2,1)}, bf16[192,4096]{1,0:T(8,128)(2,1)S(1)}, u32[]{:S(2)}, u32[]{:S(2)}) collective-permute-start(bf16[192,4096]{1,0:T(8,128)(2,1)} %get-tuple-element.42.refs_5_), channel_id=1, source_target_pairs={{0,4},{4,0},{8,12},{12,8},{16,20},{20,16},{24,28},{28,24},{1,5},{5... | collective-permute-start | bytes 4718600 | tf_op jit(solution)/shard_map/ppermute | solution.py:583
  160.6 25.2 %collective-permute-start.16 = (s16[272,1536]{1,0:T(8,128)(2,1)}, s16[272,1536]{1,0:T(8,128)(2,1)}, u32[]{:S(2)}, u32[]{:S(2)}) collective-permute-start(s16[272,1536]{1,0:T(8,128)(2,1)} %get-tuple-element.41), channel_id=1, source_target_pairs={{0,8},{4,12},{24,16},{28,20},{1,9},{5,13},{25,17},{29,21},{2,10},{... | collective-permute-start | bytes 2506760 | tf_op jit(solution)/shard_map/ppermute | solution.py:578
  162.6 64.2 %collective-permute-start.26 = (s16[272,3072]{1,0:T(8,128)(2,1)}, s16[272,3072]{1,0:T(8,128)(2,1)}, u32[]{:S(2)}, u32[]{:S(2)}) collective-permute-start(s16[272,3072]{1,0:T(8,128)(2,1)} %get-tuple-element.40.refs_1_), channel_id=1, source_target_pairs={{0,8},{4,12},{24,16},{28,20},{1,9},{5,13},{25,17},{29,21},{2,10},{... | collective-permute-start | bytes 5013512 | tf_op jit(solution)/shard_map/ppermute | solution.py:585
  167.0 42.8 %collective-permute-start.15 = (s16[272,1536]{1,0:T(8,128)(2,1)}, s16[272,1536]{1,0:T(8,128)(2,1)}, u32[]{:S(2)}, u32[]{:S(2)}) collective-permute-start(s16[272,1536]{1,0:T(8,128)(2,1)} %shard_map.81.refs_9_), channel_id=1, source_target_pairs={{8,16},{12,20},{16,8},{20,12},{9,17},{13,21},{17,9},{21,13},{10,18... | collective-permute-start | bytes 2506760 | tf_op jit(solution)/shard_map/ppermute | solution.py:584
  188.9 23.0 %collective-permute-start.21 = (s16[272,1536]{1,0:T(8,128)(2,1)}, s16[272,1536]{1,0:T(8,128)(2,1)S(1)}, u32[]{:S(2)}, u32[]{:S(2)}) collective-permute-start(s16[272,1536]{1,0:T(8,128)(2,1)} %shard_map.83.refs_9_), channel_id=1, source_target_pairs={{8,16},{12,20},{16,8},{20,12},{9,17},{13,21},{17,9},{21,13},{10,18... | collective-permute-start | bytes 2506760 | tf_op jit(solution)/shard_map/ppermute | solution.py:593
  192.7 26.4 %collective-permute-start.23 = (s16[400,1024]{1,0:T(8,128)(2,1)S(1)}, s16[400,1024]{1,0:T(8,128)(2,1)S(1)}, u32[]{:S(2)}, u32[]{:S(2)}) collective-permute-start(s16[400,1024]{1,0:T(8,128)(2,1)S(1)} %copy-done.23), channel_id=1, source_target_pairs={{0,1},{1,0},{2,3},{3,2},{4,5},{5,4},{6,7},{7,6},{8,9},{9,8},{10,11... | collective-permute-start | bytes 2457608 | tf_op jit(solution)/shard_map/ppermute | solution.py:591
  208.6 25.7 %collective-permute-start.24 = (s16[400,1024]{1,0:T(8,128)(2,1)}, s16[400,1024]{1,0:T(8,128)(2,1)S(1)}, u32[]{:S(2)}, u32[]{:S(2)}) collective-permute-start(s16[400,1024]{1,0:T(8,128)(2,1)} %get-tuple-element.49), channel_id=1, source_target_pairs={{0,1},{1,0},{2,3},{3,2},{4,5},{5,4},{6,7},{7,6},{8,9},{9,8},{10,11... | collective-permute-start | bytes 2457608 | tf_op jit(solution)/shard_map/ppermute | solution.py:596
  216.6 48.6 %collective-permute-start.22 = (s16[288,3072]{1,0:T(8,128)(2,1)}, s16[288,3072]{1,0:T(8,128)(2,1)}, u32[]{:S(2)}, u32[]{:S(2)}) collective-permute-start(s16[288,3072]{1,0:T(8,128)(2,1)} %get-tuple-element.47.refs_4_), channel_id=1, source_target_pairs={{8,0},{12,4},{16,24},{20,28},{9,1},{13,5},{17,25},{21,29},{10,2},{... | collective-permute-start | bytes 5308424 | tf_op jit(solution)/shard_map/ppermute | solution.py:599
  224.0 41.3 %collective-permute-start.25 = (s16[480,1024]{1,0:T(8,128)(2,1)}, s16[480,1024]{1,0:T(8,128)(2,1)}, u32[]{:S(2)}, u32[]{:S(2)}) collective-permute-start(s16[480,1024]{1,0:T(8,128)(2,1)} %shard_map.86.refs_1_), channel_id=1, source_target_pairs={{0,2},{1,3},{2,0},{3,1},{4,6},{5,7},{6,4},{7,5},{8,10},{9,11},{10,... | collective-permute-start | bytes 2949128 | tf_op jit(solution)/shard_map/ppermute | solution.py:602
  225.4 49.6 %collective-permute-start.28 = (s16[288,3072]{1,0:T(8,128)(2,1)S(1)}, s16[288,3072]{1,0:T(8,128)(2,1)S(1)}, u32[]{:S(2)}, u32[]{:S(2)}) collective-permute-start(s16[288,3072]{1,0:T(8,128)(2,1)S(1)} %copy-done.5), channel_id=1, source_target_pairs={{0,8},{4,12},{24,16},{28,20},{1,9},{5,13},{25,17},{29,21},{2,10},{... | collective-permute-start | bytes 5308424 | tf_op jit(solution)/shard_map/ppermute | solution.py:598
  230.5 10.4 %copy-start.22 = (s32[8]{0:T(128)S(1)}, s32[8]{0:T(128)}, u32[]{:S(2)}) copy-start(s32[8]{0:T(128)} %param.12) | copy-start | bytes 100
  230.5 44.5 %collective-permute-start.29 = (s16[272,3072]{1,0:T(8,128)(2,1)}, s16[272,3072]{1,0:T(8,128)(2,1)}, u32[]{:S(2)}, u32[]{:S(2)}) collective-permute-start(s16[272,3072]{1,0:T(8,128)(2,1)} %shard_map.87.refs_4_), channel_id=1, source_target_pairs={{8,16},{12,20},{16,8},{20,12},{9,17},{13,21},{17,9},{21,13},{10,18... | collective-permute-start | bytes 5013512 | tf_op jit(solution)/shard_map/ppermute | solution.py:604
  238.9 26.3 %collective-permute-start.27 = (s16[400,1024]{1,0:T(8,128)(2,1)}, s16[400,1024]{1,0:T(8,128)(2,1)}, u32[]{:S(2)}, u32[]{:S(2)}) collective-permute-start(s16[400,1024]{1,0:T(8,128)(2,1)} %shard_map.88), channel_id=1, source_target_pairs={{0,2},{1,3},{2,0},{3,1},{4,6},{5,7},{6,4},{7,5},{8,10},{9,11},{10,... | collective-permute-start | bytes 2457608 | tf_op jit(solution)/shard_map/ppermute | solution.py:606
  (22 other events, 64.5 us)

commit v4 on v3

--- a/solution.py
+++ b/solution.py
@@ -11,7 +11,7 @@
 WIDE = 32
 STEPS = 64.0
 TOP = 32000.0
-VMEM = 56 * 2**20
+VMEM = 63 * 2**20 + 2**19
 
 
 def encode(groups, last):
@@ -530,9 +530,6 @@
     def line(*hops):
         return [(2 * a + c, 2 * b + c) for a, b in hops for c in range(2)]
 
-    def trade(pair):
-        return lax.all_to_all(pair, "blk", 0, 0, axis_index_groups=[[2 * z, 2 * z + 1] for z in range(4)])
-
     inward, middle, outward = line((0, 1), (3, 2)), line((1, 2), (2, 1)), line((1, 0), (2, 3))
 
     def ints(*values):

time: 283 us -> 277 us (0.979)
  local copies, waits for them, and re-layouts: 18.5 us -> 8 us
  waiting for transfers between devices: 47 us -> 51.1 us
    unnamed x50 -> x10, local copies, waits for them, and re-layouts: 15.4 us -> 4.9 us
  transfers between devices with their start and end apart: 30 -> 30, of which waited for: 8 -> 8; matrix products, arithmetic and copies ran while one was open for 3% -> 3% of each run, Pallas kernels for 58% -> 59%
where the time goes in v4:
time: 277 us; the launch traced here: 276 us
  Pallas kernels  171 us (62%)
  waiting for transfers between devices  51.1 us (18%)
  starting transfers between devices  41.4 us (15%)
  local copies, waits for them, and re-layouts  8 us (3%)
  other arithmetic  4 us (1%)
    pallas_call x4, Pallas kernels, cycle_call(): pl.pallas_call(functools.partial(cycle_kernel, keeps=got is not None, ski...  73.2 us
    pallas_call x4, Pallas kernels, ladder_call(): pl.pallas_call(kernel, grid_spec=pltpu.PrefetchScalarGridSpec(num_scalar_...  58.5 us
    ppermute x1, waiting for transfers between devices, paired_shards(): y2 = lax.ppermute(to_y2, 'red', along_y)  24.7 us
    ppermute x1, waiting for transfers between devices, paired_shards(): rx = lax.ppermute(mine, 'red', along_x)  14.3 us
    pallas_call x4, Pallas kernels, hop(): pl.pallas_call(functools.partial(hop_kernel, joins=joins, skip=skip, trai...  13.6 us
    pallas_call x1, Pallas kernels, settle(): pl.pallas_call(settle_kernel, grid_spec=pltpu.PrefetchScalarGridSpec(num_...  9.7 us
    pallas_call x2, Pallas kernels, turn(): pl.pallas_call(functools.partial(turn_kernel, trailer=trailer), grid_spec...  7.56 us
  transfers between devices with their start and end apart: 30, of which 8 were waited for; matrix products, arithmetic and copies ran while one was open for 3% of the time, Pallas kernels for 59%

profile of v4, /device:TPU:8, one launch (start us, length us, event | category | flops | bytes accessed | tf_op | source)
XLA Modules:
  0.0 276.2 jit_solution(12691826254555923951)
XLA Ops:
  0.0 3.4 %copy.23 = bf16[24,8,32,128]{3,1,2,0:T(8,128)(2,1)} copy(bf16[24,8,32,128]{3,2,1,0:T(8,128)(2,1)} %bitcast.21) | data formatting | bytes 3145728
  9.0 4.6 %collective-permute-start.3 = (bf16[192,4096]{1,0:T(8,128)(2,1)}, bf16[192,4096]{1,0:T(8,128)(2,1)}, u32[]{:S(2)}, u32[]{:S(2)}) collective-permute-start(bf16[192,4096]{1,0:T(8,128)(2,1)} %bitcast.19.refs_0_), channel_id=1, source_target_pairs={{8,16},{12,20},{16,8},{20,12},{9,17},{13,21},{17,9},{21,13},{10,18... | collective-permute-start | bytes 4718600 | tf_op jit(solution)/shard_map/ppermute | solution.py:548
  14.2 14.2 %shard_map.73.refs_2_.refs_3_ = f32[384,2048]{1,0:T(8,128)} custom-call(s32[8]{0:T(128)} %broadcast_3_at_ref.2.at_ref, bf16[192,4096]{1,0:T(8,128)(2,1)} %bitcast.19.refs_0_, bf16[192,4096]{1,0:T(8,128)(2,1)} %collective-permute-done.4.refs_1_, bf16[4096,2048]{1,0:T(8,128)(2,1)} %refs_8_.3), custom_call_target="tpu_custom_call" | custom-call | flops 1000 | bytes 1000 | tf_op jit(solution)/shard_map/pallas_call | solution.py:301
  28.3 14.3 %collective-permute-done.rx_ref = bf16[256,3072]{1,0:T(8,128)(2,1)} collective-permute-done((bf16[256,3072]{1,0:T(8,128)(2,1)}, bf16[256,3072]{1,0:T(8,128)(2,1)}, u32[]{:S(2)}, u32[]{:S(2)}) %collective-permute-start) | collective-permute-done | bytes 1572896 | tf_op jit(solution)/shard_map/ppermute | solution.py:543
  45.1 3.0 %collective-permute-done.3.refs_1_ = bf16[192,4096]{1,0:T(8,128)(2,1)} collective-permute-done((bf16[192,4096]{1,0:T(8,128)(2,1)}, bf16[192,4096]{1,0:T(8,128)(2,1)}, u32[]{:S(2)}, u32[]{:S(2)}) %collective-permute-start.3) | collective-permute-done | bytes 1572896 | tf_op jit(solution)/shard_map/ppermute | solution.py:548
  48.1 2.6 shard_map.74
  54.3 2.5 collective-permute-start.10
  56.7 3.6 %collective-permute-start.9 = (bf16[192,4096]{1,0:T(8,128)(2,1)}, bf16[192,4096]{1,0:T(8,128)(2,1)}, u32[]{:S(2)}, u32[]{:S(2)}) collective-permute-start(bf16[192,4096]{1,0:T(8,128)(2,1)} %get-tuple-element.30.refs_0_), channel_id=1, source_target_pairs={{8,16},{12,20},{16,8},{20,12},{9,17},{13,21},{17,9},{21,13},{10,18... | collective-permute-start | bytes 4718600 | tf_op jit(solution)/shard_map/ppermute | solution.py:555
  60.4 15.6 %shard_map.75 = (f32[1,384,2048]{2,1,0:T(8,128)}, s16[416,2048]{1,0:T(8,128)(2,1)}) custom-call(s32[4]{0:T(128)} %pad_add_fusion.3.at_ref, bf16[192,4096]{1,0:T(8,128)(2,1)} %get-tuple-element.30.refs_0_, bf16[192,4096]{1,0:T(8,128)(2,1)} %collective-permute-done.7.refs_1_, bf16[4096,2048]{1,0:T(8,128)(2,1)} %refs_8_.3, f32[384,2048]{1,0:T(8,128)} %shard_map.73.refs_2_.refs_3_), custom_call_target="tpu_custom_call" | custom-call | flops 1000 | bytes 1000 | tf_op jit(solution)/shard_map/pallas_call | solution.py:301
  76.0 17.4 %shard_map.76.refs_0_ = s16[1040,1536]{1,0:T(8,128)(2,1)} custom-call(s32[5]{0:T(128)} %get-tuple-element.51.at_ref, bf16[256,3072]{1,0:T(8,128)(2,1)} %bitcast.20.own_ref, bf16[256,3072]{1,0:T(8,128)(2,1)} %collective-permute-done.rx_ref, bf16[256,3072]{1,0:T(8,128)(2,1)} %collective-permute-done.1.ry_ref, ...), custom_call_target="tpu_custom_call" | custom-call | flops 21850001408 | bytes 1000 | tf_op jit(solution)/shard_map/pallas_call | solution.py:170
  94.7 17.4 %shard_map.77.refs_1_ = s16[1040,1536]{1,0:T(8,128)(2,1)} custom-call(s32[5]{0:T(128)} %get-tuple-element.51.at_ref, bf16[256,3072]{1,0:T(8,128)(2,1)} %bitcast.20.own_ref, bf16[256,3072]{1,0:T(8,128)(2,1)} %collective-permute-done.rx_ref, bf16[256,3072]{1,0:T(8,128)(2,1)} %collective-permute-done.1.ry_ref, ...), custom_call_target="tpu_custom_call" | custom-call | flops 21850001408 | bytes 1000 | tf_op jit(solution)/shard_map/pallas_call | solution.py:170
  113.8 2.4 collective-permute-start.14
  116.7 19.2 %shard_map.78 = (f32[4,256,3072]{2,1,0:T(8,128)}, s16[272,1536]{1,0:T(8,128)(2,1)}, s16[272,3072]{1,0:T(8,128)(2,1)}, s16[288,3072]{1,0:T(8,128)(2,1)}) custom-call(s32[5]{0:T(128)} %get-tuple-element.52.at_ref, bf16[256,3072]{1,0:T(8,128)(2,1)} %bitcast.20.own_ref, bf16[256,3072]{1,0:T(8,128)(2,1)} %collective-permute-done.rx_ref, ...), custom_call_target="tpu_custom_call" | custom-call | flops 21850001408 | bytes 1000 | tf_op jit(solution)/shard_map/pallas_call | solution.py:170
  137.3 19.2 %shard_map.79 = (f32[4,256,3072]{2,1,0:T(8,128)}, s16[272,1536]{1,0:T(8,128)(2,1)}, s16[272,3072]{1,0:T(8,128)(2,1)}, s16[288,3072]{1,0:T(8,128)(2,1)}) custom-call(s32[5]{0:T(128)} %get-tuple-element.52.at_ref, bf16[256,3072]{1,0:T(8,128)(2,1)} %bitcast.20.own_ref, ...), custom_call_target="tpu_custom_call", output_to_operand_aliasing={{0}: (9, {}), {2}: (10, {}), {3}: (11, {})} | custom-call | flops 21850001408 | bytes 1000 | tf_op jit(solution)/shard_map/pallas_call | solution.py:170
  156.5 2.4 collective-permute-done.13.refs_4_.refs_0_
  162.7 3.0 %shard_map.81.refs_9_ = s16[272,1536]{1,0:T(8,128)(2,1)} custom-call(f32[4,256,3072]{2,1,0:T(8,128)} %get-tuple-element.36.refs_3_.base_ref.refs_0_.refs_1_, s16[272,1536]{1,0:T(8,128)(2,1)} %collective-permute-done.13.refs_4_.refs_0_, s16[272,3072]{1,0:T(8,128)(2,1)} %get-tuple-element.40.refs_1_), custom_call_target="tpu_custom_call" | custom-call | flops 4600001024 | bytes 1000 | tf_op jit(solution)/shard_map/pallas_call | solution.py:220
  165.7 3.8 %collective-permute-start.15 = (s16[272,1536]{1,0:T(8,128)(2,1)}, s16[272,1536]{1,0:T(8,128)(2,1)}, u32[]{:S(2)}, u32[]{:S(2)}) collective-permute-start(s16[272,1536]{1,0:T(8,128)(2,1)} %shard_map.81.refs_9_), channel_id=1, source_target_pairs={{8,16},{12,20},{16,8},{20,12},{9,17},{13,21},{17,9},{21,13},{10,18... | collective-permute-start | bytes 2506760 | tf_op jit(solution)/shard_map/ppermute | solution.py:581
  169.5 14.4 %shard_map.82 = (f32[1,384,1024]{2,1,0:T(8,128)}, s16[400,1024]{1,0:T(8,128)(2,1)}) custom-call(s32[6]{0:T(128)} %stack.51.at_ref, bf16[192,4096]{1,0:T(8,128)(2,1)} %get-tuple-element.32.refs_0_, bf16[192,4096]{1,0:T(8,128)(2,1)} %collective-permute-done.10.refs_2_.refs_1_, bf16[192,4096]{1,0:T(8,128)(2,1)} %collective-permute-done.8.refs_1_.refs_2_, ...), custom_call_target="tpu_custom_call" | custom-call | flops 1000 | bytes 1000 | tf_op jit(solution)/shard_map/pallas_call | solution.py:301
  183.9 3.0 %shard_map.83.refs_9_ = s16[272,1536]{1,0:T(8,128)(2,1)} custom-call(f32[4,256,3072]{2,1,0:T(8,128)} %get-tuple-element.36.refs_3_.base_ref.refs_0_.refs_1_, s16[272,1536]{1,0:T(8,128)(2,1)} %collective-permute-done.16.refs_0_, f32[1,384,1024]{2,1,0:T(8,128)} %get-tuple-element.44.refs_1_.refs_2_.refs_10_.refs_11_), custom_call_target="tpu_custom_call" | custom-call | flops 4600001024 | bytes 1000 | tf_op jit(solution)/shard_map/pallas_call | solution.py:220
  186.9 2.8 collective-permute-start.21
  191.0 14.4 %shard_map.84 = (f32[1,384,1024]{2,1,0:T(8,128)}, s16[400,1024]{1,0:T(8,128)(2,1)}) custom-call(s32[6]{0:T(128)} %stack.52.at_ref, bf16[192,4096]{1,0:T(8,128)(2,1)} %get-tuple-element.32.refs_0_, bf16[192,4096]{1,0:T(8,128)(2,1)} %collective-permute-done.10.refs_2_.refs_1_, bf16[192,4096]{1,0:T(8,128)(2,1)} %collective-permute-done.8.refs_1_.refs_2_, ...), custom_call_target="tpu_custom_call" | custom-call | flops 1000 | bytes 1000 | tf_op jit(solution)/shard_map/pallas_call | solution.py:301
  205.4 1.6 collective-permute-start.24
  206.9 2.9 %collective-permute-done.21.refs_1_ = s16[272,1536]{1,0:T(8,128)(2,1)} collective-permute-done((s16[272,1536]{1,0:T(8,128)(2,1)}, s16[272,1536]{1,0:T(8,128)(2,1)}, u32[]{:S(2)}, u32[]{:S(2)}) %collective-permute-start.21) | collective-permute-done | bytes 835616 | tf_op jit(solution)/shard_map/ppermute | solution.py:590
  209.8 3.9 %shard_map.85 = (s16[288,3072]{1,0:T(8,128)(2,1)}, s16[288,3072]{1,0:T(8,128)(2,1)}) custom-call(f32[4,256,3072]{2,1,0:T(8,128)} %get-tuple-element.36.refs_3_.base_ref.refs_0_.refs_1_, s16[272,1536]{1,0:T(8,128)(2,1)} %collective-permute-done.15.refs_0_, s16[272,1536]{1,0:T(8,128)(2,1)} %collective-permute-done.21.refs_1_, ...), custom_call_target="tpu_custom_call", output_to_operand_aliasing={{1}: (3, {})} | custom-call | flops 1000 | bytes 1000 | tf_op jit(solution)/shard_map/pallas_call | solution.py:220
  213.7 2.5 collective-permute-start.22
  216.2 3.8 %shard_map.86.refs_1_ = s16[480,1024]{1,0:T(8,128)(2,1)} custom-call(s32[1]{0:T(128)} %bitcast.9.at_ref, f32[1,384,2048]{2,1,0:T(8,128)} %get-tuple-element.31.refs_0_.refs_5_.refs_6_, s16[416,2048]{1,0:T(8,128)(2,1)} %collective-permute-done.20.refs_10_.refs_1_.refs_7_.refs_8_.refs_9_, f32[1,384,1024]{2,1,0:T(8,128)} %get-tuple-element.44.refs_1_.refs_2_.refs_10_.refs_11_, ...), custom_call_target="tpu_custom_call" | custom-call | flops 1000 | bytes 1000 | tf_op jit(solution)/shard_map/pallas_call | solution.py:331
  222.8 3.7 %shard_map.87.refs_4_ = s16[272,3072]{1,0:T(8,128)(2,1)} custom-call(f32[4,256,3072]{2,1,0:T(8,128)} %get-tuple-element.36.refs_3_.base_ref.refs_0_.refs_1_, s16[272,3072]{1,0:T(8,128)(2,1)} %collective-permute-done.26.refs_0_, s16[480,1024]{1,0:T(8,128)(2,1)} %shard_map.86.refs_1_), custom_call_target="tpu_custom_call" | custom-call | flops 9200001024 | bytes 1000 | tf_op jit(solution)/shard_map/pallas_call | solution.py:220
  226.6 2.7 collective-permute-start.29
  229.3 3.8 %shard_map.88 = s16[400,1024]{1,0:T(8,128)(2,1)} custom-call(s32[1]{0:T(128)} %bitcast.9.at_ref, f32[1,384,2048]{2,1,0:T(8,128)} %get-tuple-element.31.refs_0_.refs_5_.refs_6_, s16[416,2048]{1,0:T(8,128)(2,1)} %collective-permute-done.20.refs_10_.refs_1_.refs_7_.refs_8_.refs_9_, f32[1,384,1024]{2,1,0:T(8,128)} %get-tuple-element.46.refs_3_.refs_2_.refs_15_.refs_16_, ...), custom_call_target="tpu_custom_call" | custom-call | flops 1000 | bytes 1000 | tf_op jit(solution)/shard_map/pallas_call | solution.py:331
  236.2 24.7 %collective-permute-done.27.refs_23_.refs_24_.refs_25_ = s16[400,1024]{1,0:T(8,128)(2,1)} collective-permute-done((s16[400,1024]{1,0:T(8,128)(2,1)}, s16[400,1024]{1,0:T(8,128)(2,1)}, u32[]{:S(2)}, u32[]{:S(2)}) %collective-permute-start.27) | collective-permute-done | bytes 819232 | tf_op jit(solution)/shard_map/ppermute | solution.py:603
  261.0 9.7 %shard_map.89.settled_ref = f32[8,48,16,128]{3,2,1,0:T(8,128)} custom-call(s32[2]{0:T(128)} %pad_add_fusion.at_ref, f32[4,256,3072]{2,1,0:T(8,128)} %get-tuple-element.36.refs_3_.base_ref.refs_0_.refs_1_, f32[4,256,3072]{2,1,0:T(8,128)} %get-tuple-element.36.refs_3_.base_ref.refs_0_.refs_1_, ...), custom_call_target="tpu_custom_call" | custom-call | flops 8050000896 | bytes 1000 | tf_op jit(solution)/shard_map/pallas_call | solution.py:442
  270.7 5.5 %shard_map.90 = f32[8,48,16,128]{3,2,1,0:T(8,128)} custom-call(s32[2]{0:T(128)} %pad_add_fusion.at_ref, f32[8]{0:T(128)} %select_reduce_fusion.slab_ref, f32[48]{0:T(128)} %dynamic_slice.9.pair_ref, f32[16,128]{1,0:T(8,128)} %broadcast_add_fusion.base_ref, f32[8,48,16,128]{3,2,1,0:T(8,128)} %shard_map.89.settled_ref, ...), custom_call_target="tpu_custom_call" | custom-call | flops 1000 | bytes 1000 | tf_op jit(solution)/shard_map/pallas_call | solution.py:489
  (69 shorter events, 28.0 us)
Async XLA Ops:
  3.4 10.1 %collective-permute-start.4 = (bf16[192,4096]{1,0:T(8,128)(2,1)}, bf16[192,4096]{1,0:T(8,128)(2,1)}, u32[]{:S(2)}, u32[]{:S(2)}) collective-permute-start(bf16[192,4096]{1,0:T(8,128)(2,1)} %bitcast.19.refs_0_), channel_id=1, source_target_pairs={{0,4},{4,0},{8,12},{12,8},{16,20},{20,16},{24,28},{28,24},{1,5},{5... | collective-permute-start | bytes 4718600 | tf_op jit(solution)/shard_map/ppermute | solution.py:549
  5.5 37.1 %collective-permute-start = (bf16[256,3072]{1,0:T(8,128)(2,1)}, bf16[256,3072]{1,0:T(8,128)(2,1)}, u32[]{:S(2)}, u32[]{:S(2)}) collective-permute-start(bf16[256,3072]{1,0:T(8,128)(2,1)} %bitcast.20.own_ref), channel_id=1, source_target_pairs={{0,1},{1,0},{2,3},{3,2},{4,5},{5,4},{6,7},{7,6},{8,9},{9,8},{10,11... | collective-permute-start | bytes 4718600 | tf_op jit(solution)/shard_map/ppermute | solution.py:543
  7.0 36.8 %collective-permute-start.1 = (bf16[256,3072]{1,0:T(8,128)(2,1)}, bf16[256,3072]{1,0:T(8,128)(2,1)}, u32[]{:S(2)}, u32[]{:S(2)}) collective-permute-start(bf16[256,3072]{1,0:T(8,128)(2,1)} %bitcast.20.own_ref), channel_id=1, source_target_pairs={{0,2},{1,3},{2,0},{3,1},{4,6},{5,7},{6,4},{7,5},{8,10},{9,11},{10,... | collective-permute-start | bytes 4718600 | tf_op jit(solution)/shard_map/ppermute | solution.py:544
  8.5 36.6 %collective-permute-start.2 = (bf16[192,4096]{1,0:T(8,128)(2,1)}, bf16[192,4096]{1,0:T(8,128)(2,1)}, u32[]{:S(2)}, u32[]{:S(2)}) collective-permute-start(bf16[192,4096]{1,0:T(8,128)(2,1)} %bitcast.19.refs_0_), channel_id=1, source_target_pairs={{0,8},{4,12},{8,0},{12,4},{16,24},{20,28},{24,16},{28,20},{1,9},{5... | collective-permute-start | bytes 4718600 | tf_op jit(solution)/shard_map/ppermute | solution.py:547
  9.0 39.1 %collective-permute-start.3 = (bf16[192,4096]{1,0:T(8,128)(2,1)}, bf16[192,4096]{1,0:T(8,128)(2,1)}, u32[]{:S(2)}, u32[]{:S(2)}) collective-permute-start(bf16[192,4096]{1,0:T(8,128)(2,1)} %bitcast.19.refs_0_), channel_id=1, source_target_pairs={{8,16},{12,20},{16,8},{20,12},{9,17},{13,21},{17,9},{21,13},{10,18... | collective-permute-start | bytes 4718600 | tf_op jit(solution)/shard_map/ppermute | solution.py:548
  50.7 6.0 %collective-permute-start.7 = (bf16[192,4096]{1,0:T(8,128)(2,1)}, bf16[192,4096]{1,0:T(8,128)(2,1)}, u32[]{:S(2)}, u32[]{:S(2)}) collective-permute-start(bf16[192,4096]{1,0:T(8,128)(2,1)} %get-tuple-element.30.refs_0_), channel_id=1, source_target_pairs={{0,4},{4,0},{8,12},{12,8},{16,20},{20,16},{24,28},{28,24},{1,5},{5... | collective-permute-start | bytes 4718600 | tf_op jit(solution)/shard_map/ppermute | solution.py:557
  50.8 25.2 %collective-permute-start.8 = (bf16[192,4096]{1,0:T(8,128)(2,1)}, bf16[192,4096]{1,0:T(8,128)(2,1)}, u32[]{:S(2)}, u32[]{:S(2)}) collective-permute-start(bf16[192,4096]{1,0:T(8,128)(2,1)} %get-tuple-element.32.refs_0_), channel_id=1, source_target_pairs={{0,4},{4,0},{8,12},{12,8},{16,20},{20,16},{24,28},{28,24},{1,5},{5... | collective-permute-start | bytes 4718600 | tf_op jit(solution)/shard_map/ppermute | solution.py:558
  51.3 24.7 %collective-permute-start.5 = (bf16[128,3072]{1,0:T(8,128)(2,1)}, bf16[128,3072]{1,0:T(8,128)(2,1)}, u32[]{:S(2)}, u32[]{:S(2)}) collective-permute-start(bf16[128,3072]{1,0:T(8,128)(2,1)} %get-tuple-element.28), channel_id=1, source_target_pairs={{0,2},{1,3},{2,0},{3,1},{4,6},{5,7},{6,4},{7,5},{8,10},{9,11},{10,... | collective-permute-start | bytes 2359304 | tf_op jit(solution)/shard_map/ppermute | solution.py:554
  51.8 24.2 %collective-permute-start.6 = (bf16[128,3072]{1,0:T(8,128)(2,1)}, bf16[128,3072]{1,0:T(8,128)(2,1)}, u32[]{:S(2)}, u32[]{:S(2)}) collective-permute-start(bf16[128,3072]{1,0:T(8,128)(2,1)} %get-tuple-element.29), channel_id=1, source_target_pairs={{0,1},{1,0},{2,3},{3,2},{4,5},{5,4},{6,7},{7,6},{8,9},{9,8},{10,11... | collective-permute-start | bytes 2359304 | tf_op jit(solution)/shard_map/ppermute | solution.py:553
  54.3 39.2 %collective-permute-start.10 = (bf16[192,4096]{1,0:T(8,128)(2,1)}, bf16[192,4096]{1,0:T(8,128)(2,1)}, u32[]{:S(2)}, u32[]{:S(2)}) collective-permute-start(bf16[192,4096]{1,0:T(8,128)(2,1)} %get-tuple-element.32.refs_0_), channel_id=1, source_target_pairs={{8,0},{12,4},{16,24},{20,28},{9,1},{13,5},{17,25},{21,29},{10,2},{... | collective-permute-start | bytes 4718600 | tf_op jit(solution)/shard_map/ppermute | solution.py:556
  56.7 38.0 %collective-permute-start.9 = (bf16[192,4096]{1,0:T(8,128)(2,1)}, bf16[192,4096]{1,0:T(8,128)(2,1)}, u32[]{:S(2)}, u32[]{:S(2)}) collective-permute-start(bf16[192,4096]{1,0:T(8,128)(2,1)} %get-tuple-element.30.refs_0_), channel_id=1, source_target_pairs={{8,16},{12,20},{16,8},{20,12},{9,17},{13,21},{17,9},{21,13},{10,18... | collective-permute-start | bytes 4718600 | tf_op jit(solution)/shard_map/ppermute | solution.py:555
  93.4 23.0 %collective-permute-start.12 = (s16[1040,1536]{1,0:T(8,128)(2,1)}, s16[1040,1536]{1,0:T(8,128)(2,1)}, u32[]{:S(2)}, u32[]{:S(2)}) collective-permute-start(s16[1040,1536]{1,0:T(8,128)(2,1)} %shard_map.76.refs_0_), channel_id=1, source_target_pairs={{0,4},{4,0},{8,12},{12,8},{16,20},{20,16},{24,28},{28,24},{1,5},{5... | collective-permute-start | bytes 9584648 | tf_op jit(solution)/shard_map/ppermute | solution.py:569
  112.2 23.8 %collective-permute-start.11 = (s16[1040,1536]{1,0:T(8,128)(2,1)}, s16[1040,1536]{1,0:T(8,128)(2,1)}, u32[]{:S(2)}, u32[]{:S(2)}) collective-permute-start(s16[1040,1536]{1,0:T(8,128)(2,1)} %shard_map.77.refs_1_), channel_id=1, source_target_pairs={{0,4},{4,0},{8,12},{12,8},{16,20},{20,16},{24,28},{28,24},{1,5},{5... | collective-permute-start | bytes 9584648 | tf_op jit(solution)/shard_map/ppermute | solution.py:571
  112.2 57.2 %collective-permute-start.20 = (s16[416,2048]{1,0:T(8,128)(2,1)}, s16[416,2048]{1,0:T(8,128)(2,1)}, u32[]{:S(2)}, u32[]{:S(2)}) collective-permute-start(s16[416,2048]{1,0:T(8,128)(2,1)} %get-tuple-element.43), channel_id=1, source_target_pairs={{0,1},{1,0},{2,3},{3,2},{4,5},{5,4},{6,7},{7,6},{8,9},{9,8},{10,11... | collective-permute-start | bytes 5111816 | tf_op jit(solution)/shard_map/ppermute | solution.py:563
  113.8 42.7 %collective-permute-start.14 = (bf16[192,4096]{1,0:T(8,128)(2,1)}, bf16[192,4096]{1,0:T(8,128)(2,1)}, u32[]{:S(2)}, u32[]{:S(2)}) collective-permute-start(bf16[192,4096]{1,0:T(8,128)(2,1)} %collective-permute-done.9.refs_1_.refs_4_), channel_id=1, source_target_pairs={{8,0},{12,4},{16,24},{20,28},{9,1},{13,5},{17,25},{21,29},{10,2},{... | collective-permute-start | bytes 4718600 | tf_op jit(solution)/shard_map/ppermute | solution.py:576
  116.2 45.2 %collective-permute-start.17 = (bf16[192,4096]{1,0:T(8,128)(2,1)}, bf16[192,4096]{1,0:T(8,128)(2,1)}, u32[]{:S(2)}, u32[]{:S(2)}) collective-permute-start(bf16[192,4096]{1,0:T(8,128)(2,1)} %collective-permute-done.10.refs_2_.refs_1_), channel_id=1, source_target_pairs={{0,4},{4,0},{8,12},{12,8},{16,20},{20,16},{24,28},{28,24},{1,5},{5... | collective-permute-start | bytes 4718600 | tf_op jit(solution)/shard_map/ppermute | solution.py:560
  116.4 49.3 %collective-permute-start.18 = (bf16[192,4096]{1,0:T(8,128)(2,1)}, bf16[192,4096]{1,0:T(8,128)(2,1)}, u32[]{:S(2)}, u32[]{:S(2)}) collective-permute-start(bf16[192,4096]{1,0:T(8,128)(2,1)} %collective-permute-done.9.refs_1_.refs_4_), channel_id=1, source_target_pairs={{0,4},{4,0},{8,12},{12,8},{16,20},{20,16},{24,28},{28,24},{1,5},{5... | collective-permute-start | bytes 4718600 | tf_op jit(solution)/shard_map/ppermute | solution.py:559
  136.0 22.9 %collective-permute-start.13 = (s16[272,1536]{1,0:T(8,128)(2,1)}, s16[272,1536]{1,0:T(8,128)(2,1)}, u32[]{:S(2)}, u32[]{:S(2)}) collective-permute-start(s16[272,1536]{1,0:T(8,128)(2,1)} %get-tuple-element.37), channel_id=1, source_target_pairs={{0,8},{4,12},{24,16},{28,20},{1,9},{5,13},{25,17},{29,21},{2,10},{... | collective-permute-start | bytes 2506760 | tf_op jit(solution)/shard_map/ppermute | solution.py:573
  159.5 10.0 %collective-permute-start.19 = (bf16[192,4096]{1,0:T(8,128)(2,1)}, bf16[192,4096]{1,0:T(8,128)(2,1)}, u32[]{:S(2)}, u32[]{:S(2)}) collective-permute-start(bf16[192,4096]{1,0:T(8,128)(2,1)} %get-tuple-element.42.refs_5_), channel_id=1, source_target_pairs={{0,4},{4,0},{8,12},{12,8},{16,20},{20,16},{24,28},{28,24},{1,5},{5... | collective-permute-start | bytes 4718600 | tf_op jit(solution)/shard_map/ppermute | solution.py:580
  159.5 24.5 %collective-permute-start.16 = (s16[272,1536]{1,0:T(8,128)(2,1)}, s16[272,1536]{1,0:T(8,128)(2,1)}, u32[]{:S(2)}, u32[]{:S(2)}) collective-permute-start(s16[272,1536]{1,0:T(8,128)(2,1)} %get-tuple-element.41), channel_id=1, source_target_pairs={{0,8},{4,12},{24,16},{28,20},{1,9},{5,13},{25,17},{29,21},{2,10},{... | collective-permute-start | bytes 2506760 | tf_op jit(solution)/shard_map/ppermute | solution.py:575
  161.4 61.5 %collective-permute-start.26 = (s16[272,3072]{1,0:T(8,128)(2,1)}, s16[272,3072]{1,0:T(8,128)(2,1)}, u32[]{:S(2)}, u32[]{:S(2)}) collective-permute-start(s16[272,3072]{1,0:T(8,128)(2,1)} %get-tuple-element.40.refs_1_), channel_id=1, source_target_pairs={{0,8},{4,12},{24,16},{28,20},{1,9},{5,13},{25,17},{29,21},{2,10},{... | collective-permute-start | bytes 5013512 | tf_op jit(solution)/shard_map/ppermute | solution.py:582
  165.7 41.2 %collective-permute-start.15 = (s16[272,1536]{1,0:T(8,128)(2,1)}, s16[272,1536]{1,0:T(8,128)(2,1)}, u32[]{:S(2)}, u32[]{:S(2)}) collective-permute-start(s16[272,1536]{1,0:T(8,128)(2,1)} %shard_map.81.refs_9_), channel_id=1, source_target_pairs={{8,16},{12,20},{16,8},{20,12},{9,17},{13,21},{17,9},{21,13},{10,18... | collective-permute-start | bytes 2506760 | tf_op jit(solution)/shard_map/ppermute | solution.py:581
  186.9 22.9 %collective-permute-start.21 = (s16[272,1536]{1,0:T(8,128)(2,1)}, s16[272,1536]{1,0:T(8,128)(2,1)}, u32[]{:S(2)}, u32[]{:S(2)}) collective-permute-start(s16[272,1536]{1,0:T(8,128)(2,1)} %shard_map.83.refs_9_), channel_id=1, source_target_pairs={{8,16},{12,20},{16,8},{20,12},{9,17},{13,21},{17,9},{21,13},{10,18... | collective-permute-start | bytes 2506760 | tf_op jit(solution)/shard_map/ppermute | solution.py:590
  189.7 26.5 %collective-permute-start.23 = (s16[400,1024]{1,0:T(8,128)(2,1)}, s16[400,1024]{1,0:T(8,128)(2,1)}, u32[]{:S(2)}, u32[]{:S(2)}) collective-permute-start(s16[400,1024]{1,0:T(8,128)(2,1)} %get-tuple-element.48), channel_id=1, source_target_pairs={{0,1},{1,0},{2,3},{3,2},{4,5},{5,4},{6,7},{7,6},{8,9},{9,8},{10,11... | collective-permute-start | bytes 2457608 | tf_op jit(solution)/shard_map/ppermute | solution.py:588
  205.4 23.9 %collective-permute-start.24 = (s16[400,1024]{1,0:T(8,128)(2,1)}, s16[400,1024]{1,0:T(8,128)(2,1)}, u32[]{:S(2)}, u32[]{:S(2)}) collective-permute-start(s16[400,1024]{1,0:T(8,128)(2,1)} %get-tuple-element.49), channel_id=1, source_target_pairs={{0,1},{1,0},{2,3},{3,2},{4,5},{5,4},{6,7},{7,6},{8,9},{9,8},{10,11... | collective-permute-start | bytes 2457608 | tf_op jit(solution)/shard_map/ppermute | solution.py:593
  213.7 47.3 %collective-permute-start.22 = (s16[288,3072]{1,0:T(8,128)(2,1)}, s16[288,3072]{1,0:T(8,128)(2,1)}, u32[]{:S(2)}, u32[]{:S(2)}) collective-permute-start(s16[288,3072]{1,0:T(8,128)(2,1)} %get-tuple-element.47.refs_4_), channel_id=1, source_target_pairs={{8,0},{12,4},{16,24},{20,28},{9,1},{13,5},{17,25},{21,29},{10,2},{... | collective-permute-start | bytes 5308424 | tf_op jit(solution)/shard_map/ppermute | solution.py:596
  220.0 40.9 %collective-permute-start.25 = (s16[480,1024]{1,0:T(8,128)(2,1)}, s16[480,1024]{1,0:T(8,128)(2,1)}, u32[]{:S(2)}, u32[]{:S(2)}) collective-permute-start(s16[480,1024]{1,0:T(8,128)(2,1)} %shard_map.86.refs_1_), channel_id=1, source_target_pairs={{0,2},{1,3},{2,0},{3,1},{4,6},{5,7},{6,4},{7,5},{8,10},{9,11},{10,... | collective-permute-start | bytes 2949128 | tf_op jit(solution)/shard_map/ppermute | solution.py:599
  221.5 49.1 %collective-permute-start.28 = (s16[288,3072]{1,0:T(8,128)(2,1)}, s16[288,3072]{1,0:T(8,128)(2,1)}, u32[]{:S(2)}, u32[]{:S(2)}) collective-permute-start(s16[288,3072]{1,0:T(8,128)(2,1)} %get-tuple-element.50), channel_id=1, source_target_pairs={{0,8},{4,12},{24,16},{28,20},{1,9},{5,13},{25,17},{29,21},{2,10},{... | collective-permute-start | bytes 5308424 | tf_op jit(solution)/shard_map/ppermute | solution.py:595
  226.6 7.5 %copy-start.2 = (f32[128]{0:T(128)S(1)}, f32[128]{0:T(128)}, u32[]{:S(2)}) copy-start(f32[128]{0:T(128)} %param.11) | copy-start | bytes 1540
  226.6 8.2 %copy-start.3 = (s32[8]{0:T(128)S(1)}, s32[8]{0:T(128)}, u32[]{:S(2)}) copy-start(s32[8]{0:T(128)} %param.12) | copy-start | bytes 100
  226.6 44.1 %collective-permute-start.29 = (s16[272,3072]{1,0:T(8,128)(2,1)}, s16[272,3072]{1,0:T(8,128)(2,1)}, u32[]{:S(2)}, u32[]{:S(2)}) collective-permute-start(s16[272,3072]{1,0:T(8,128)(2,1)} %shard_map.87.refs_4_), channel_id=1, source_target_pairs={{8,16},{12,20},{16,8},{20,12},{9,17},{13,21},{17,9},{21,13},{10,18... | collective-permute-start | bytes 5013512 | tf_op jit(solution)/shard_map/ppermute | solution.py:601
  233.0 27.9 %collective-permute-start.27 = (s16[400,1024]{1,0:T(8,128)(2,1)}, s16[400,1024]{1,0:T(8,128)(2,1)}, u32[]{:S(2)}, u32[]{:S(2)}) collective-permute-start(s16[400,1024]{1,0:T(8,128)(2,1)} %shard_map.88), channel_id=1, source_target_pairs={{0,2},{1,3},{2,0},{3,1},{4,6},{5,7},{6,4},{7,5},{8,10},{9,11},{10,... | collective-permute-start | bytes 2457608 | tf_op jit(solution)/shard_map/ppermute | solution.py:603
  (2 other events, 10.4 us)

commit v5 on v4

--- a/solution.py
+++ b/solution.py
@@ -48,7 +48,7 @@
 
 
 def light(weight=0):
-    return pl.CostEstimate(flops=weight * 1150000000 + 1000, bytes_accessed=1000, transcendentals=0)
+    return pl.CostEstimate(flops=int(weight * 1.15e9) + 1000, bytes_accessed=1000, transcendentals=0)
 
 
 def bring(candidates, code, target, sem):
@@ -584,18 +584,18 @@
     stays = jnp.where(x_place == chip // 2, 0, 1)
     rest = [[g2, g4], [g2_s, g4_s], [g3, g5], [g3_s, g5_s]]
     at = ints(0, stays, end, end, end, end)
-    keep1, to_x = ladder_call(rest, ladder_ints, at, True, after=(to_mid, x0), columns=2)
+    keep1, to_x = ladder_call(rest, ladder_ints, at, True, after=(to_mid, x0), columns=2, tile=256)
     x1 = lax.ppermute(to_x, "red", along_x)
     to_mid = hop(sums, 0, [r0b], 1, after=(keep1,))
     mid_b = lax.ppermute(to_mid, "blk", middle)
     at = ints(1, stays, end, end, end, end)
-    keep2, to_x = ladder_call(rest, ladder_ints, at, True, after=(to_mid,), columns=2)
+    keep2, to_x = ladder_call(rest, ladder_ints, at, True, after=(to_mid,), columns=2, tile=256)
     x2 = lax.ppermute(to_x, "red", along_x)
     to_outer, s2 = hop(sums, 2, [mid_a, mid_b], parts=2, through=(s2,), after=(keep2,), weight=0, trailer=WIDE)
     r2 = lax.ppermute(s2, "blk", inward)
     outer = lax.ppermute(to_outer, "blk", outward)
     near = jnp.where(red // 2 == chip // 2, 1, 0)
-    to_y1 = turn(ints(1 - near), (keep0, x0), (keep1, x1), 0, after=(to_outer,), weight=0, trailer=6 * TRAILER)
+    to_y1 = turn(ints(1 - near), (keep0, x0), (keep1, x1), 0, after=(to_outer,), weight=0, trailer=4 * TRAILER)
     y1 = lax.ppermute(to_y1, "red", along_y)
     to_inner = hop(sums, 1, [r1], parts=2, after=(to_y1,), weight=8)
     inner = lax.ppermute(to_inner, "blk", middle)

time: 277 us -> 275 us (level)
  no operation moved by 1% of the time
where the time goes in v5:
time: 275 us; the launch traced here: 274 us
  Pallas kernels  170 us (62%)
  waiting for transfers between devices  49.7 us (18%)
  starting transfers between devices  42.1 us (15%)
  local copies, waits for them, and re-layouts  8.06 us (3%)
  other arithmetic  3.95 us (1%)
    pallas_call x4, Pallas kernels, cycle_call(): pl.pallas_call(functools.partial(cycle_kernel, keeps=got is not None, ski...  73.2 us
    pallas_call x4, Pallas kernels, ladder_call(): pl.pallas_call(kernel, grid_spec=pltpu.PrefetchScalarGridSpec(num_scalar_...  57.2 us
    ppermute x1, waiting for transfers between devices, paired_shards(): y2 = lax.ppermute(to_y2, 'red', along_y)  23.3 us
    ppermute x1, waiting for transfers between devices, paired_shards(): rx = lax.ppermute(mine, 'red', along_x)  14.3 us
    pallas_call x4, Pallas kernels, hop(): pl.pallas_call(functools.partial(hop_kernel, joins=joins, skip=skip, trai...  13.6 us
    pallas_call x1, Pallas kernels, settle(): pl.pallas_call(settle_kernel, grid_spec=pltpu.PrefetchScalarGridSpec(num_...  9.71 us
    pallas_call x2, Pallas kernels, turn(): pl.pallas_call(functools.partial(turn_kernel, trailer=trailer), grid_spec...  7.55 us
  transfers between devices with their start and end apart: 30, of which 8 were waited for; matrix products, arithmetic and copies ran while one was open for 3% of the time, Pallas kernels for 59%

profile of v5, /device:TPU:8, one launch (start us, length us, event | category | flops | bytes accessed | tf_op | source)
XLA Modules:
  0.0 274.1 jit_solution(5737116025841086364)
XLA Ops:
  0.0 3.4 %copy.23 = bf16[24,8,32,128]{3,1,2,0:T(8,128)(2,1)} copy(bf16[24,8,32,128]{3,2,1,0:T(8,128)(2,1)} %bitcast.21) | data formatting | bytes 3145728
  9.0 4.6 %collective-permute-start.3 = (bf16[192,4096]{1,0:T(8,128)(2,1)}, bf16[192,4096]{1,0:T(8,128)(2,1)}, u32[]{:S(2)}, u32[]{:S(2)}) collective-permute-start(bf16[192,4096]{1,0:T(8,128)(2,1)} %bitcast.19.refs_0_), channel_id=1, source_target_pairs={{8,16},{12,20},{16,8},{20,12},{9,17},{13,21},{17,9},{21,13},{10,18... | collective-permute-start | bytes 4718600 | tf_op jit(solution)/shard_map/ppermute | solution.py:548
  14.2 14.2 %shard_map.73.refs_2_.refs_3_ = f32[384,2048]{1,0:T(8,128)} custom-call(s32[8]{0:T(128)} %broadcast_3_at_ref.2.at_ref, bf16[192,4096]{1,0:T(8,128)(2,1)} %bitcast.19.refs_0_, bf16[192,4096]{1,0:T(8,128)(2,1)} %collective-permute-done.4.refs_1_, bf16[4096,2048]{1,0:T(8,128)(2,1)} %refs_8_.3), custom_call_target="tpu_custom_call" | custom-call | flops 1000 | bytes 1000 | tf_op jit(solution)/shard_map/pallas_call | solution.py:301
  28.3 14.3 %collective-permute-done.rx_ref = bf16[256,3072]{1,0:T(8,128)(2,1)} collective-permute-done((bf16[256,3072]{1,0:T(8,128)(2,1)}, bf16[256,3072]{1,0:T(8,128)(2,1)}, u32[]{:S(2)}, u32[]{:S(2)}) %collective-permute-start) | collective-permute-done | bytes 1572896 | tf_op jit(solution)/shard_map/ppermute | solution.py:543
  45.1 3.0 %collective-permute-done.3.refs_1_ = bf16[192,4096]{1,0:T(8,128)(2,1)} collective-permute-done((bf16[192,4096]{1,0:T(8,128)(2,1)}, bf16[192,4096]{1,0:T(8,128)(2,1)}, u32[]{:S(2)}, u32[]{:S(2)}) %collective-permute-start.3) | collective-permute-done | bytes 1572896 | tf_op jit(solution)/shard_map/ppermute | solution.py:548
  48.1 2.6 shard_map.74
  54.3 2.5 collective-permute-start.10
  56.7 3.6 %collective-permute-start.9 = (bf16[192,4096]{1,0:T(8,128)(2,1)}, bf16[192,4096]{1,0:T(8,128)(2,1)}, u32[]{:S(2)}, u32[]{:S(2)}) collective-permute-start(bf16[192,4096]{1,0:T(8,128)(2,1)} %get-tuple-element.30.refs_0_), channel_id=1, source_target_pairs={{8,16},{12,20},{16,8},{20,12},{9,17},{13,21},{17,9},{21,13},{10,18... | collective-permute-start | bytes 4718600 | tf_op jit(solution)/shard_map/ppermute | solution.py:555
  60.4 15.6 %shard_map.75 = (f32[1,384,2048]{2,1,0:T(8,128)}, s16[416,2048]{1,0:T(8,128)(2,1)}) custom-call(s32[4]{0:T(128)} %pad_add_fusion.3.at_ref, bf16[192,4096]{1,0:T(8,128)(2,1)} %get-tuple-element.30.refs_0_, bf16[192,4096]{1,0:T(8,128)(2,1)} %collective-permute-done.7.refs_1_, bf16[4096,2048]{1,0:T(8,128)(2,1)} %refs_8_.3, f32[384,2048]{1,0:T(8,128)} %shard_map.73.refs_2_.refs_3_), custom_call_target="tpu_custom_call" | custom-call | flops 1000 | bytes 1000 | tf_op jit(solution)/shard_map/pallas_call | solution.py:301
  76.0 17.4 %shard_map.76.refs_0_ = s16[1040,1536]{1,0:T(8,128)(2,1)} custom-call(s32[5]{0:T(128)} %get-tuple-element.51.at_ref, bf16[256,3072]{1,0:T(8,128)(2,1)} %bitcast.20.own_ref, bf16[256,3072]{1,0:T(8,128)(2,1)} %collective-permute-done.rx_ref, bf16[256,3072]{1,0:T(8,128)(2,1)} %collective-permute-done.1.ry_ref, ...), custom_call_target="tpu_custom_call" | custom-call | flops 21850001408 | bytes 1000 | tf_op jit(solution)/shard_map/pallas_call | solution.py:170
  94.7 17.4 %shard_map.77.refs_1_ = s16[1040,1536]{1,0:T(8,128)(2,1)} custom-call(s32[5]{0:T(128)} %get-tuple-element.51.at_ref, bf16[256,3072]{1,0:T(8,128)(2,1)} %bitcast.20.own_ref, bf16[256,3072]{1,0:T(8,128)(2,1)} %collective-permute-done.rx_ref, bf16[256,3072]{1,0:T(8,128)(2,1)} %collective-permute-done.1.ry_ref, ...), custom_call_target="tpu_custom_call" | custom-call | flops 21850001408 | bytes 1000 | tf_op jit(solution)/shard_map/pallas_call | solution.py:170
  113.8 2.4 collective-permute-start.14
  116.7 19.2 %shard_map.78 = (f32[4,256,3072]{2,1,0:T(8,128)}, s16[272,1536]{1,0:T(8,128)(2,1)}, s16[272,3072]{1,0:T(8,128)(2,1)}, s16[288,3072]{1,0:T(8,128)(2,1)}) custom-call(s32[5]{0:T(128)} %get-tuple-element.52.at_ref, bf16[256,3072]{1,0:T(8,128)(2,1)} %bitcast.20.own_ref, bf16[256,3072]{1,0:T(8,128)(2,1)} %collective-permute-done.rx_ref, ...), custom_call_target="tpu_custom_call" | custom-call | flops 21850001408 | bytes 1000 | tf_op jit(solution)/shard_map/pallas_call | solution.py:170
  137.3 19.2 %shard_map.79 = (f32[4,256,3072]{2,1,0:T(8,128)}, s16[272,1536]{1,0:T(8,128)(2,1)}, s16[272,3072]{1,0:T(8,128)(2,1)}, s16[288,3072]{1,0:T(8,128)(2,1)}) custom-call(s32[5]{0:T(128)} %get-tuple-element.52.at_ref, bf16[256,3072]{1,0:T(8,128)(2,1)} %bitcast.20.own_ref, ...), custom_call_target="tpu_custom_call", output_to_operand_aliasing={{0}: (9, {}), {2}: (10, {}), {3}: (11, {})} | custom-call | flops 21850001408 | bytes 1000 | tf_op jit(solution)/shard_map/pallas_call | solution.py:170
  156.5 2.4 collective-permute-done.13.refs_4_.refs_0_
  162.7 3.0 %shard_map.81.refs_9_ = s16[272,1536]{1,0:T(8,128)(2,1)} custom-call(f32[4,256,3072]{2,1,0:T(8,128)} %get-tuple-element.36.refs_3_.base_ref.refs_0_.refs_1_, s16[272,1536]{1,0:T(8,128)(2,1)} %collective-permute-done.13.refs_4_.refs_0_, s16[272,3072]{1,0:T(8,128)(2,1)} %get-tuple-element.40.refs_1_), custom_call_target="tpu_custom_call" | custom-call | flops 4600001024 | bytes 1000 | tf_op jit(solution)/shard_map/pallas_call | solution.py:220
  165.7 3.8 %collective-permute-start.15 = (s16[272,1536]{1,0:T(8,128)(2,1)}, s16[272,1536]{1,0:T(8,128)(2,1)}, u32[]{:S(2)}, u32[]{:S(2)}) collective-permute-start(s16[272,1536]{1,0:T(8,128)(2,1)} %shard_map.81.refs_9_), channel_id=1, source_target_pairs={{8,16},{12,20},{16,8},{20,12},{9,17},{13,21},{17,9},{21,13},{10,18... | collective-permute-start | bytes 2506760 | tf_op jit(solution)/shard_map/ppermute | solution.py:581
  169.5 13.7 %shard_map.82 = (f32[1,384,1024]{2,1,0:T(8,128)}, s16[400,1024]{1,0:T(8,128)(2,1)}) custom-call(s32[6]{0:T(128)} %stack.51.at_ref, bf16[192,4096]{1,0:T(8,128)(2,1)} %get-tuple-element.32.refs_0_, bf16[192,4096]{1,0:T(8,128)(2,1)} %collective-permute-done.10.refs_2_.refs_1_, bf16[192,4096]{1,0:T(8,128)(2,1)} %collective-permute-done.8.refs_1_.refs_2_, ...), custom_call_target="tpu_custom_call" | custom-call | flops 1000 | bytes 1000 | tf_op jit(solution)/shard_map/pallas_call | solution.py:301
  183.3 3.0 %shard_map.83.refs_9_ = s16[272,1536]{1,0:T(8,128)(2,1)} custom-call(f32[4,256,3072]{2,1,0:T(8,128)} %get-tuple-element.36.refs_3_.base_ref.refs_0_.refs_1_, s16[272,1536]{1,0:T(8,128)(2,1)} %collective-permute-done.16.refs_0_, f32[1,384,1024]{2,1,0:T(8,128)} %get-tuple-element.44.refs_1_.refs_2_.refs_10_.refs_11_), custom_call_target="tpu_custom_call" | custom-call | flops 4600001024 | bytes 1000 | tf_op jit(solution)/shard_map/pallas_call | solution.py:220
  186.3 3.4 %collective-permute-start.21 = (s16[272,1536]{1,0:T(8,128)(2,1)}, s16[272,1536]{1,0:T(8,128)(2,1)}, u32[]{:S(2)}, u32[]{:S(2)}) collective-permute-start(s16[272,1536]{1,0:T(8,128)(2,1)} %shard_map.83.refs_9_), channel_id=1, source_target_pairs={{8,16},{12,20},{16,8},{20,12},{9,17},{13,21},{17,9},{21,13},{10,18... | collective-permute-start | bytes 2506760 | tf_op jit(solution)/shard_map/ppermute | solution.py:590
  191.0 13.7 %shard_map.84 = (f32[1,384,1024]{2,1,0:T(8,128)}, s16[400,1024]{1,0:T(8,128)(2,1)}) custom-call(s32[6]{0:T(128)} %stack.52.at_ref, bf16[192,4096]{1,0:T(8,128)(2,1)} %get-tuple-element.32.refs_0_, bf16[192,4096]{1,0:T(8,128)(2,1)} %collective-permute-done.10.refs_2_.refs_1_, bf16[192,4096]{1,0:T(8,128)(2,1)} %collective-permute-done.8.refs_1_.refs_2_, ...), custom_call_target="tpu_custom_call" | custom-call | flops 1000 | bytes 1000 | tf_op jit(solution)/shard_map/pallas_call | solution.py:301
  204.7 1.6 collective-permute-start.24
  206.2 3.0 %collective-permute-done.21.refs_1_ = s16[272,1536]{1,0:T(8,128)(2,1)} collective-permute-done((s16[272,1536]{1,0:T(8,128)(2,1)}, s16[272,1536]{1,0:T(8,128)(2,1)}, u32[]{:S(2)}, u32[]{:S(2)}) %collective-permute-start.21) | collective-permute-done | bytes 835616 | tf_op jit(solution)/shard_map/ppermute | solution.py:590
  209.2 3.9 %shard_map.85 = (s16[288,3072]{1,0:T(8,128)(2,1)}, s16[288,3072]{1,0:T(8,128)(2,1)}) custom-call(f32[4,256,3072]{2,1,0:T(8,128)} %get-tuple-element.36.refs_3_.base_ref.refs_0_.refs_1_, s16[272,1536]{1,0:T(8,128)(2,1)} %collective-permute-done.15.refs_0_, s16[272,1536]{1,0:T(8,128)(2,1)} %collective-permute-done.21.refs_1_, ...), custom_call_target="tpu_custom_call", output_to_operand_aliasing={{1}: (3, {})} | custom-call | flops 1000 | bytes 1000 | tf_op jit(solution)/shard_map/pallas_call | solution.py:220
  213.1 2.5 collective-permute-start.22
  215.6 3.8 %shard_map.86.refs_1_ = s16[448,1024]{1,0:T(8,128)(2,1)} custom-call(s32[1]{0:T(128)} %bitcast.9.at_ref, f32[1,384,2048]{2,1,0:T(8,128)} %get-tuple-element.31.refs_0_.refs_5_.refs_6_, s16[416,2048]{1,0:T(8,128)(2,1)} %collective-permute-done.20.refs_10_.refs_1_.refs_7_.refs_8_.refs_9_, f32[1,384,1024]{2,1,0:T(8,128)} %get-tuple-element.44.refs_1_.refs_2_.refs_10_.refs_11_, ...), custom_call_target="tpu_custom_call" | custom-call | flops 1000 | bytes 1000 | tf_op jit(solution)/shard_map/pallas_call | solution.py:331
  222.2 3.7 %shard_map.87.refs_4_ = s16[272,3072]{1,0:T(8,128)(2,1)} custom-call(f32[4,256,3072]{2,1,0:T(8,128)} %get-tuple-element.36.refs_3_.base_ref.refs_0_.refs_1_, s16[272,3072]{1,0:T(8,128)(2,1)} %collective-permute-done.26.refs_0_, s16[448,1024]{1,0:T(8,128)(2,1)} %shard_map.86.refs_1_), custom_call_target="tpu_custom_call" | custom-call | flops 9200001024 | bytes 1000 | tf_op jit(solution)/shard_map/pallas_call | solution.py:220
  226.0 2.7 collective-permute-start.29
  228.6 3.8 %shard_map.88 = s16[400,1024]{1,0:T(8,128)(2,1)} custom-call(s32[1]{0:T(128)} %bitcast.9.at_ref, f32[1,384,2048]{2,1,0:T(8,128)} %get-tuple-element.31.refs_0_.refs_5_.refs_6_, s16[416,2048]{1,0:T(8,128)(2,1)} %collective-permute-done.20.refs_10_.refs_1_.refs_7_.refs_8_.refs_9_, f32[1,384,1024]{2,1,0:T(8,128)} %get-tuple-element.46.refs_3_.refs_2_.refs_15_.refs_16_, ...), custom_call_target="tpu_custom_call" | custom-call | flops 1000 | bytes 1000 | tf_op jit(solution)/shard_map/pallas_call | solution.py:331
  235.6 23.3 %collective-permute-done.27.refs_23_.refs_24_.refs_25_ = s16[400,1024]{1,0:T(8,128)(2,1)} collective-permute-done((s16[400,1024]{1,0:T(8,128)(2,1)}, s16[400,1024]{1,0:T(8,128)(2,1)}, u32[]{:S(2)}, u32[]{:S(2)}) %collective-permute-start.27) | collective-permute-done | bytes 819232 | tf_op jit(solution)/shard_map/ppermute | solution.py:603
  258.9 9.7 %shard_map.89.settled_ref = f32[8,48,16,128]{3,2,1,0:T(8,128)} custom-call(s32[2]{0:T(128)} %pad_add_fusion.at_ref, f32[4,256,3072]{2,1,0:T(8,128)} %get-tuple-element.36.refs_3_.base_ref.refs_0_.refs_1_, f32[4,256,3072]{2,1,0:T(8,128)} %get-tuple-element.36.refs_3_.base_ref.refs_0_.refs_1_, ...), custom_call_target="tpu_custom_call" | custom-call | flops 8050000896 | bytes 1000 | tf_op jit(solution)/shard_map/pallas_call | solution.py:442
  268.7 5.5 %shard_map.90 = f32[8,48,16,128]{3,2,1,0:T(8,128)} custom-call(s32[2]{0:T(128)} %pad_add_fusion.at_ref, f32[8]{0:T(128)} %select_reduce_fusion.slab_ref, f32[48]{0:T(128)} %dynamic_slice.9.pair_ref, f32[16,128]{1,0:T(8,128)} %broadcast_add_fusion.base_ref, f32[8,48,16,128]{3,2,1,0:T(8,128)} %shard_map.89.settled_ref, ...), custom_call_target="tpu_custom_call" | custom-call | flops 1000 | bytes 1000 | tf_op jit(solution)/shard_map/pallas_call | solution.py:489
  (69 shorter events, 28.0 us)
Async XLA Ops:
  3.4 10.1 %collective-permute-start.4 = (bf16[192,4096]{1,0:T(8,128)(2,1)}, bf16[192,4096]{1,0:T(8,128)(2,1)}, u32[]{:S(2)}, u32[]{:S(2)}) collective-permute-start(bf16[192,4096]{1,0:T(8,128)(2,1)} %bitcast.19.refs_0_), channel_id=1, source_target_pairs={{0,4},{4,0},{8,12},{12,8},{16,20},{20,16},{24,28},{28,24},{1,5},{5... | collective-permute-start | bytes 4718600 | tf_op jit(solution)/shard_map/ppermute | solution.py:549
  5.5 37.1 %collective-permute-start = (bf16[256,3072]{1,0:T(8,128)(2,1)}, bf16[256,3072]{1,0:T(8,128)(2,1)}, u32[]{:S(2)}, u32[]{:S(2)}) collective-permute-start(bf16[256,3072]{1,0:T(8,128)(2,1)} %bitcast.20.own_ref), channel_id=1, source_target_pairs={{0,1},{1,0},{2,3},{3,2},{4,5},{5,4},{6,7},{7,6},{8,9},{9,8},{10,11... | collective-permute-start | bytes 4718600 | tf_op jit(solution)/shard_map/ppermute | solution.py:543
  7.0 36.8 %collective-permute-start.1 = (bf16[256,3072]{1,0:T(8,128)(2,1)}, bf16[256,3072]{1,0:T(8,128)(2,1)}, u32[]{:S(2)}, u32[]{:S(2)}) collective-permute-start(bf16[256,3072]{1,0:T(8,128)(2,1)} %bitcast.20.own_ref), channel_id=1, source_target_pairs={{0,2},{1,3},{2,0},{3,1},{4,6},{5,7},{6,4},{7,5},{8,10},{9,11},{10,... | collective-permute-start | bytes 4718600 | tf_op jit(solution)/shard_map/ppermute | solution.py:544
  8.5 36.6 %collective-permute-start.2 = (bf16[192,4096]{1,0:T(8,128)(2,1)}, bf16[192,4096]{1,0:T(8,128)(2,1)}, u32[]{:S(2)}, u32[]{:S(2)}) collective-permute-start(bf16[192,4096]{1,0:T(8,128)(2,1)} %bitcast.19.refs_0_), channel_id=1, source_target_pairs={{0,8},{4,12},{8,0},{12,4},{16,24},{20,28},{24,16},{28,20},{1,9},{5... | collective-permute-start | bytes 4718600 | tf_op jit(solution)/shard_map/ppermute | solution.py:547
  9.0 39.1 %collective-permute-start.3 = (bf16[192,4096]{1,0:T(8,128)(2,1)}, bf16[192,4096]{1,0:T(8,128)(2,1)}, u32[]{:S(2)}, u32[]{:S(2)}) collective-permute-start(bf16[192,4096]{1,0:T(8,128)(2,1)} %bitcast.19.refs_0_), channel_id=1, source_target_pairs={{8,16},{12,20},{16,8},{20,12},{9,17},{13,21},{17,9},{21,13},{10,18... | collective-permute-start | bytes 4718600 | tf_op jit(solution)/shard_map/ppermute | solution.py:548
  50.7 6.0 %collective-permute-start.7 = (bf16[192,4096]{1,0:T(8,128)(2,1)}, bf16[192,4096]{1,0:T(8,128)(2,1)}, u32[]{:S(2)}, u32[]{:S(2)}) collective-permute-start(bf16[192,4096]{1,0:T(8,128)(2,1)} %get-tuple-element.30.refs_0_), channel_id=1, source_target_pairs={{0,4},{4,0},{8,12},{12,8},{16,20},{20,16},{24,28},{28,24},{1,5},{5... | collective-permute-start | bytes 4718600 | tf_op jit(solution)/shard_map/ppermute | solution.py:557
  50.8 25.2 %collective-permute-start.8 = (bf16[192,4096]{1,0:T(8,128)(2,1)}, bf16[192,4096]{1,0:T(8,128)(2,1)}, u32[]{:S(2)}, u32[]{:S(2)}) collective-permute-start(bf16[192,4096]{1,0:T(8,128)(2,1)} %get-tuple-element.32.refs_0_), channel_id=1, source_target_pairs={{0,4},{4,0},{8,12},{12,8},{16,20},{20,16},{24,28},{28,24},{1,5},{5... | collective-permute-start | bytes 4718600 | tf_op jit(solution)/shard_map/ppermute | solution.py:558
  51.3 24.7 %collective-permute-start.5 = (bf16[128,3072]{1,0:T(8,128)(2,1)}, bf16[128,3072]{1,0:T(8,128)(2,1)}, u32[]{:S(2)}, u32[]{:S(2)}) collective-permute-start(bf16[128,3072]{1,0:T(8,128)(2,1)} %get-tuple-element.28), channel_id=1, source_target_pairs={{0,2},{1,3},{2,0},{3,1},{4,6},{5,7},{6,4},{7,5},{8,10},{9,11},{10,... | collective-permute-start | bytes 2359304 | tf_op jit(solution)/shard_map/ppermute | solution.py:554
  51.8 24.2 %collective-permute-start.6 = (bf16[128,3072]{1,0:T(8,128)(2,1)}, bf16[128,3072]{1,0:T(8,128)(2,1)}, u32[]{:S(2)}, u32[]{:S(2)}) collective-permute-start(bf16[128,3072]{1,0:T(8,128)(2,1)} %get-tuple-element.29), channel_id=1, source_target_pairs={{0,1},{1,0},{2,3},{3,2},{4,5},{5,4},{6,7},{7,6},{8,9},{9,8},{10,11... | collective-permute-start | bytes 2359304 | tf_op jit(solution)/shard_map/ppermute | solution.py:553
  54.3 39.2 %collective-permute-start.10 = (bf16[192,4096]{1,0:T(8,128)(2,1)}, bf16[192,4096]{1,0:T(8,128)(2,1)}, u32[]{:S(2)}, u32[]{:S(2)}) collective-permute-start(bf16[192,4096]{1,0:T(8,128)(2,1)} %get-tuple-element.32.refs_0_), channel_id=1, source_target_pairs={{8,0},{12,4},{16,24},{20,28},{9,1},{13,5},{17,25},{21,29},{10,2},{... | collective-permute-start | bytes 4718600 | tf_op jit(solution)/shard_map/ppermute | solution.py:556
  56.7 38.0 %collective-permute-start.9 = (bf16[192,4096]{1,0:T(8,128)(2,1)}, bf16[192,4096]{1,0:T(8,128)(2,1)}, u32[]{:S(2)}, u32[]{:S(2)}) collective-permute-start(bf16[192,4096]{1,0:T(8,128)(2,1)} %get-tuple-element.30.refs_0_), channel_id=1, source_target_pairs={{8,16},{12,20},{16,8},{20,12},{9,17},{13,21},{17,9},{21,13},{10,18... | collective-permute-start | bytes 4718600 | tf_op jit(solution)/shard_map/ppermute | solution.py:555
  93.4 23.0 %collective-permute-start.12 = (s16[1040,1536]{1,0:T(8,128)(2,1)}, s16[1040,1536]{1,0:T(8,128)(2,1)}, u32[]{:S(2)}, u32[]{:S(2)}) collective-permute-start(s16[1040,1536]{1,0:T(8,128)(2,1)} %shard_map.76.refs_0_), channel_id=1, source_target_pairs={{0,4},{4,0},{8,12},{12,8},{16,20},{20,16},{24,28},{28,24},{1,5},{5... | collective-permute-start | bytes 9584648 | tf_op jit(solution)/shard_map/ppermute | solution.py:569
  112.2 23.8 %collective-permute-start.11 = (s16[1040,1536]{1,0:T(8,128)(2,1)}, s16[1040,1536]{1,0:T(8,128)(2,1)}, u32[]{:S(2)}, u32[]{:S(2)}) collective-permute-start(s16[1040,1536]{1,0:T(8,128)(2,1)} %shard_map.77.refs_1_), channel_id=1, source_target_pairs={{0,4},{4,0},{8,12},{12,8},{16,20},{20,16},{24,28},{28,24},{1,5},{5... | collective-permute-start | bytes 9584648 | tf_op jit(solution)/shard_map/ppermute | solution.py:571
  112.2 57.2 %collective-permute-start.20 = (s16[416,2048]{1,0:T(8,128)(2,1)}, s16[416,2048]{1,0:T(8,128)(2,1)}, u32[]{:S(2)}, u32[]{:S(2)}) collective-permute-start(s16[416,2048]{1,0:T(8,128)(2,1)} %get-tuple-element.43), channel_id=1, source_target_pairs={{0,1},{1,0},{2,3},{3,2},{4,5},{5,4},{6,7},{7,6},{8,9},{9,8},{10,11... | collective-permute-start | bytes 5111816 | tf_op jit(solution)/shard_map/ppermute | solution.py:563
  113.8 42.7 %collective-permute-start.14 = (bf16[192,4096]{1,0:T(8,128)(2,1)}, bf16[192,4096]{1,0:T(8,128)(2,1)}, u32[]{:S(2)}, u32[]{:S(2)}) collective-permute-start(bf16[192,4096]{1,0:T(8,128)(2,1)} %collective-permute-done.9.refs_1_.refs_4_), channel_id=1, source_target_pairs={{8,0},{12,4},{16,24},{20,28},{9,1},{13,5},{17,25},{21,29},{10,2},{... | collective-permute-start | bytes 4718600 | tf_op jit(solution)/shard_map/ppermute | solution.py:576
  116.2 45.2 %collective-permute-start.17 = (bf16[192,4096]{1,0:T(8,128)(2,1)}, bf16[192,4096]{1,0:T(8,128)(2,1)}, u32[]{:S(2)}, u32[]{:S(2)}) collective-permute-start(bf16[192,4096]{1,0:T(8,128)(2,1)} %collective-permute-done.10.refs_2_.refs_1_), channel_id=1, source_target_pairs={{0,4},{4,0},{8,12},{12,8},{16,20},{20,16},{24,28},{28,24},{1,5},{5... | collective-permute-start | bytes 4718600 | tf_op jit(solution)/shard_map/ppermute | solution.py:560
  116.4 49.3 %collective-permute-start.18 = (bf16[192,4096]{1,0:T(8,128)(2,1)}, bf16[192,4096]{1,0:T(8,128)(2,1)}, u32[]{:S(2)}, u32[]{:S(2)}) collective-permute-start(bf16[192,4096]{1,0:T(8,128)(2,1)} %collective-permute-done.9.refs_1_.refs_4_), channel_id=1, source_target_pairs={{0,4},{4,0},{8,12},{12,8},{16,20},{20,16},{24,28},{28,24},{1,5},{5... | collective-permute-start | bytes 4718600 | tf_op jit(solution)/shard_map/ppermute | solution.py:559
  136.0 22.9 %collective-permute-start.13 = (s16[272,1536]{1,0:T(8,128)(2,1)}, s16[272,1536]{1,0:T(8,128)(2,1)}, u32[]{:S(2)}, u32[]{:S(2)}) collective-permute-start(s16[272,1536]{1,0:T(8,128)(2,1)} %get-tuple-element.37), channel_id=1, source_target_pairs={{0,8},{4,12},{24,16},{28,20},{1,9},{5,13},{25,17},{29,21},{2,10},{... | collective-permute-start | bytes 2506760 | tf_op jit(solution)/shard_map/ppermute | solution.py:573
  159.5 10.0 %collective-permute-start.19 = (bf16[192,4096]{1,0:T(8,128)(2,1)}, bf16[192,4096]{1,0:T(8,128)(2,1)}, u32[]{:S(2)}, u32[]{:S(2)}) collective-permute-start(bf16[192,4096]{1,0:T(8,128)(2,1)} %get-tuple-element.42.refs_5_), channel_id=1, source_target_pairs={{0,4},{4,0},{8,12},{12,8},{16,20},{20,16},{24,28},{28,24},{1,5},{5... | collective-permute-start | bytes 4718600 | tf_op jit(solution)/shard_map/ppermute | solution.py:580
  159.5 23.8 %collective-permute-start.16 = (s16[272,1536]{1,0:T(8,128)(2,1)}, s16[272,1536]{1,0:T(8,128)(2,1)}, u32[]{:S(2)}, u32[]{:S(2)}) collective-permute-start(s16[272,1536]{1,0:T(8,128)(2,1)} %get-tuple-element.41), channel_id=1, source_target_pairs={{0,8},{4,12},{24,16},{28,20},{1,9},{5,13},{25,17},{29,21},{2,10},{... | collective-permute-start | bytes 2506760 | tf_op jit(solution)/shard_map/ppermute | solution.py:575
  161.4 60.8 %collective-permute-start.26 = (s16[272,3072]{1,0:T(8,128)(2,1)}, s16[272,3072]{1,0:T(8,128)(2,1)}, u32[]{:S(2)}, u32[]{:S(2)}) collective-permute-start(s16[272,3072]{1,0:T(8,128)(2,1)} %get-tuple-element.40.refs_1_), channel_id=1, source_target_pairs={{0,8},{4,12},{24,16},{28,20},{1,9},{5,13},{25,17},{29,21},{2,10},{... | collective-permute-start | bytes 5013512 | tf_op jit(solution)/shard_map/ppermute | solution.py:582
  165.7 40.6 %collective-permute-start.15 = (s16[272,1536]{1,0:T(8,128)(2,1)}, s16[272,1536]{1,0:T(8,128)(2,1)}, u32[]{:S(2)}, u32[]{:S(2)}) collective-permute-start(s16[272,1536]{1,0:T(8,128)(2,1)} %shard_map.81.refs_9_), channel_id=1, source_target_pairs={{8,16},{12,20},{16,8},{20,12},{9,17},{13,21},{17,9},{21,13},{10,18... | collective-permute-start | bytes 2506760 | tf_op jit(solution)/shard_map/ppermute | solution.py:581
  186.3 22.9 %collective-permute-start.21 = (s16[272,1536]{1,0:T(8,128)(2,1)}, s16[272,1536]{1,0:T(8,128)(2,1)}, u32[]{:S(2)}, u32[]{:S(2)}) collective-permute-start(s16[272,1536]{1,0:T(8,128)(2,1)} %shard_map.83.refs_9_), channel_id=1, source_target_pairs={{8,16},{12,20},{16,8},{20,12},{9,17},{13,21},{17,9},{21,13},{10,18... | collective-permute-start | bytes 2506760 | tf_op jit(solution)/shard_map/ppermute | solution.py:590
  189.7 25.9 %collective-permute-start.23 = (s16[400,1024]{1,0:T(8,128)(2,1)}, s16[400,1024]{1,0:T(8,128)(2,1)}, u32[]{:S(2)}, u32[]{:S(2)}) collective-permute-start(s16[400,1024]{1,0:T(8,128)(2,1)} %get-tuple-element.48), channel_id=1, source_target_pairs={{0,1},{1,0},{2,3},{3,2},{4,5},{5,4},{6,7},{7,6},{8,9},{9,8},{10,11... | collective-permute-start | bytes 2457608 | tf_op jit(solution)/shard_map/ppermute | solution.py:588
  204.7 23.9 %collective-permute-start.24 = (s16[400,1024]{1,0:T(8,128)(2,1)}, s16[400,1024]{1,0:T(8,128)(2,1)}, u32[]{:S(2)}, u32[]{:S(2)}) collective-permute-start(s16[400,1024]{1,0:T(8,128)(2,1)} %get-tuple-element.49), channel_id=1, source_target_pairs={{0,1},{1,0},{2,3},{3,2},{4,5},{5,4},{6,7},{7,6},{8,9},{9,8},{10,11... | collective-permute-start | bytes 2457608 | tf_op jit(solution)/shard_map/ppermute | solution.py:593
  213.1 45.8 %collective-permute-start.22 = (s16[288,3072]{1,0:T(8,128)(2,1)}, s16[288,3072]{1,0:T(8,128)(2,1)}, u32[]{:S(2)}, u32[]{:S(2)}) collective-permute-start(s16[288,3072]{1,0:T(8,128)(2,1)} %get-tuple-element.47.refs_4_), channel_id=1, source_target_pairs={{8,0},{12,4},{16,24},{20,28},{9,1},{13,5},{17,25},{21,29},{10,2},{... | collective-permute-start | bytes 5308424 | tf_op jit(solution)/shard_map/ppermute | solution.py:596
  219.4 39.5 %collective-permute-start.25 = (s16[448,1024]{1,0:T(8,128)(2,1)}, s16[448,1024]{1,0:T(8,128)(2,1)}, u32[]{:S(2)}, u32[]{:S(2)}) collective-permute-start(s16[448,1024]{1,0:T(8,128)(2,1)} %shard_map.86.refs_1_), channel_id=1, source_target_pairs={{0,2},{1,3},{2,0},{3,1},{4,6},{5,7},{6,4},{7,5},{8,10},{9,11},{10,... | collective-permute-start | bytes 2752520 | tf_op jit(solution)/shard_map/ppermute | solution.py:599
  220.9 47.8 %collective-permute-start.28 = (s16[288,3072]{1,0:T(8,128)(2,1)}, s16[288,3072]{1,0:T(8,128)(2,1)}, u32[]{:S(2)}, u32[]{:S(2)}) collective-permute-start(s16[288,3072]{1,0:T(8,128)(2,1)} %get-tuple-element.50), channel_id=1, source_target_pairs={{0,8},{4,12},{24,16},{28,20},{1,9},{5,13},{25,17},{29,21},{2,10},{... | collective-permute-start | bytes 5308424 | tf_op jit(solution)/shard_map/ppermute | solution.py:595
  225.9 7.6 %copy-start.2 = (f32[128]{0:T(128)S(1)}, f32[128]{0:T(128)}, u32[]{:S(2)}) copy-start(f32[128]{0:T(128)} %param.11) | copy-start | bytes 1540
  225.9 8.3 %copy-start.3 = (s32[8]{0:T(128)S(1)}, s32[8]{0:T(128)}, u32[]{:S(2)}) copy-start(s32[8]{0:T(128)} %param.12) | copy-start | bytes 100
  226.0 42.7 %collective-permute-start.29 = (s16[272,3072]{1,0:T(8,128)(2,1)}, s16[272,3072]{1,0:T(8,128)(2,1)}, u32[]{:S(2)}, u32[]{:S(2)}) collective-permute-start(s16[272,3072]{1,0:T(8,128)(2,1)} %shard_map.87.refs_4_), channel_id=1, source_target_pairs={{8,16},{12,20},{16,8},{20,12},{9,17},{13,21},{17,9},{21,13},{10,18... | collective-permute-start | bytes 5013512 | tf_op jit(solution)/shard_map/ppermute | solution.py:601
  232.4 26.5 %collective-permute-start.27 = (s16[400,1024]{1,0:T(8,128)(2,1)}, s16[400,1024]{1,0:T(8,128)(2,1)}, u32[]{:S(2)}, u32[]{:S(2)}) collective-permute-start(s16[400,1024]{1,0:T(8,128)(2,1)} %shard_map.88), channel_id=1, source_target_pairs={{0,2},{1,3},{2,0},{3,1},{4,6},{5,7},{6,4},{7,5},{8,10},{9,11},{10,... | collective-permute-start | bytes 2457608 | tf_op jit(solution)/shard_map/ppermute | solution.py:603
  (2 other events, 10.4 us)
